TPU v7x, 32 devices: a whole 2x2x4 slice. The times are simulated.
32 devices in a mesh: depth: 4 (over y, x), res: 8 (over z, core).
Axes of the slice: x: 2, y: 2, z: 4, core: 2. Of those that a mesh axis runs over, the one named last changes fastest.
Arguments:
- family_activity: bfloat16 [1024, 8, 768], P('depth', 'res'), may hold values from -6 to 6
- rescale_factor: float32 [768], replicated, may hold values from 0.25 to 1.75
- asking_weights: bfloat16 [768, 768], P(('depth', 'res')), may hold values from -1.203125 to 1.203125
- lookup_weights: bfloat16 [768, 768], P(('depth', 'res')), may hold values from -1.203125 to 1.203125
- payload_weights: bfloat16 [768, 768], P(('depth', 'res')), may hold values from -0.21875 to 0.21875
- exit_weights: bfloat16 [768, 768], P(('depth', 'res')), may hold values from -0.625 to 0.625
- upstream_adjoint: bfloat16 [1024, 8, 768], P('depth', 'res'), may hold values from -6 to 6
Outputs:
- final_result: bfloat16 [1024, 8, 768], P('depth', 'res')
- alignment_gradient: bfloat16 [1024, 8, 768], P('depth', 'res')
- query_gradient: float32 [768, 768], P(('depth', 'res'))
- key_gradient: float32 [768, 768], P(('depth', 'res'))
- value_gradient: float32 [768, 768], P(('depth', 'res'))
- output_gradient: float32 [768, 768], P(('depth', 'res'))
- gain_gradient: float32 [768], P(('depth', 'res'))
All inputs are finite; a program needn't handle non-finite values.
Results may differ from a plain program's by a relative error of at most 0.022.
The roundings to bfloat16 on the way count: a program that leaves them out, or rounds other values in their place, can miss the bound.
Values may be sent and summed in bfloat16 or wider, within the bound.
No kernel may reach another device: no remote copies, remote signals or barrier semaphores. Data moves between devices by JAX's collectives and lax.ppermute only.
A program may use at most 128 MiB of HBM per device.

v0:
```python
import functools

import jax
import jax.numpy as jnp
from jax import lax
from jax.experimental import pallas as pl
from jax.experimental.pallas import tpu as pltpu
from jax.sharding import Mesh, PartitionSpec as P

HEADS = 12
HEAD_DIM = 64


def standardize_entries(family_activity, rescale_factor):
    payload_entries = family_activity.astype(jnp.float32)
    centered = payload_entries - jnp.mean(payload_entries, axis=-1, keepdims=True)
    reciprocal_spread = lax.rsqrt(jnp.mean(centered * centered, axis=-1, keepdims=True) + 1e-05)
    standardized_entries = centered * reciprocal_spread
    return (
        (standardized_entries * rescale_factor).astype(jnp.bfloat16),
        standardized_entries,
        reciprocal_spread,
    )


def project(rows, weight, factor):
    return (factor * jnp.dot(rows, weight, preferred_element_type=jnp.float32)).astype(jnp.bfloat16)


def to_heads(array):
    count, cols = (array.shape[0], array.shape[1])
    return jnp.transpose(array.reshape(count, cols, HEADS, HEAD_DIM), (1, 2, 0, 3)).reshape(
        cols * HEADS, count, HEAD_DIM
    )


def from_heads(array, cols):
    count = array.shape[1]
    return jnp.transpose(array.reshape(cols, HEADS, count, HEAD_DIM), (2, 0, 1, 3)).reshape(
        count, cols, HEADS * HEAD_DIM
    )


def head_pass(query, keys, payload_entries, d_att):
    scale = HEAD_DIM ** (-0.5)
    scores = jnp.dot(query, keys.T, preferred_element_type=jnp.float32)
    probs = jax.nn.softmax(scores, axis=-1)
    probs_b = probs.astype(jnp.bfloat16)
    mixed_homologs = jnp.dot(probs_b, payload_entries, preferred_element_type=jnp.float32).astype(
        jnp.bfloat16
    )
    d_probs = jnp.dot(d_att, payload_entries.T, preferred_element_type=jnp.float32)
    d_scores = probs * (d_probs - jnp.sum(probs * d_probs, axis=-1, keepdims=True))
    d_scores_b = d_scores.astype(jnp.bfloat16)
    d_query = (scale * jnp.dot(d_scores_b, keys, preferred_element_type=jnp.float32)).astype(
        jnp.bfloat16
    )
    key_part = jnp.einsum("st,sd->td", d_scores_b, query, preferred_element_type=jnp.float32)
    value_part = jnp.einsum("st,sd->td", probs_b, d_att, preferred_element_type=jnp.float32)
    return (mixed_homologs, d_query, key_part, value_part)


def general_body(
    family_activity,
    rescale_factor,
    asking_weights,
    lookup_weights,
    payload_weights,
    exit_weights,
    upstream_adjoint,
    axes=("depth", "res"),
):
    query_weight, key_weight, value_weight, output_matrix = (
        lax.all_gather(asking_weights, axes, axis=0, tiled=True),
        lax.all_gather(lookup_weights, axes, axis=0, tiled=True),
        lax.all_gather(payload_weights, axes, axis=0, tiled=True),
        lax.all_gather(exit_weights, axes, axis=0, tiled=True),
    )
    homologs_each_shard, positions_each_shard, embed_span = family_activity.shape
    standardized_source, standardized_entries, reciprocal_spread = standardize_entries(
        family_activity, rescale_factor
    )
    query = project(standardized_source, query_weight, HEAD_DIM ** (-0.5))
    keys = project(standardized_source, key_weight, 1.0)
    payload_entries = project(standardized_source, value_weight, 1.0)
    keys_all, values_all = (
        lax.all_gather(keys, "depth", axis=0, tiled=True),
        lax.all_gather(payload_entries, "depth", axis=0, tiled=True),
    )
    d_att = jnp.dot(upstream_adjoint, output_matrix.T, preferred_element_type=jnp.float32).astype(
        jnp.bfloat16
    )

    def per_head(items):
        return head_pass(items[0], items[1], items[2], items[3])

    mixed_homologs, d_query, key_part, value_part = lax.map(
        per_head, (to_heads(query), to_heads(keys_all), to_heads(values_all), to_heads(d_att))
    )
    mixed_homologs = from_heads(mixed_homologs, positions_each_shard)
    d_query = from_heads(d_query, positions_each_shard)
    key_part = from_heads(key_part, positions_each_shard)
    value_part = from_heads(value_part, positions_each_shard)
    rows = homologs_each_shard * positions_each_shard
    normed_rows = standardized_source.reshape(rows, embed_span)
    part_query = jnp.dot(
        normed_rows.T, d_query.reshape(rows, embed_span), preferred_element_type=jnp.float32
    )
    part_out = jnp.dot(
        mixed_homologs.reshape(rows, embed_span).T,
        upstream_adjoint.reshape(rows, embed_span),
        preferred_element_type=jnp.float32,
    )
    stacked = jnp.stack([key_part, value_part], axis=2).astype(jnp.bfloat16)
    summed = (
        lax.psum_scatter(stacked, "depth", scatter_dimension=0, tiled=True)
        .astype(jnp.float32)
        .astype(jnp.bfloat16)
    )
    d_keys = summed[:, :, 0, :]
    d_values = summed[:, :, 1, :]
    final_result = (
        family_activity.astype(jnp.float32)
        + jnp.dot(mixed_homologs, output_matrix, preferred_element_type=jnp.float32)
    ).astype(jnp.bfloat16)
    part_key = jnp.dot(
        normed_rows.T, d_keys.reshape(rows, embed_span), preferred_element_type=jnp.float32
    )
    part_value = jnp.dot(
        normed_rows.T, d_values.reshape(rows, embed_span), preferred_element_type=jnp.float32
    )
    d_normed = jnp.dot(d_query, query_weight.T, preferred_element_type=jnp.float32)
    d_normed = d_normed + jnp.dot(d_keys, key_weight.T, preferred_element_type=jnp.float32)
    d_normed = d_normed + jnp.dot(d_values, value_weight.T, preferred_element_type=jnp.float32)
    part_gain = jnp.sum((d_normed * standardized_entries).reshape(rows, embed_span), axis=0)
    unit_gradient = d_normed * rescale_factor
    alignment_gradient = upstream_adjoint.astype(jnp.float32) + reciprocal_spread * (
        unit_gradient
        - jnp.mean(unit_gradient, axis=-1, keepdims=True)
        - standardized_entries
        * jnp.mean(unit_gradient * standardized_entries, axis=-1, keepdims=True)
    )
    query_gradient, key_gradient, value_gradient, output_gradient, gain_gradient = (
        lax.psum_scatter(part_query, axes, scatter_dimension=0, tiled=True),
        lax.psum_scatter(part_key, axes, scatter_dimension=0, tiled=True),
        lax.psum_scatter(part_value, axes, scatter_dimension=0, tiled=True),
        lax.psum_scatter(part_out, axes, scatter_dimension=0, tiled=True),
        lax.psum_scatter(part_gain, axes, scatter_dimension=0, tiled=True),
    )
    return (
        final_result,
        alignment_gradient.astype(jnp.bfloat16),
        query_gradient,
        key_gradient,
        value_gradient,
        output_gradient,
        gain_gradient,
    )


F32, BF16 = jnp.float32, jnp.bfloat16
SCALE = HEAD_DIM ** (-0.5)


def swap(value, axis, size, bits):
    return lax.ppermute(value, axis, [(i, i ^ bits) for i in range(size)])


def dot(a, b, contract=(1, 0)):
    return lax.dot_general(
        a, b, (((contract[0],), (contract[1],)), ((), ())), preferred_element_type=F32
    )


def unit_rows(x):
    x = x.astype(F32)
    centered = x - jnp.mean(x, axis=-1, keepdims=True)
    inverse = lax.rsqrt(jnp.mean(centered * centered, axis=-1, keepdims=True) + 1e-05)
    return centered * inverse, inverse


def head_masks(span):
    lane = lax.broadcasted_iota(jnp.int32, (8, span), 1)
    return [
        ((lane >= at) & (lane < at + HEAD_DIM)).astype(F32)[0:1].astype(BF16)
        for at in range(0, span, HEAD_DIM)
    ]


def fetch(pairs, sems):
    copies = [pltpu.make_async_copy(src, dst, sems.at[i]) for i, (src, dst) in enumerate(pairs)]
    for copy in copies:
        copy.start()
    return copies


class Sender:
    def __init__(self, sems):
        self.sems, self.copies = sems, []

    def send(self, src, dst):
        copy = pltpu.make_async_copy(src, dst, self.sems.at[len(self.copies)])
        copy.start()
        self.copies.append(copy)

    def finish(self):
        for copy in self.copies:
            copy.wait()


def pack_kernel(dims, w_query, w_key, w_value, w_out, out, out_cut):
    depth, zs, shard, block, span = dims
    for d in range(depth):
        lanes = slice(d * span, (d + 1) * span)
        for i, w in enumerate((w_query, w_key, w_value)):
            out[d, :, i * span : (i + 1) * span] = w[:, lanes]
        out_cut[d] = w_out[:, lanes]


def norm_kernel(dims, *refs):
    depth, zs, shard, block, span = dims
    gain, xs_h, refs = refs[0], refs[1 : 1 + depth], refs[1 + depth :]
    normed_h, normed_t_h, xs, normed, normed_t, in_sems, out_sems = refs
    copies = fetch([(xs_h[j], xs.at[j]) for j in range(depth)], in_sems)
    sender = Sender(out_sems)
    for j in range(depth):
        copies[j].wait()
        unit, _ = unit_rows(xs[j])
        rows = pl.ds(j * block, block)
        wide = unit * gain[...]
        normed[rows, :] = wide.astype(BF16)
        sender.send(normed.at[rows], normed_h.at[rows])
        normed_t[:, rows] = jnp.transpose(wide).astype(BF16)
        sender.send(normed_t.at[:, rows], normed_t_h.at[:, rows])
    sender.finish()


def forward_kernel(dims, *refs):
    depth, zs, shard, block, span = dims
    heads = span // HEAD_DIM
    pos, w_near, w_far, normed_h = refs[:4]
    query_h, keys_h, values_h, keys_t_h, att_t_h, lse_h, wq_h, wk_h, wv_h, w_out_h = refs[4:14]
    outs_h, refs = refs[14 : 14 + depth], refs[14 + depth :]
    normed, query, keys, values, keys_t, values_t, att_t, lse = refs[:8]
    wq, wk, wv, w_out, outs, in_sems, out_sems = refs[8:]
    copies = fetch([(normed_h, normed)], in_sems)
    sender = Sender(out_sems)

    own_z, first = pos[0], pos[1] == 0
    for z in range(zs):
        for d in range(depth):
            near, far = w_near[z ^ own_z, d].astype(F32), w_far[z ^ own_z, d].astype(F32)
            both = jnp.concatenate(
                [jnp.where(first, near, far), jnp.where(first, far, near)], axis=0
            ).astype(BF16)
            rows = slice((d * zs + z) * 2 * shard, (d * zs + z + 1) * 2 * shard)
            for i, w in enumerate((wq, wk, wv)):
                w[rows, :] = both[:, i * span : (i + 1) * span]
            rows = slice(z * 2 * shard, (z + 1) * 2 * shard)
            w_out[rows, d * span : (d + 1) * span] = both[:, 3 * span :]
    for src, dst in ((wq, wq_h), (wk, wk_h), (wv, wv_h), (w_out, w_out_h)):
        sender.send(src, dst)
    copies[0].wait()

    query[...] = (SCALE * dot(normed[...], wq[...])).astype(BF16)
    key = dot(normed[...], wk[...])
    keys[...] = key.astype(BF16)
    keys_t[...] = jnp.transpose(key).astype(BF16)
    value = dot(normed[...], wv[...])
    values[...] = value.astype(BF16)
    values_t[...] = jnp.transpose(value).astype(BF16)
    for src, dst in ((query, query_h), (keys, keys_h), (values, values_h), (keys_t, keys_t_h)):
        sender.send(src, dst)

    masks = head_masks(span)

    units = [(j, h) for j in range(depth) for h in range(heads)]

    def score(j, h):
        return dot(keys[...], query[j * block : (j + 1) * block, :] * masks[h], (1, 1))

    ready = [score(*unit) for unit in units[:2]]
    for i, (j, h) in enumerate(units):
        cols, lanes = slice(j * block, (j + 1) * block), slice(h * HEAD_DIM, (h + 1) * HEAD_DIM)
        scores = ready.pop(0)
        top = jnp.max(scores, axis=0, keepdims=True)
        e = jnp.exp(scores - top)
        total = jnp.sum(e, axis=0, keepdims=True)
        if i + 2 < len(units):
            ready.append(score(*units[i + 2]))
        att_t[lanes, cols] = dot(values_t[lanes, :], e.astype(BF16)) * (1.0 / total)
        lse[h, :, cols] = top + jnp.log(total)
    sender.send(att_t, att_t_h)
    sender.send(lse, lse_h)
    att = jnp.transpose(att_t[...]).astype(BF16)
    for j in range(depth):
        outs[j] = dot(att[j * block : (j + 1) * block], w_out[...]).astype(BF16)
        sender.send(outs.at[j], outs_h[j])
    sender.finish()


def backward_kernel(dims, *refs):
    depth, zs, shard, block, span = dims
    heads = span // HEAD_DIM
    pos, refs = refs[0], refs[1:]
    gs_h, refs = refs[:depth], refs[depth:]
    (w_out_h, query_h, keys_h, values_h, keys_t_h, lse_h, normed_t_h, att_t_h) = refs[:8]
    (wq_h, wk_h, wv_h, near, far), refs = refs[8:13], refs[13:]
    dns_h, refs = refs[: depth + 1], refs[depth + 1 :]
    (gs, w_out, query, keys, values, keys_t, lse, normed_t, att_t, wq, wk, wv) = refs[:12]
    (d_att, delta, d_query_t, d_keys, d_values, grad_out, dns, in_sems, out_sems) = refs[12:]
    copies = fetch(
        [(w_out_h, w_out)]
        + [(gs_h[j], gs.at[pl.ds(j * block, block)]) for j in range(depth)]
        + [
            (att_t_h, att_t),
            (keys_h, keys),
            (query_h, query),
            (values_h, values),
            (lse_h, lse),
            (keys_t_h, keys_t),
            (normed_t_h, normed_t),
            (wq_h, wq),
            (wk_h, wk),
            (wv_h, wv),
        ],
        in_sems,
    )
    loaded, later = 7 + depth, copies[7 + depth :]

    d_keys[...] = jnp.zeros_like(d_keys)
    d_values[...] = jnp.zeros_like(d_values)
    for copy in copies[: 2 + depth]:
        copy.wait()
    part = dot(gs[...], w_out[...], (1, 1)).astype(BF16)
    d_att[...] = part
    product = jnp.transpose(part.astype(F32)) * att_t[...]
    for h in range(heads):
        delta[h] = jnp.sum(product[h * HEAD_DIM : (h + 1) * HEAD_DIM], axis=0, keepdims=True)
    for copy in copies[2 + depth : loaded]:
        copy.wait()
    masks = head_masks(span)

    def step(j, _):
        cols = pl.ds(pl.multiple_of(j * block, block), block)
        q_block, g_block = query[cols, :], d_att[cols, :]
        qs = [q_block * m for m in masks]
        ds = [g_block * m for m in masks]

        def pair(h):
            return dot(keys[...], qs[h], (1, 1)), dot(values[...], ds[h], (1, 1))

        pairs = [pair(h) for h in range(min(2, heads))]
        for h in range(heads):
            scores, d_probs = pairs[h]
            probs = jnp.exp(scores - lse[h, :, cols])
            d_scores = (probs * (d_probs - delta[h, :, cols])).astype(BF16)
            if h + 2 < heads:
                pairs.append(pair(h + 2))
            values_add = dot(probs.astype(BF16), ds[h])
            keys_add = dot(d_scores, qs[h])
            value_part = values_add if h == 0 else value_part + values_add
            key_part = keys_add if h == 0 else key_part + keys_add
            lanes = slice(h * HEAD_DIM, (h + 1) * HEAD_DIM)
            d_query_t[lanes, cols] = SCALE * dot(keys_t[lanes, :], d_scores)
        d_values[...] += value_part.astype(BF16).astype(F32)
        d_keys[...] += key_part.astype(BF16).astype(F32)
        return 0

    lax.fori_loop(0, depth, step, 0)
    for copy in later:
        copy.wait()
    d_query = jnp.transpose(d_query_t[...]).astype(BF16)
    d_key, d_value = d_keys[...].astype(BF16), d_values[...].astype(BF16)
    sender = Sender(out_sems)
    for i in range(0, depth, 2):
        rows = slice(i * block, (i + 2) * block)
        d_normed = dot(d_query[rows], wq[...], (1, 1))
        d_normed = d_normed + dot(d_key[rows], wk[...], (1, 1))
        d_normed = d_normed + dot(d_value[rows], wv[...], (1, 1))
        dns[rows, :] = d_normed.astype(BF16)
        for j in (i, i + 1):
            if j < depth - 1:
                sender.send(dns.at[pl.ds(j * block, block)], dns_h[j])
            else:
                half = block // 2
                sender.send(dns.at[pl.ds(j * block, half)], dns_h[j])
                sender.send(dns.at[pl.ds(j * block + half, half)], dns_h[j + 1])

    grad_out[...] = dot(att_t[...].astype(BF16), gs[...])
    grads = [dot(normed_t[...], d) for d in (d_query, d_key, d_value)]
    own_z, first, own_d = pos[0], pos[1] == 0, pos[2]
    for d in range(depth):
        for z in range(zs):
            sides = []
            for c in range(2):
                row, row_out = ((d * zs + z) * 2 + c) * shard, (z * 2 + c) * shard
                sides.append(
                    [g[row : row + shard] for g in grads]
                    + [grad_out[row_out : row_out + shard, d * span : (d + 1) * span]]
                )
            at = 0
            for one, two in zip(*sides):
                lanes = slice(at, at + one.shape[1])
                at += one.shape[1]
                near[z ^ own_z, d ^ own_d, :, lanes] = jnp.where(first, one, two).astype(BF16)
                far[z ^ own_z, d ^ own_d, :, lanes] = jnp.where(first, two, one).astype(BF16)
    sender.finish()


def align_kernel(dims, gain, x, upstream, *refs):
    dns, out = refs[:-1], refs[-1]
    d_normed = dns[0][...].astype(F32)
    for part in dns[1:]:
        d_normed = d_normed + part[...].astype(F32)
    unit, inverse = unit_rows(x[...])
    d_unit = d_normed * gain[...]
    out[...] = (
        upstream[...].astype(F32)
        + inverse
        * (
            d_unit
            - jnp.mean(d_unit, axis=-1, keepdims=True)
            - unit * jnp.mean(d_unit * unit, axis=-1, keepdims=True)
        )
    ).astype(BF16)


def finish_kernel(dims, *refs):
    depth, zs, shard, block, span = dims
    pos, gain, weights, acc, refs = refs[0], refs[1], refs[2:5], refs[5], refs[6:]
    parts, outs = refs[: depth - 1], refs[depth - 1 :]
    own_d = pos[2]
    blocks = [acc[0][:, : 3 * span]] + [p[...].astype(F32) for p in parts]
    for d in range(depth):
        lanes = slice(d * span, (d + 1) * span)
        total = blocks[0]
        for k in range(1, depth):
            total = jnp.where((d ^ own_d) == k, blocks[k], total)
        for i in range(3):
            outs[i][:, lanes] = total[:, i * span : (i + 1) * span]
        outs[3][:, lanes] = acc[d ^ own_d][:, 3 * span :]
    column = weights[0][...].astype(F32) * outs[0][...]
    for w, grad in zip(weights[1:], outs[1:3]):
        column = column + w[...].astype(F32) * grad[...]
    column = jnp.sum(column, axis=1, keepdims=True)
    wide = jnp.concatenate([column, jnp.zeros((128 - shard, 1), F32)], axis=0)
    row = jnp.transpose(jnp.broadcast_to(wide, (128, 128)))[0:1, :shard]
    outs[4][...] = row / gain[...]


VMEM, ANY, SMEM = pltpu.VMEM, pl.ANY, pltpu.SMEM


def call(kernel, dims, ins, outs, scratch, sems, flops, mib=56):
    args = [a for a, _ in ins]
    shapes = [jax.ShapeDtypeStruct(shape, kind) for shape, kind, _ in outs]
    size = sum(a.size * a.dtype.itemsize for a in args + shapes)
    return pl.pallas_call(
        functools.partial(kernel, dims),
        out_shape=shapes,
        in_specs=[pl.BlockSpec(memory_space=space) for _, space in ins],
        out_specs=[pl.BlockSpec(memory_space=space) for _, _, space in outs],
        scratch_shapes=[pltpu.VMEM(shape, kind) for shape, kind in scratch]
        + [pltpu.SemaphoreType.DMA((n,)) for n in sems],
        compiler_params=pltpu.CompilerParams(vmem_limit_bytes=mib * 1024 * 1024),
        cost_estimate=pl.CostEstimate(flops=flops, bytes_accessed=size, transcendentals=0),
    )(*args)


def head_body(depth, res, *args):
    x, gain, w_query, w_key, w_value, w_out, upstream = args
    homologs, _, width = x.shape
    span, zs = width // depth, res // 2
    shard = w_query.shape[0]
    total, heads = homologs * depth, span // HEAD_DIM
    dims = (depth, zs, shard, homologs, span)
    x = x.reshape(homologs, width)
    upstream = upstream.reshape(homologs, width)
    gain = gain.reshape(1, width)
    pos = jnp.stack([lax.axis_index(a) for a in ("z", "core", "depth")]).astype(jnp.int32)

    xs = [x] + [swap(x, "depth", depth, k) for k in range(1, depth - 1)]

    packed, out_cut = call(
        pack_kernel,
        dims,
        [(w, VMEM) for w in (w_query, w_key, w_value, w_out)],
        [((depth, shard, 3 * span), BF16, VMEM), ((depth, shard, span), BF16, VMEM)],
        [],
        [],
        1000,
    )
    mine = lax.all_to_all(packed, "depth", 0, 0, tiled=True)
    mine = jnp.concatenate([mine, out_cut], axis=2)
    mine, *xs = lax.optimization_barrier([mine] + xs)
    xs.append(swap(xs[0], "depth", depth, depth - 1))
    parts = [mine] + [swap(mine, "z", zs, k) for k in range(1, zs)]
    gs = [upstream] + [swap(upstream, "depth", depth, k) for k in range(1, depth)]

    rows, turned = ((total, span), BF16), ((span, total), BF16)
    half = homologs // 2
    block, halved = ((homologs, width), BF16), ((half, width), BF16)
    blocks = ((depth, homologs, width), BF16)
    norm, stats = ((total, width), BF16), ((heads, 1, total), F32)
    in_weights, out_weights = ((width, span), BF16), ((span, width), BF16)
    pass_flops = 2 * total * total * span
    normed, normed_t = call(
        norm_kernel,
        dims,
        [(gain, VMEM)] + [(a, ANY) for a in xs],
        [norm + (ANY,), ((width, total), BF16, ANY)],
        [blocks, norm, ((width, total), BF16)],
        [depth, 2 * depth],
        1000,
    )
    normed, pos, *parts = lax.optimization_barrier([normed, pos] + parts)
    w_near = jnp.stack(parts, axis=0)
    w_far = swap(w_near, "core", 2, 1)

    turned_f32 = ((span, total), F32)
    saved = [rows, rows, rows, turned, turned_f32, stats] + [in_weights] * 3 + [out_weights]
    query, keys, values, keys_t, att_t, lse, wq, wk, wv, wo, *outs = call(
        forward_kernel,
        dims,
        [(pos, SMEM), (w_near, VMEM), (w_far, VMEM), (normed, ANY)],
        [s + (ANY,) for s in saved + [block] * depth],
        [norm, rows, rows, rows, turned, turned, turned_f32, stats]
        + [in_weights] * 3
        + [out_weights, blocks],
        [1, len(saved) + depth],
        8 * pass_flops,
        44,
    )

    packed = (zs, depth, shard, 4 * span)
    near, far, *dns = call(
        backward_kernel,
        dims,
        [(pos, SMEM)]
        + [(a, ANY) for a in gs + [wo, query, keys, values, keys_t, lse, normed_t]]
        + [(a, ANY) for a in (att_t, wq, wk, wv)],
        [(packed, BF16, VMEM)] * 2 + [s + (ANY,) for s in [block] * 3 + [halved] * 2],
        [norm, out_weights, rows, rows, rows, turned, stats, ((width, total), BF16)]
        + [turned_f32, in_weights, in_weights, in_weights]
        + [rows, stats, turned_f32]
        + [((total, span), F32)] * 2
        + [((span, width), F32), norm],
        [depth + 11, depth + 1],
        24 * pass_flops,
    )

    outs = [outs[0]] + [swap(outs[k], "depth", depth, k) for k in range(1, depth)]
    near, far, dns, outs = lax.optimization_barrier((near, far, dns, outs))

    far = swap(far, "core", 2, 1)
    dn0, dn1, dn2, dn3_top, dn3_bottom = dns
    top, bottom = swap(dn3_top, "depth", depth, 1), swap(dn3_bottom, "depth", depth, 2)
    sums = [near[k].astype(F32) + far[k].astype(F32) for k in range(zs)]
    low = [swap(sums[k].astype(BF16), "z", zs, k) for k in range(1, zs)]
    low[0], top, bottom = lax.optimization_barrier((low[0], top, bottom))
    dn2 = dn2.astype(F32) + jnp.concatenate([top, jnp.zeros_like(top)], axis=0).astype(F32)
    dn1 = dn1.astype(F32) + jnp.concatenate([jnp.zeros_like(bottom), bottom], axis=0).astype(F32)
    dn1 = swap(dn1.astype(BF16), "depth", depth, 1)
    dn2 = swap(dn2.astype(BF16), "depth", depth, 2)
    low[0], outs = lax.optimization_barrier((low[0], outs))
    final_result = (x.astype(F32) + sum(o.astype(F32) for o in outs)).astype(BF16)
    acc = sums[0] + sum(p.astype(F32) for p in low)
    parts = [
        swap(acc[k, :, : 3 * span].astype(BF16), "depth", depth, k) for k in range(1, depth)
    ]
    alignment = call(
        align_kernel,
        dims,
        [(a, VMEM) for a in (gain, x, upstream, dn0, dn1, dn2)],
        [block + (VMEM,)],
        [],
        [],
        1000 * total * width,
        16,
    )[0]
    alignment, *parts = lax.optimization_barrier([alignment] + parts)
    first_row = (lax.axis_index("depth") * res + pos[0] * 2 + pos[1]) * shard
    own_gain = lax.dynamic_slice(gain, (0, first_row), (1, shard))
    grad_query, grad_key, grad_value, grad_out, gain_rows = call(
        finish_kernel,
        dims,
        [(pos, SMEM)]
        + [(a, VMEM) for a in [own_gain, w_query, w_key, w_value, acc] + parts],
        [((shard, width), F32, VMEM)] * 4 + [((1, shard), F32, VMEM)],
        [],
        [],
        1000,
        16,
    )
    return (
        final_result.reshape(homologs, 1, width),
        alignment.reshape(homologs, 1, width),
        grad_query,
        grad_key,
        grad_value,
        grad_out,
        gain_rows.reshape(shard),
    )


def solution(mesh):
    depth, res = mesh.shape["depth"], mesh.shape["res"]
    powers = depth & (depth - 1) == 0 and res & (res - 1) == 0 and res > 1
    if powers and depth == 4 and res >= 4 and HEADS % depth == 0:
        axes = ("depth", "z", "core")
        mesh = Mesh(mesh.devices.reshape(depth, res // 2, 2), axes)
        res_axes, run = ("z", "core"), functools.partial(head_body, depth, res)
    else:
        axes = ("depth", "res")
        res_axes, run = ("res",), general_body

    def body(*args):
        if args[0].shape[1] != 1:
            return general_body(*args, axes=axes)
        return run(*args)

    rows = P("depth", res_axes, None)
    weight = P(axes, None)
    return jax.shard_map(
        body,
        mesh=mesh,
        in_specs=(rows, P(), weight, weight, weight, weight, rows),
        out_specs=(rows, rows, weight, weight, weight, weight, P(axes)),
        check_vma=False,
    )
```

profile of v0, /device:TPU:0, one launch (start us, length us, event | category | flops | bytes accessed | tf_op | source)
XLA Modules:
  0.0 107.9 jit_solution(16148226974888451323)
XLA Ops:
  0.6 3.0 %collective-permute-start.1 = (bf16[256,768]{1,0:T(8,128)(2,1)}, bf16[256,768]{1,0:T(8,128)(2,1)S(1)}, u32[]{:S(2)}, u32[]{:S(2)}) collective-permute-start(bf16[256,768]{1,0:T(8,128)(2,1)} %bitcast.33), channel_id=1, source_target_pairs={{0,16},{8,24},{16,0},{24,8},{1,17},{9,25},{17,1},{25,9},{2,18},{10... | collective-permute-start | bytes 1179656 | tf_op jit(solution)/shard_map/ppermute | solution.py:166
  3.7 1.5 %collective-permute-start = (bf16[256,768]{1,0:T(8,128)(2,1)}, bf16[256,768]{1,0:T(8,128)(2,1)S(1)}, u32[]{:S(2)}, u32[]{:S(2)}) collective-permute-start(bf16[256,768]{1,0:T(8,128)(2,1)} %bitcast.34), channel_id=1, source_target_pairs={{0,8},{8,0},{16,24},{24,16},{1,9},{9,1},{17,25},{25,17},{2,10},{10... | collective-permute-start | bytes 1179656 | tf_op jit(solution)/shard_map/ppermute | solution.py:166
  5.2 1.6 %shard_map.126 = (bf16[4,24,576]{2,1,0:T(8,128)(2,1)}, bf16[4,24,192]{2,1,0:T(8,128)(2,1)}) custom-call(bf16[24,768]{1,0:T(8,128)(2,1)} %refs_2_.1, bf16[24,768]{1,0:T(8,128)(2,1)} %refs_3_.1, bf16[24,768]{1,0:T(8,128)(2,1)} %refs_4_.1, bf16[24,768]{1,0:T(8,128)(2,1)} %w_out.1), custom_call_target="tpu_custom_call" | custom-call | flops 1000 | bytes 294912 | tf_op jit(solution)/shard_map/pallas_call | solution.py:459
  6.7 9.0 %all_to_all.5 = bf16[4,24,576]{2,1,0:T(8,128)(2,1)S(1)} all-to-all(bf16[4,24,576]{2,1,0:T(8,128)(2,1)} %get-tuple-element.70), channel_id=1, replica_groups=mesh['depth'=4,'z'=4,'core'=2] {'depth'}, dimensions={0} | all-to-all | bytes 221184 | tf_op jit(solution)/shard_map/all_to_all | solution.py:494
  15.8 0.9 pad_maximum_fusion.1
  16.8 2.5 %collective-permute-start.2 = (bf16[256,768]{1,0:T(8,128)(2,1)}, bf16[256,768]{1,0:T(8,128)(2,1)S(1)}, u32[]{:S(2)}, u32[]{:S(2)}) collective-permute-start(bf16[256,768]{1,0:T(8,128)(2,1)} %bitcast.35), channel_id=1, source_target_pairs={{0,24},{8,16},{16,8},{24,0},{1,25},{9,17},{17,9},{25,1},{2,26},{10... | collective-permute-start | bytes 1179656 | tf_op jit(solution)/shard_map/ppermute | solution.py:166
  19.2 3.6 %collective-permute-start.5 = (bf16[4,24,768]{2,1,0:T(8,128)(2,1)S(1)}, bf16[4,24,768]{2,1,0:T(8,128)(2,1)S(1)}, u32[]{:S(2)}, u32[]{:S(2)}) collective-permute-start(bf16[4,24,768]{2,1,0:T(8,128)(2,1)S(1)} %pad_maximum_fusion.1), channel_id=1, source_target_pairs={{0,6},{2,4},{4,2},{6,0},{1,7},{3,5},{5,3},{7,1},{8,14},{10,12},{12... | collective-permute-start | bytes 442376 | tf_op jit(solution)/shard_map/ppermute | solution.py:166
  23.6 1.3 %reshape.54.refs_0_.gain = f32[1,768]{1,0:T(1,128)} reshape(f32[768]{0:T(1024)} %param.8) | data formatting | bytes 6144 | tf_op jit(solution)/shard_map/reshape | solution.py:480
  24.9 2.6 %collective-permute-done.2.refs_4_ = bf16[256,768]{1,0:T(8,128)(2,1)S(1)} collective-permute-done((bf16[256,768]{1,0:T(8,128)(2,1)}, bf16[256,768]{1,0:T(8,128)(2,1)S(1)}, u32[]{:S(2)}, u32[]{:S(2)}) %collective-permute-start.2) | collective-permute-done | bytes 393248 | tf_op jit(solution)/shard_map/ppermute | solution.py:166
  28.3 4.2 %shard_map.127 = (bf16[1024,768]{1,0:T(8,128)(2,1)}, bf16[768,1024]{1,0:T(8,128)(2,1)}) custom-call(f32[1,768]{1,0:T(1,128)} %reshape.54.refs_0_.gain, bf16[256,768]{1,0:T(8,128)(2,1)} %bitcast.36, bf16[256,768]{1,0:T(8,128)(2,1)} %copy-done.24, bf16[256,768]{1,0:T(8,128)(2,1)} %copy-done.23, bf16[256,768]{1,0:T(8,128)(2,1)} %copy-done.25), custom_call_target="tpu_custom_call" | custom-call | flops 1000 | bytes 4721664 | tf_op jit(solution)/shard_map/pallas_call | solution.py:459
  32.6 1.0 collective-permute-done.4
  33.7 1.2 %collective-permute-start.8 = (bf16[256,768]{1,0:T(8,128)(2,1)S(1)}, bf16[256,768]{1,0:T(8,128)(2,1)S(1)}, u32[]{:S(2)}, u32[]{:S(2)}) collective-permute-start(bf16[256,768]{1,0:T(8,128)(2,1)S(1)} %bitcast.39), channel_id=1, source_target_pairs={{0,24},{8,16},{16,8},{24,0},{1,25},{9,17},{17,9},{25,1},{2,26},{10... | collective-permute-start | bytes 1179656 | tf_op jit(solution)/shard_map/ppermute | solution.py:166
  35.4 1.8 %collective-permute-start.6 = (bf16[256,768]{1,0:T(8,128)(2,1)S(1)}, bf16[256,768]{1,0:T(8,128)(2,1)S(1)}, u32[]{:S(2)}, u32[]{:S(2)}) collective-permute-start(bf16[256,768]{1,0:T(8,128)(2,1)S(1)} %bitcast.41), channel_id=1, source_target_pairs={{0,8},{8,0},{16,24},{24,16},{1,9},{9,1},{17,25},{25,17},{2,10},{10... | collective-permute-start | bytes 1179656 | tf_op jit(solution)/shard_map/ppermute | solution.py:166
  37.3 1.4 %copy-done.7 = bf16[1024,768]{1,0:T(8,128)(2,1)S(1)} copy-done((bf16[1024,768]{1,0:T(8,128)(2,1)S(1)}, bf16[1024,768]{1,0:T(8,128)(2,1)}, u32[]{:S(2)}) %copy-start.7) | copy-done | bytes 1572888
  38.7 10.7 %shard_map.128 = (bf16[1024,192]{1,0:T(8,128)(2,1)S(1)}, bf16[1024,192]{1,0:T(8,128)(2,1)S(1)}, bf16[1024,192]{1,0:T(8,128)(2,1)S(1)}, bf16[192,1024]{1,0:T(8,12...) custom-call(s32[3]{0:T(128)S(1)} %pad_add_fusion.refs_0_, ...), custom_call_target="tpu_custom_call" | custom-call | flops 3221225472 | bytes 7876620 | tf_op jit(solution)/shard_map/pallas_call | solution.py:459
  49.4 0.9 copy-done.11
  51.9 0.8 copy-done.14
  56.8 1.5 %collective-permute-start.11 = (bf16[256,768]{1,0:T(8,128)(2,1)S(1)}, bf16[256,768]{1,0:T(8,128)(2,1)S(1)}, u32[]{:S(2)}, u32[]{:S(2)}) collective-permute-start(bf16[256,768]{1,0:T(8,128)(2,1)S(1)} %get-tuple-element.103), channel_id=1, source_target_pairs={{0,16},{8,24},{16,0},{24,8},{1,17},{9,25},{17,1},{25,9},{2,18},{10... | collective-permute-start | bytes 1179656 | tf_op jit(solution)/shard_map/ppermute | solution.py:166
  58.3 1.8 %collective-permute-start.12 = (bf16[256,768]{1,0:T(8,128)(2,1)S(1)}, bf16[256,768]{1,0:T(8,128)(2,1)S(1)}, u32[]{:S(2)}, u32[]{:S(2)}) collective-permute-start(bf16[256,768]{1,0:T(8,128)(2,1)S(1)} %get-tuple-element.104), channel_id=1, source_target_pairs={{0,24},{8,16},{16,8},{24,0},{1,25},{9,17},{17,9},{25,1},{2,26},{10... | collective-permute-start | bytes 1179656 | tf_op jit(solution)/shard_map/ppermute | solution.py:166
  61.0 16.8 %shard_map.129 = (bf16[4,4,24,768]{3,2,1,0:T(8,128)(2,1)}, bf16[4,4,24,768]{3,2,1,0:T(8,128)(2,1)}, bf16[256,768]{1,0:T(8,128)(2,1)}, bf16[256,768]{1,0:T(8,128)...) custom-call(s32[3]{0:T(128)} %copy-done.5, bf16[256,768]{1,0:T(8,128)(2,1)} %bitcast.38, ...), custom_call_target="tpu_custom_call" | custom-call | flops 9663676416 | bytes 9449484 | tf_op jit(solution)/shard_map/pallas_call | solution.py:459
  78.2 1.5 %collective-permute-start.16 = (bf16[128,768]{1,0:T(8,128)(2,1)}, bf16[128,768]{1,0:T(8,128)(2,1)S(1)}, u32[]{:S(2)}, u32[]{:S(2)}) collective-permute-start(bf16[128,768]{1,0:T(8,128)(2,1)} %get-tuple-element.108), channel_id=1, source_target_pairs={{0,16},{8,24},{16,0},{24,8},{1,17},{9,25},{17,1},{25,9},{2,18},{10... | collective-permute-start | bytes 589832 | tf_op jit(solution)/shard_map/ppermute | solution.py:166
  80.1 1.9 %fusion.2 = (bf16[4,24,768]{2,1,0:T(8,128)(2,1)}, bf16[4,24,768]{2,1,0:T(8,128)(2,1)}, bf16[4,24,768]{2,1,0:T(8,128)(2,1)}) fusion(bf16[4,4,24,768]{3,2,1,0:T(8,128)(2,1)S(1)} %collective-permute-done.13, bf16[4,4,24,768]{3,2,1,0:T(8,128)(2,1)} %get-tuple-element.105), kind=kLoop, calls=%fused_computation.10 | loop fusion | flops 884736 | bytes 1327104 | tf_op jit(solution)/shard_map/convert_element_type | solution.py:560
  82.0 1.2 %collective-permute-start.14 = (bf16[4,24,768]{2,1,0:T(8,128)(2,1)}, bf16[4,24,768]{2,1,0:T(8,128)(2,1)S(1)}, u32[]{:S(2)}, u32[]{:S(2)}) collective-permute-start(bf16[4,24,768]{2,1,0:T(8,128)(2,1)} %get-tuple-element.137), channel_id=1, source_target_pairs={{0,2},{2,0},{4,6},{6,4},{1,3},{3,1},{5,7},{7,5},{8,10},{10,8},{12,... | collective-permute-start | bytes 442376 | tf_op jit(solution)/shard_map/ppermute | solution.py:166
  85.8 2.6 %collective-permute-start.19 = (bf16[4,24,768]{2,1,0:T(8,128)(2,1)}, bf16[4,24,768]{2,1,0:T(8,128)(2,1)S(1)}, u32[]{:S(2)}, u32[]{:S(2)}) collective-permute-start(bf16[4,24,768]{2,1,0:T(8,128)(2,1)} %get-tuple-element.135), channel_id=1, source_target_pairs={{0,4},{2,6},{4,0},{6,2},{1,5},{3,7},{5,1},{7,3},{8,12},{10,14},{12... | collective-permute-start | bytes 442376 | tf_op jit(solution)/shard_map/ppermute | solution.py:166
  89.7 1.6 %collective-permute-start.18 = (bf16[256,768]{1,0:T(8,128)(2,1)S(1)}, bf16[256,768]{1,0:T(8,128)(2,1)S(1)}, u32[]{:S(2)}, u32[]{:S(2)}) collective-permute-start(bf16[256,768]{1,0:T(8,128)(2,1)S(1)} %add_convert_fusion), channel_id=1, source_target_pairs={{0,16},{8,24},{16,0},{24,8},{1,17},{9,25},{17,1},{25,9},{2,18},{10... | collective-permute-start | bytes 1179656 | tf_op jit(solution)/shard_map/ppermute | solution.py:166
  91.2 8.0 %collective-permute-done.19 = bf16[4,24,768]{2,1,0:T(8,128)(2,1)S(1)} collective-permute-done((bf16[4,24,768]{2,1,0:T(8,128)(2,1)}, bf16[4,24,768]{2,1,0:T(8,128)(2,1)S(1)}, u32[]{:S(2)}, u32[]{:S(2)}) %collective-permute-start.19) | collective-permute-done | bytes 147488 | tf_op jit(solution)/shard_map/ppermute | solution.py:166
  99.3 1.0 fusion.4
  100.3 1.6 %collective-permute-start.23 = (bf16[24,576]{1,0:T(8,128)(2,1)S(1)}, bf16[24,576]{1,0:T(8,128)(2,1)S(1)}, u32[]{:S(2)}, u32[]{:S(2)}) collective-permute-start(bf16[24,576]{1,0:T(8,128)(2,1)S(1)} %get-tuple-element.138), channel_id=1, source_target_pairs={{0,24},{8,16},{16,8},{24,0},{1,25},{9,17},{17,9},{25,1},{2,26},{10... | collective-permute-start | bytes 82952 | tf_op jit(solution)/shard_map/ppermute | solution.py:166
  102.5 1.4 %collective-permute-start.21 = (bf16[24,576]{1,0:T(8,128)(2,1)S(1)}, bf16[24,576]{1,0:T(8,128)(2,1)S(1)}, u32[]{:S(2)}, u32[]{:S(2)}) collective-permute-start(bf16[24,576]{1,0:T(8,128)(2,1)S(1)} %get-tuple-element.140), channel_id=1, source_target_pairs={{0,8},{8,0},{16,24},{24,16},{1,9},{9,1},{17,25},{25,17},{2,10},{10... | collective-permute-start | bytes 82952 | tf_op jit(solution)/shard_map/ppermute | solution.py:166
  103.9 1.0 fusion
  105.0 1.4 %shard_map.130 = bf16[256,768]{1,0:T(8,128)(2,1)} custom-call(f32[1,768]{1,0:T(1,128)S(1)} %copy-done.4, bf16[256,768]{1,0:T(8,128)(2,1)S(1)} %bitcast.37, bf16[256,768]{1,0:T(8,128)(2,1)S(1)} %bitcast.42, bf16[256,768]{1,0:T(8,128)(2,1)S(1)} %copy-done.10, bf16[256,768]{1,0:T(8,128)(2,1)S(1)} %collective-permute-done.17.refs_1_, ...), custom_call_target="tpu_custom_call" | custom-call | flops 786432000 | bytes 2362368 | tf_op jit(solution)/shard_map/pallas_call | solution.py:459
  106.4 1.5 %shard_map.131 = (f32[24,768]{1,0:T(8,128)}, f32[24,768]{1,0:T(8,128)}, f32[24,768]{1,0:T(8,128)}, f32[24,768]{1,0:T(8,128)}, f32[1,24]{1,0:T(1,128)}) custom-call(s32[3]{0:T(128)S(1)} %copy-done.6, f32[1,24]{1,0:T(1,128)S(1)} %dynamic-slice_bitcast_fusion.refs_1_, bf16[24,768]{1,0:T(8,128)(2,1)S(1)} %copy-done.1, bf16[24,768]{1,0:T(8,128)(2,1)S(1)} %copy-done.2, ...), custom_call_target="tpu_custom_call" | custom-call | flops 1000 | bytes 783564 | tf_op jit(solution)/shard_map/pallas_call | solution.py:459
  (93 shorter events, 12.7 us)
Async XLA Ops:
  0.6 16.1 %collective-permute-start.1 = (bf16[256,768]{1,0:T(8,128)(2,1)}, bf16[256,768]{1,0:T(8,128)(2,1)S(1)}, u32[]{:S(2)}, u32[]{:S(2)}) collective-permute-start(bf16[256,768]{1,0:T(8,128)(2,1)} %bitcast.33), channel_id=1, source_target_pairs={{0,16},{8,24},{16,0},{24,8},{1,17},{9,25},{17,1},{25,9},{2,18},{10... | collective-permute-start | bytes 1179656 | tf_op jit(solution)/shard_map/ppermute | solution.py:166
  3.7 13.1 %collective-permute-start = (bf16[256,768]{1,0:T(8,128)(2,1)}, bf16[256,768]{1,0:T(8,128)(2,1)S(1)}, u32[]{:S(2)}, u32[]{:S(2)}) collective-permute-start(bf16[256,768]{1,0:T(8,128)(2,1)} %bitcast.34), channel_id=1, source_target_pairs={{0,8},{8,0},{16,24},{24,16},{1,9},{9,1},{17,25},{25,17},{2,10},{10... | collective-permute-start | bytes 1179656 | tf_op jit(solution)/shard_map/ppermute | solution.py:166
  15.8 17.9 %copy-start.8 = (bf16[256,1,768]{2,0,1:T(8,128)(2,1)S(1)}, bf16[256,1,768]{2,0,1:T(8,128)(2,1)}, u32[]{:S(2)}) copy-start(bf16[256,1,768]{2,0,1:T(8,128)(2,1)} %param.13) | copy-start | bytes 1179652
  16.8 10.8 %collective-permute-start.2 = (bf16[256,768]{1,0:T(8,128)(2,1)}, bf16[256,768]{1,0:T(8,128)(2,1)S(1)}, u32[]{:S(2)}, u32[]{:S(2)}) collective-permute-start(bf16[256,768]{1,0:T(8,128)(2,1)} %bitcast.35), channel_id=1, source_target_pairs={{0,24},{8,16},{16,8},{24,0},{1,25},{9,17},{17,9},{25,1},{2,26},{10... | collective-permute-start | bytes 1179656 | tf_op jit(solution)/shard_map/ppermute | solution.py:166
  19.2 13.3 %collective-permute-start.5 = (bf16[4,24,768]{2,1,0:T(8,128)(2,1)S(1)}, bf16[4,24,768]{2,1,0:T(8,128)(2,1)S(1)}, u32[]{:S(2)}, u32[]{:S(2)}) collective-permute-start(bf16[4,24,768]{2,1,0:T(8,128)(2,1)S(1)} %pad_maximum_fusion.1), channel_id=1, source_target_pairs={{0,6},{2,4},{4,2},{6,0},{1,7},{3,5},{5,3},{7,1},{8,14},{10,12},{12... | collective-permute-start | bytes 442376 | tf_op jit(solution)/shard_map/ppermute | solution.py:166
  22.8 10.7 %collective-permute-start.4 = (bf16[4,24,768]{2,1,0:T(8,128)(2,1)S(1)}, bf16[4,24,768]{2,1,0:T(8,128)(2,1)S(1)}, u32[]{:S(2)}, u32[]{:S(2)}) collective-permute-start(bf16[4,24,768]{2,1,0:T(8,128)(2,1)S(1)} %pad_maximum_fusion.1), channel_id=1, source_target_pairs={{0,4},{2,6},{4,0},{6,2},{1,5},{3,7},{5,1},{7,3},{8,12},{10,14},{12... | collective-permute-start | bytes 442376 | tf_op jit(solution)/shard_map/ppermute | solution.py:166
  22.8 10.7 %collective-permute-start.3 = (bf16[4,24,768]{2,1,0:T(8,128)(2,1)S(1)}, bf16[4,24,768]{2,1,0:T(8,128)(2,1)S(1)}, u32[]{:S(2)}, u32[]{:S(2)}) collective-permute-start(bf16[4,24,768]{2,1,0:T(8,128)(2,1)S(1)} %pad_maximum_fusion.1), channel_id=1, source_target_pairs={{0,2},{2,0},{4,6},{6,4},{1,3},{3,1},{5,7},{7,5},{8,10},{10,8},{12,... | collective-permute-start | bytes 442376 | tf_op jit(solution)/shard_map/ppermute | solution.py:166
  24.9 24.5 %copy-start.5 = (s32[3]{0:T(128)}, s32[3]{0:T(128)S(1)}, u32[]{:S(2)}) copy-start(s32[3]{0:T(128)S(1)} %pad_add_fusion.refs_0_) | copy-start | bytes 40
  33.6 3.6 %collective-permute-start.9 = (bf16[4,4,24,768]{3,2,1,0:T(8,128)(2,1)S(1)}, bf16[4,4,24,768]{3,2,1,0:T(8,128)(2,1)S(1)}, u32[]{:S(2)}, u32[]{:S(2)}) collective-permute-start(bf16[4,4,24,768]{3,2,1,0:T(8,128)(2,1)S(1)} %pad_maximum_fusion.refs_1_), channel_id=1, source_target_pairs={{0,1},{1,0},{2,3},{3,2},{4,5},{5,4},{6,7},{7,6},{8,9},{9,8},{10,11... | collective-permute-start | bytes 1769480 | tf_op jit(solution)/shard_map/ppermute | solution.py:166
  33.7 24.6 %collective-permute-start.8 = (bf16[256,768]{1,0:T(8,128)(2,1)S(1)}, bf16[256,768]{1,0:T(8,128)(2,1)S(1)}, u32[]{:S(2)}, u32[]{:S(2)}) collective-permute-start(bf16[256,768]{1,0:T(8,128)(2,1)S(1)} %bitcast.39), channel_id=1, source_target_pairs={{0,24},{8,16},{16,8},{24,0},{1,25},{9,17},{17,9},{25,1},{2,26},{10... | collective-permute-start | bytes 1179656 | tf_op jit(solution)/shard_map/ppermute | solution.py:166
  34.9 25.2 %collective-permute-start.7 = (bf16[256,768]{1,0:T(8,128)(2,1)S(1)}, bf16[256,768]{1,0:T(8,128)(2,1)S(1)}, u32[]{:S(2)}, u32[]{:S(2)}) collective-permute-start(bf16[256,768]{1,0:T(8,128)(2,1)S(1)} %bitcast.40), channel_id=1, source_target_pairs={{0,16},{8,24},{16,0},{24,8},{1,17},{9,25},{17,1},{25,9},{2,18},{10... | collective-permute-start | bytes 1179656 | tf_op jit(solution)/shard_map/ppermute | solution.py:166
  35.4 24.7 %collective-permute-start.6 = (bf16[256,768]{1,0:T(8,128)(2,1)S(1)}, bf16[256,768]{1,0:T(8,128)(2,1)S(1)}, u32[]{:S(2)}, u32[]{:S(2)}) collective-permute-start(bf16[256,768]{1,0:T(8,128)(2,1)S(1)} %bitcast.41), channel_id=1, source_target_pairs={{0,8},{8,0},{16,24},{24,16},{1,9},{9,1},{17,25},{25,17},{2,10},{10... | collective-permute-start | bytes 1179656 | tf_op jit(solution)/shard_map/ppermute | solution.py:166
  56.6 21.2 %collective-permute-start.10 = (bf16[256,768]{1,0:T(8,128)(2,1)S(1)}, bf16[256,768]{1,0:T(8,128)(2,1)S(1)}, u32[]{:S(2)}, u32[]{:S(2)}) collective-permute-start(bf16[256,768]{1,0:T(8,128)(2,1)S(1)} %get-tuple-element.102), channel_id=1, source_target_pairs={{0,8},{8,0},{16,24},{24,16},{1,9},{9,1},{17,25},{25,17},{2,10},{10... | collective-permute-start | bytes 1179656 | tf_op jit(solution)/shard_map/ppermute | solution.py:166
  56.8 21.0 %collective-permute-start.11 = (bf16[256,768]{1,0:T(8,128)(2,1)S(1)}, bf16[256,768]{1,0:T(8,128)(2,1)S(1)}, u32[]{:S(2)}, u32[]{:S(2)}) collective-permute-start(bf16[256,768]{1,0:T(8,128)(2,1)S(1)} %get-tuple-element.103), channel_id=1, source_target_pairs={{0,16},{8,24},{16,0},{24,8},{1,17},{9,25},{17,1},{25,9},{2,18},{10... | collective-permute-start | bytes 1179656 | tf_op jit(solution)/shard_map/ppermute | solution.py:166
  58.3 19.5 %collective-permute-start.12 = (bf16[256,768]{1,0:T(8,128)(2,1)S(1)}, bf16[256,768]{1,0:T(8,128)(2,1)S(1)}, u32[]{:S(2)}, u32[]{:S(2)}) collective-permute-start(bf16[256,768]{1,0:T(8,128)(2,1)S(1)} %get-tuple-element.104), channel_id=1, source_target_pairs={{0,24},{8,16},{16,8},{24,0},{1,25},{9,17},{17,9},{25,1},{2,26},{10... | collective-permute-start | bytes 1179656 | tf_op jit(solution)/shard_map/ppermute | solution.py:166
  61.0 22.2 %copy-start.6 = (s32[3]{0:T(128)S(1)}, s32[3]{0:T(128)}, u32[]{:S(2)}) copy-start(s32[3]{0:T(128)} %copy-done.5) | copy-start | bytes 40
  77.8 11.8 %copy-start.21 = (bf16[256,768]{1,0:T(8,128)(2,1)S(1)}, bf16[256,768]{1,0:T(8,128)(2,1)}, u32[]{:S(2)}) copy-start(bf16[256,768]{1,0:T(8,128)(2,1)} %get-tuple-element.121) | copy-start | bytes 1179652
  77.8 2.3 %collective-permute-start.13 = (bf16[4,4,24,768]{3,2,1,0:T(8,128)(2,1)}, bf16[4,4,24,768]{3,2,1,0:T(8,128)(2,1)S(1)}, u32[]{:S(2)}, u32[]{:S(2)}) collective-permute-start(bf16[4,4,24,768]{3,2,1,0:T(8,128)(2,1)} %get-tuple-element.106), channel_id=1, source_target_pairs={{0,1},{1,0},{2,3},{3,2},{4,5},{5,4},{6,7},{7,6},{8,9},{9,8},{10,11... | collective-permute-start | bytes 1769480 | tf_op jit(solution)/shard_map/ppermute | solution.py:166
  77.9 11.1 %collective-permute-start.15 = (bf16[128,768]{1,0:T(8,128)(2,1)}, bf16[128,768]{1,0:T(8,128)(2,1)S(1)}, u32[]{:S(2)}, u32[]{:S(2)}) collective-permute-start(bf16[128,768]{1,0:T(8,128)(2,1)} %get-tuple-element.107), channel_id=1, source_target_pairs={{0,8},{8,0},{16,24},{24,16},{1,9},{9,1},{17,25},{25,17},{2,10},{10... | collective-permute-start | bytes 589832 | tf_op jit(solution)/shard_map/ppermute | solution.py:166
  78.2 10.9 %collective-permute-start.16 = (bf16[128,768]{1,0:T(8,128)(2,1)}, bf16[128,768]{1,0:T(8,128)(2,1)S(1)}, u32[]{:S(2)}, u32[]{:S(2)}) collective-permute-start(bf16[128,768]{1,0:T(8,128)(2,1)} %get-tuple-element.108), channel_id=1, source_target_pairs={{0,16},{8,24},{16,0},{24,8},{1,17},{9,25},{17,1},{25,9},{2,18},{10... | collective-permute-start | bytes 589832 | tf_op jit(solution)/shard_map/ppermute | solution.py:166
  82.0 7.1 %collective-permute-start.14 = (bf16[4,24,768]{2,1,0:T(8,128)(2,1)}, bf16[4,24,768]{2,1,0:T(8,128)(2,1)S(1)}, u32[]{:S(2)}, u32[]{:S(2)}) collective-permute-start(bf16[4,24,768]{2,1,0:T(8,128)(2,1)} %get-tuple-element.137), channel_id=1, source_target_pairs={{0,2},{2,0},{4,6},{6,4},{1,3},{3,1},{5,7},{7,5},{8,10},{10,8},{12,... | collective-permute-start | bytes 442376 | tf_op jit(solution)/shard_map/ppermute | solution.py:166
  85.8 13.5 %collective-permute-start.19 = (bf16[4,24,768]{2,1,0:T(8,128)(2,1)}, bf16[4,24,768]{2,1,0:T(8,128)(2,1)S(1)}, u32[]{:S(2)}, u32[]{:S(2)}) collective-permute-start(bf16[4,24,768]{2,1,0:T(8,128)(2,1)} %get-tuple-element.135), channel_id=1, source_target_pairs={{0,4},{2,6},{4,0},{6,2},{1,5},{3,7},{5,1},{7,3},{8,12},{10,14},{12... | collective-permute-start | bytes 442376 | tf_op jit(solution)/shard_map/ppermute | solution.py:166
  88.4 15.5 %copy-start = (bf16[256,1,768]{2,0,1:T(8,128)(2,1)S(1)}, bf16[256,1,768]{2,0,1:T(8,128)(2,1)}, u32[]{:S(2)}) copy-start(bf16[256,1,768]{2,0,1:T(8,128)(2,1)} %param.7) | copy-start | bytes 1179652
  88.4 10.9 %collective-permute-start.20 = (bf16[4,24,768]{2,1,0:T(8,128)(2,1)}, bf16[4,24,768]{2,1,0:T(8,128)(2,1)S(1)}, u32[]{:S(2)}, u32[]{:S(2)}) collective-permute-start(bf16[4,24,768]{2,1,0:T(8,128)(2,1)} %get-tuple-element.136), channel_id=1, source_target_pairs={{0,6},{2,4},{4,2},{6,0},{1,7},{3,5},{5,3},{7,1},{8,14},{10,12},{12... | collective-permute-start | bytes 442376 | tf_op jit(solution)/shard_map/ppermute | solution.py:166
  89.1 15.8 %collective-permute-start.17 = (bf16[256,768]{1,0:T(8,128)(2,1)S(1)}, bf16[256,768]{1,0:T(8,128)(2,1)S(1)}, u32[]{:S(2)}, u32[]{:S(2)}) collective-permute-start(bf16[256,768]{1,0:T(8,128)(2,1)S(1)} %add_convert_fusion.1), channel_id=1, source_target_pairs={{0,8},{8,0},{16,24},{24,16},{1,9},{9,1},{17,25},{25,17},{2,10},{10... | collective-permute-start | bytes 1179656 | tf_op jit(solution)/shard_map/ppermute | solution.py:166
  89.6 15.3 %copy-start.4 = (f32[1,768]{1,0:T(1,128)S(1)}, f32[1,768]{1,0:T(1,128)}, u32[]{:S(2)}) copy-start(f32[1,768]{1,0:T(1,128)} %reshape.54.refs_0_.gain) | copy-start | bytes 9220
  89.6 15.3 %copy-start.9 = (bf16[256,1,768]{2,0,1:T(8,128)(2,1)S(1)}, bf16[256,1,768]{2,0,1:T(8,128)(2,1)}, u32[]{:S(2)}) copy-start(bf16[256,1,768]{2,0,1:T(8,128)(2,1)} %param.13) | copy-start | bytes 1179652
  89.7 15.3 %copy-start.10 = (bf16[256,768]{1,0:T(8,128)(2,1)S(1)}, bf16[256,768]{1,0:T(8,128)(2,1)}, u32[]{:S(2)}) copy-start(bf16[256,768]{1,0:T(8,128)(2,1)} %get-tuple-element.118.refs_0_) | copy-start | bytes 1179652
  89.7 15.2 %collective-permute-start.18 = (bf16[256,768]{1,0:T(8,128)(2,1)S(1)}, bf16[256,768]{1,0:T(8,128)(2,1)S(1)}, u32[]{:S(2)}, u32[]{:S(2)}) collective-permute-start(bf16[256,768]{1,0:T(8,128)(2,1)S(1)} %add_convert_fusion), channel_id=1, source_target_pairs={{0,16},{8,24},{16,0},{24,8},{1,17},{9,25},{17,1},{25,9},{2,18},{10... | collective-permute-start | bytes 1179656 | tf_op jit(solution)/shard_map/ppermute | solution.py:166
  100.3 6.0 %collective-permute-start.23 = (bf16[24,576]{1,0:T(8,128)(2,1)S(1)}, bf16[24,576]{1,0:T(8,128)(2,1)S(1)}, u32[]{:S(2)}, u32[]{:S(2)}) collective-permute-start(bf16[24,576]{1,0:T(8,128)(2,1)S(1)} %get-tuple-element.138), channel_id=1, source_target_pairs={{0,24},{8,16},{16,8},{24,0},{1,25},{9,17},{17,9},{25,1},{2,26},{10... | collective-permute-start | bytes 82952 | tf_op jit(solution)/shard_map/ppermute | solution.py:166
  101.9 4.4 %collective-permute-start.22 = (bf16[24,576]{1,0:T(8,128)(2,1)S(1)}, bf16[24,576]{1,0:T(8,128)(2,1)S(1)}, u32[]{:S(2)}, u32[]{:S(2)}) collective-permute-start(bf16[24,576]{1,0:T(8,128)(2,1)S(1)} %get-tuple-element.139), channel_id=1, source_target_pairs={{0,16},{8,24},{16,0},{24,8},{1,17},{9,25},{17,1},{25,9},{2,18},{10... | collective-permute-start | bytes 82952 | tf_op jit(solution)/shard_map/ppermute | solution.py:166
  102.5 3.9 %collective-permute-start.21 = (bf16[24,576]{1,0:T(8,128)(2,1)S(1)}, bf16[24,576]{1,0:T(8,128)(2,1)S(1)}, u32[]{:S(2)}, u32[]{:S(2)}) collective-permute-start(bf16[24,576]{1,0:T(8,128)(2,1)S(1)} %get-tuple-element.140), channel_id=1, source_target_pairs={{0,8},{8,0},{16,24},{24,16},{1,9},{9,1},{17,25},{25,17},{2,10},{10... | collective-permute-start | bytes 82952 | tf_op jit(solution)/shard_map/ppermute | solution.py:166
  (21 other events, 53.7 us)
where the time goes:
time: 109 us; the launch traced here: 108 us
  Pallas kernels  36.2 us (33%)
  starting transfers between devices  30.3 us (28%)
  local copies, waits for them, and re-layouts  12.8 us (12%)
  waiting for transfers between devices  12.1 us (11%)
  blocking collectives  9.04 us (8%)
  other arithmetic  5.09 us (5%)
  between operations  2.28 us (2%)
    pallas_call x6, Pallas kernels, call(): pl.pallas_call(functools.partial(kernel, dims), out_shape=shapes, in_spec...  36.2 us
    ppermute x24, starting transfers between devices, swap(): return lax.ppermute(value, axis, [(i, i ^ bits) for i in range(size)])  30.3 us
    ppermute x24, waiting for transfers between devices, swap(): return lax.ppermute(value, axis, [(i, i ^ bits) for i in range(size)])  12.1 us
    unnamed x58, local copies, waits for them, and re-layouts  10.2 us
    all_to_all x1, blocking collectives, head_body(): mine = lax.all_to_all(packed, 'depth', 0, 0, tiled=True)  9.04 us
  transfers between devices with their start and end apart: 24, of which 4 were waited for; matrix products, arithmetic and copies ran while one was open for 7% of the time, Pallas kernels for 32%

commit v1 on v0

--- a/solution.py
+++ b/solution.py
@@ -514,7 +514,9 @@
         [depth, 2 * depth],
         1000,
     )
-    normed, pos, *parts = lax.optimization_barrier([normed, pos] + parts)
+    first_row = (lax.axis_index("depth") * res + pos[0] * 2 + pos[1]) * shard
+    own_gain = lax.dynamic_slice(gain, (0, first_row), (1, shard))
+    normed, pos, own_gain, *parts = lax.optimization_barrier([normed, pos, own_gain] + parts)
     w_near = jnp.stack(parts, axis=0)
     w_far = swap(w_near, "core", 2, 1)
 
@@ -530,7 +532,6 @@
         + [out_weights, blocks],
         [1, len(saved) + depth],
         8 * pass_flops,
-        44,
     )
 
     packed = (zs, depth, shard, 4 * span)
@@ -556,16 +557,17 @@
     far = swap(far, "core", 2, 1)
     dn0, dn1, dn2, dn3_top, dn3_bottom = dns
     top, bottom = swap(dn3_top, "depth", depth, 1), swap(dn3_bottom, "depth", depth, 2)
-    sums = [near[k].astype(F32) + far[k].astype(F32) for k in range(zs)]
-    low = [swap(sums[k].astype(BF16), "z", zs, k) for k in range(1, zs)]
-    low[0], top, bottom = lax.optimization_barrier((low[0], top, bottom))
+    sums = [near[k].astype(F32) + far[k].astype(F32) for k in range(1, zs)]
+    low = [swap(part.astype(BF16), "z", zs, k + 1) for k, part in enumerate(sums)]
+    low[0], top, bottom, outs = lax.optimization_barrier((low[0], top, bottom, outs))
     dn2 = dn2.astype(F32) + jnp.concatenate([top, jnp.zeros_like(top)], axis=0).astype(F32)
     dn1 = dn1.astype(F32) + jnp.concatenate([jnp.zeros_like(bottom), bottom], axis=0).astype(F32)
-    dn1 = swap(dn1.astype(BF16), "depth", depth, 1)
-    dn2 = swap(dn2.astype(BF16), "depth", depth, 2)
-    low[0], outs = lax.optimization_barrier((low[0], outs))
     final_result = (x.astype(F32) + sum(o.astype(F32) for o in outs)).astype(BF16)
-    acc = sums[0] + sum(p.astype(F32) for p in low)
+    dn1, dn2, final_result = lax.optimization_barrier(
+        (dn1.astype(BF16), dn2.astype(BF16), final_result)
+    )
+    dn1, dn2 = swap(dn1, "depth", depth, 1), swap(dn2, "depth", depth, 2)
+    acc = near[0].astype(F32) + far[0].astype(F32) + sum(p.astype(F32) for p in low)
     parts = [
         swap(acc[k, :, : 3 * span].astype(BF16), "depth", depth, k) for k in range(1, depth)
     ]
@@ -580,8 +582,6 @@
         16,
     )[0]
     alignment, *parts = lax.optimization_barrier([alignment] + parts)
-    first_row = (lax.axis_index("depth") * res + pos[0] * 2 + pos[1]) * shard
-    own_gain = lax.dynamic_slice(gain, (0, first_row), (1, shard))
     grad_query, grad_key, grad_value, grad_out, gain_rows = call(
         finish_kernel,
         dims,

time: 109 us -> 100 us (0.917)
  local copies, waits for them, and re-layouts: 12.8 us -> 4.64 us
  waiting for transfers between devices: 12.1 us -> 14 us
  between operations: 2.28 us -> 0.91 us
    unnamed x58 -> x40, local copies, waits for them, and re-layouts: 10.2 us -> 2.6 us
    ppermute x24, waiting for transfers between devices: 12.1 us -> 14 us  [swap(): return lax.ppermute(value, axis, [(i, i ^ bits) for i in range(size)])]
  transfers between devices with their start and end apart: 24 -> 24, of which waited for: 4 -> 9; matrix products, arithmetic and copies ran while one was open for 7% -> 7% of each run, Pallas kernels for 32% -> 35%
where the time goes in v1:
time: 100 us; the launch traced here: 99.9 us
  Pallas kernels  36.2 us (36%)
  starting transfers between devices  30.2 us (30%)
  waiting for transfers between devices  14 us (14%)
  blocking collectives  9.04 us (9%)
  other arithmetic  4.9 us (5%)
  local copies, waits for them, and re-layouts  4.64 us (5%)
    pallas_call x6, Pallas kernels, call(): pl.pallas_call(functools.partial(kernel, dims), out_shape=shapes, in_spec...  36.2 us
    ppermute x24, starting transfers between devices, swap(): return lax.ppermute(value, axis, [(i, i ^ bits) for i in range(size)])  30.2 us
    ppermute x24, waiting for transfers between devices, swap(): return lax.ppermute(value, axis, [(i, i ^ bits) for i in range(size)])  14 us
    all_to_all x1, blocking collectives, head_body(): mine = lax.all_to_all(packed, 'depth', 0, 0, tiled=True)  9.04 us
    unnamed x40, local copies, waits for them, and re-layouts  2.6 us
  transfers between devices with their start and end apart: 24, of which 9 were waited for; matrix products, arithmetic and copies ran while one was open for 7% of the time, Pallas kernels for 35%

profile of v1, /device:TPU:0, one launch (start us, length us, event | category | flops | bytes accessed | tf_op | source)
XLA Modules:
  0.0 99.9 jit_solution(18157348249776806714)
XLA Ops:
  0.6 3.0 %collective-permute-start.1 = (bf16[256,768]{1,0:T(8,128)(2,1)}, bf16[256,768]{1,0:T(8,128)(2,1)S(1)}, u32[]{:S(2)}, u32[]{:S(2)}) collective-permute-start(bf16[256,768]{1,0:T(8,128)(2,1)} %bitcast.30), channel_id=1, source_target_pairs={{0,16},{8,24},{16,0},{24,8},{1,17},{9,25},{17,1},{25,9},{2,18},{10... | collective-permute-start | bytes 1179656 | tf_op jit(solution)/shard_map/ppermute | solution.py:166
  3.7 1.5 %collective-permute-start = (bf16[256,768]{1,0:T(8,128)(2,1)}, bf16[256,768]{1,0:T(8,128)(2,1)S(1)}, u32[]{:S(2)}, u32[]{:S(2)}) collective-permute-start(bf16[256,768]{1,0:T(8,128)(2,1)} %bitcast.31), channel_id=1, source_target_pairs={{0,8},{8,0},{16,24},{24,16},{1,9},{9,1},{17,25},{25,17},{2,10},{10... | collective-permute-start | bytes 1179656 | tf_op jit(solution)/shard_map/ppermute | solution.py:166
  5.2 1.6 %shard_map.126 = (bf16[4,24,576]{2,1,0:T(8,128)(2,1)}, bf16[4,24,192]{2,1,0:T(8,128)(2,1)}) custom-call(bf16[24,768]{1,0:T(8,128)(2,1)} %refs_2_.1, bf16[24,768]{1,0:T(8,128)(2,1)} %refs_3_.1, bf16[24,768]{1,0:T(8,128)(2,1)} %refs_4_.1, bf16[24,768]{1,0:T(8,128)(2,1)} %w_out.1), custom_call_target="tpu_custom_call" | custom-call | flops 1000 | bytes 294912 | tf_op jit(solution)/shard_map/pallas_call | solution.py:459
  6.7 9.0 %all_to_all.5 = bf16[4,24,576]{2,1,0:T(8,128)(2,1)S(1)} all-to-all(bf16[4,24,576]{2,1,0:T(8,128)(2,1)} %get-tuple-element.73), channel_id=1, replica_groups=mesh['depth'=4,'z'=4,'core'=2] {'depth'}, dimensions={0} | all-to-all | bytes 221184 | tf_op jit(solution)/shard_map/all_to_all | solution.py:494
  15.8 0.9 pad_maximum_fusion.1
  16.8 2.5 %collective-permute-start.2 = (bf16[256,768]{1,0:T(8,128)(2,1)}, bf16[256,768]{1,0:T(8,128)(2,1)S(1)}, u32[]{:S(2)}, u32[]{:S(2)}) collective-permute-start(bf16[256,768]{1,0:T(8,128)(2,1)} %bitcast.32), channel_id=1, source_target_pairs={{0,24},{8,16},{16,8},{24,0},{1,25},{9,17},{17,9},{25,1},{2,26},{10... | collective-permute-start | bytes 1179656 | tf_op jit(solution)/shard_map/ppermute | solution.py:166
  19.2 3.6 %collective-permute-start.5 = (bf16[4,24,768]{2,1,0:T(8,128)(2,1)S(1)}, bf16[4,24,768]{2,1,0:T(8,128)(2,1)S(1)}, u32[]{:S(2)}, u32[]{:S(2)}) collective-permute-start(bf16[4,24,768]{2,1,0:T(8,128)(2,1)S(1)} %pad_maximum_fusion.1), channel_id=1, source_target_pairs={{0,6},{2,4},{4,2},{6,0},{1,7},{3,5},{5,3},{7,1},{8,14},{10,12},{12... | collective-permute-start | bytes 442376 | tf_op jit(solution)/shard_map/ppermute | solution.py:166
  24.4 1.3 %reshape.51.refs_0_.gain = f32[1,768]{1,0:T(1,128)} reshape(f32[768]{0:T(1024)} %param.8) | data formatting | bytes 6144 | tf_op jit(solution)/shard_map/reshape | solution.py:480
  26.2 1.4 %collective-permute-done.2.refs_4_ = bf16[256,768]{1,0:T(8,128)(2,1)S(1)} collective-permute-done((bf16[256,768]{1,0:T(8,128)(2,1)}, bf16[256,768]{1,0:T(8,128)(2,1)S(1)}, u32[]{:S(2)}, u32[]{:S(2)}) %collective-permute-start.2) | collective-permute-done | bytes 393248 | tf_op jit(solution)/shard_map/ppermute | solution.py:166
  28.3 4.2 %shard_map.127 = (bf16[1024,768]{1,0:T(8,128)(2,1)}, bf16[768,1024]{1,0:T(8,128)(2,1)}) custom-call(f32[1,768]{1,0:T(1,128)} %reshape.51.refs_0_.gain, bf16[256,768]{1,0:T(8,128)(2,1)} %bitcast.33, bf16[256,768]{1,0:T(8,128)(2,1)} %copy-done.12, bf16[256,768]{1,0:T(8,128)(2,1)} %copy-done.11, bf16[256,768]{1,0:T(8,128)(2,1)} %copy-done.13), custom_call_target="tpu_custom_call" | custom-call | flops 1000 | bytes 4721664 | tf_op jit(solution)/shard_map/pallas_call | solution.py:459
  32.6 1.0 collective-permute-done.4
  33.7 1.2 %collective-permute-start.8 = (bf16[256,768]{1,0:T(8,128)(2,1)S(1)}, bf16[256,768]{1,0:T(8,128)(2,1)S(1)}, u32[]{:S(2)}, u32[]{:S(2)}) collective-permute-start(bf16[256,768]{1,0:T(8,128)(2,1)S(1)} %bitcast.36), channel_id=1, source_target_pairs={{0,24},{8,16},{16,8},{24,0},{1,25},{9,17},{17,9},{25,1},{2,26},{10... | collective-permute-start | bytes 1179656 | tf_op jit(solution)/shard_map/ppermute | solution.py:166
  35.4 1.8 %collective-permute-start.6 = (bf16[256,768]{1,0:T(8,128)(2,1)S(1)}, bf16[256,768]{1,0:T(8,128)(2,1)S(1)}, u32[]{:S(2)}, u32[]{:S(2)}) collective-permute-start(bf16[256,768]{1,0:T(8,128)(2,1)S(1)} %bitcast.38), channel_id=1, source_target_pairs={{0,8},{8,0},{16,24},{24,16},{1,9},{9,1},{17,25},{25,17},{2,10},{10... | collective-permute-start | bytes 1179656 | tf_op jit(solution)/shard_map/ppermute | solution.py:166
  37.3 0.9 copy-done.16
  38.1 10.9 %shard_map.128 = (bf16[1024,192]{1,0:T(8,128)(2,1)}, bf16[1024,192]{1,0:T(8,128)(2,1)}, bf16[1024,192]{1,0:T(8,128)(2,1)}, bf16[192,1024]{1,0:T(8,128)(2,1)}, f3...) custom-call(s32[3]{0:T(128)} %pad_add_fusion.refs_0_, ...), custom_call_target="tpu_custom_call" | custom-call | flops 3221225472 | bytes 7876620 | tf_op jit(solution)/shard_map/pallas_call | solution.py:459
  49.3 1.5 %collective-permute-start.11 = (bf16[256,768]{1,0:T(8,128)(2,1)}, bf16[256,768]{1,0:T(8,128)(2,1)S(1)}, u32[]{:S(2)}, u32[]{:S(2)}) collective-permute-start(bf16[256,768]{1,0:T(8,128)(2,1)} %get-tuple-element.106), channel_id=1, source_target_pairs={{0,16},{8,24},{16,0},{24,8},{1,17},{9,25},{17,1},{25,9},{2,18},{10... | collective-permute-start | bytes 1179656 | tf_op jit(solution)/shard_map/ppermute | solution.py:166
  50.8 1.8 %collective-permute-start.12 = (bf16[256,768]{1,0:T(8,128)(2,1)}, bf16[256,768]{1,0:T(8,128)(2,1)S(1)}, u32[]{:S(2)}, u32[]{:S(2)}) collective-permute-start(bf16[256,768]{1,0:T(8,128)(2,1)} %get-tuple-element.107), channel_id=1, source_target_pairs={{0,24},{8,16},{16,8},{24,0},{1,25},{9,17},{17,9},{25,1},{2,26},{10... | collective-permute-start | bytes 1179656 | tf_op jit(solution)/shard_map/ppermute | solution.py:166
  52.6 2.1 %collective-permute-done.7.refs_3_ = bf16[256,768]{1,0:T(8,128)(2,1)S(1)} collective-permute-done((bf16[256,768]{1,0:T(8,128)(2,1)S(1)}, bf16[256,768]{1,0:T(8,128)(2,1)S(1)}, u32[]{:S(2)}, u32[]{:S(2)}) %collective-permute-start.7) | collective-permute-done | bytes 393248 | tf_op jit(solution)/shard_map/ppermute | solution.py:166
  55.6 16.7 %shard_map.129 = (bf16[4,4,24,768]{3,2,1,0:T(8,128)(2,1)}, bf16[4,4,24,768]{3,2,1,0:T(8,128)(2,1)}, bf16[256,768]{1,0:T(8,128)(2,1)}, bf16[256,768]{1,0:T(8,128)...) custom-call(s32[3]{0:T(128)} %pad_add_fusion.refs_0_, ...), custom_call_target="tpu_custom_call" | custom-call | flops 9663676416 | bytes 9449484 | tf_op jit(solution)/shard_map/pallas_call | solution.py:459
  73.0 1.2 %collective-permute-start.16 = (bf16[128,768]{1,0:T(8,128)(2,1)}, bf16[128,768]{1,0:T(8,128)(2,1)S(1)}, u32[]{:S(2)}, u32[]{:S(2)}) collective-permute-start(bf16[128,768]{1,0:T(8,128)(2,1)} %get-tuple-element.112), channel_id=1, source_target_pairs={{0,16},{8,24},{16,0},{24,8},{1,17},{9,25},{17,1},{25,9},{2,18},{10... | collective-permute-start | bytes 589832 | tf_op jit(solution)/shard_map/ppermute | solution.py:166
  74.6 1.2 %fusion.1 = (bf16[4,24,768]{2,1,0:T(8,128)(2,1)S(1)}, bf16[4,24,768]{2,1,0:T(8,128)(2,1)S(1)}, bf16[4,24,768]{2,1,0:T(8,128)(2,1)S(1)}) fusion(bf16[4,4,24,768]{3,2,1,0:T(8,128)(2,1)S(1)} %collective-permute-done.13, bf16[4,4,24,768]{3,2,1,0:T(8,128)(2,1)} %get-tuple-element.109), kind=kLoop, calls=%fused_computation.9 | loop fusion | flops 884736 | bytes 1327104 | tf_op jit(solution)/shard_map/convert_element_type | solution.py:561
  75.8 1.2 %collective-permute-start.14 = (bf16[4,24,768]{2,1,0:T(8,128)(2,1)S(1)}, bf16[4,24,768]{2,1,0:T(8,128)(2,1)S(1)}, u32[]{:S(2)}, u32[]{:S(2)}) collective-permute-start(bf16[4,24,768]{2,1,0:T(8,128)(2,1)S(1)} %get-tuple-element.143), channel_id=1, source_target_pairs={{0,2},{2,0},{4,6},{6,4},{1,3},{3,1},{5,7},{7,5},{8,10},{10,8},{12,... | collective-permute-start | bytes 442376 | tf_op jit(solution)/shard_map/ppermute | solution.py:166
  77.0 2.6 %collective-permute-start.19 = (bf16[4,24,768]{2,1,0:T(8,128)(2,1)S(1)}, bf16[4,24,768]{2,1,0:T(8,128)(2,1)S(1)}, u32[]{:S(2)}, u32[]{:S(2)}) collective-permute-start(bf16[4,24,768]{2,1,0:T(8,128)(2,1)S(1)} %get-tuple-element.141), channel_id=1, source_target_pairs={{0,4},{2,6},{4,0},{6,2},{1,5},{3,7},{5,1},{7,3},{8,12},{10,14},{12... | collective-permute-start | bytes 442376 | tf_op jit(solution)/shard_map/ppermute | solution.py:166
  80.2 3.8 %collective-permute-done.14 = bf16[4,24,768]{2,1,0:T(8,128)(2,1)S(1)} collective-permute-done((bf16[4,24,768]{2,1,0:T(8,128)(2,1)S(1)}, bf16[4,24,768]{2,1,0:T(8,128)(2,1)S(1)}, u32[]{:S(2)}, u32[]{:S(2)}) %collective-permute-start.14) | collective-permute-done | bytes 147488 | tf_op jit(solution)/shard_map/ppermute | solution.py:166
  84.1 1.0 %add_convert_fusion = bf16[256,768]{1,0:T(8,128)(2,1)} fusion(bf16[256,768]{1,0:T(8,128)(2,1)S(1)} %collective-permute-done.12, bf16[256,768]{1,0:T(8,128)(2,1)S(1)} %collective-permute-done.11, bf16[256,768]{1,0:T(8,128)(2,1)S(1)} %collective-permute-done.10, bf16[256,768]{1,0:T(8,128)(2,1)S(1)} %copy-done.10, bf16[256,1,768]{2,0,1:T(8,128)(2,1)S(1)} %copy-done), kind=kLoop, calls=%fused_computation | loop fusion | flops 1966080 | bytes 2359296 | tf_op jit(solution)/shard_map/convert_element_type | solution.py:565
  85.9 1.2 %collective-permute-start.18 = (bf16[256,768]{1,0:T(8,128)(2,1)S(1)}, bf16[256,768]{1,0:T(8,128)(2,1)S(1)}, u32[]{:S(2)}, u32[]{:S(2)}) collective-permute-start(bf16[256,768]{1,0:T(8,128)(2,1)S(1)} %get-tuple-element.127), channel_id=1, source_target_pairs={{0,16},{8,24},{16,0},{24,8},{1,17},{9,25},{17,1},{25,9},{2,18},{10... | collective-permute-start | bytes 1179656 | tf_op jit(solution)/shard_map/ppermute | solution.py:166
  87.0 3.9 %collective-permute-done.19 = bf16[4,24,768]{2,1,0:T(8,128)(2,1)S(1)} collective-permute-done((bf16[4,24,768]{2,1,0:T(8,128)(2,1)S(1)}, bf16[4,24,768]{2,1,0:T(8,128)(2,1)S(1)}, u32[]{:S(2)}, u32[]{:S(2)}) %collective-permute-start.19) | collective-permute-done | bytes 147488 | tf_op jit(solution)/shard_map/ppermute | solution.py:166
  91.0 1.0 %fusion.3 = (bf16[4,24,768]{2,1,0:T(8,128)(2,1)S(1)}, f32[4,24,768]{2,1,0:T(8,128)S(1)}) fusion(bf16[4,24,768]{2,1,0:T(8,128)(2,1)S(1)} %collective-permute-done.20, bf16[4,24,768]{2,1,0:T(8,128)(2,1)S(1)} %collective-permute-done.19, bf16[4,24,768]{2,1,0:T(8,128)(2,1)S(1)} %collective-permute-done.14, ...), kind=kLoop, calls=%fused_computation.17 | loop fusion | flops 737280 | bytes 1179648 | tf_op jit(solution)/shard_map/convert.2
  92.0 1.6 %collective-permute-start.23 = (bf16[24,576]{1,0:T(8,128)(2,1)S(1)}, bf16[24,576]{1,0:T(8,128)(2,1)S(1)}, u32[]{:S(2)}, u32[]{:S(2)}) collective-permute-start(bf16[24,576]{1,0:T(8,128)(2,1)S(1)} %get-tuple-element.144), channel_id=1, source_target_pairs={{0,24},{8,16},{16,8},{24,0},{1,25},{9,17},{17,9},{25,1},{2,26},{10... | collective-permute-start | bytes 82952 | tf_op jit(solution)/shard_map/ppermute | solution.py:166
  94.5 1.1 %collective-permute-start.21 = (bf16[24,576]{1,0:T(8,128)(2,1)S(1)}, bf16[24,576]{1,0:T(8,128)(2,1)S(1)}, u32[]{:S(2)}, u32[]{:S(2)}) collective-permute-start(bf16[24,576]{1,0:T(8,128)(2,1)S(1)} %get-tuple-element.146), channel_id=1, source_target_pairs={{0,8},{8,0},{16,24},{24,16},{1,9},{9,1},{17,25},{25,17},{2,10},{10... | collective-permute-start | bytes 82952 | tf_op jit(solution)/shard_map/ppermute | solution.py:166
  96.1 1.4 %shard_map.130 = bf16[256,768]{1,0:T(8,128)(2,1)} custom-call(f32[1,768]{1,0:T(1,128)S(1)} %copy-done.4, bf16[256,768]{1,0:T(8,128)(2,1)S(1)} %bitcast.34, bf16[256,768]{1,0:T(8,128)(2,1)S(1)} %bitcast.39, bf16[256,768]{1,0:T(8,128)(2,1)S(1)} %copy-done.8, bf16[256,768]{1,0:T(8,128)(2,1)S(1)} %collective-permute-done.17.refs_1_, ...), custom_call_target="tpu_custom_call" | custom-call | flops 786432000 | bytes 2362368 | tf_op jit(solution)/shard_map/pallas_call | solution.py:459
  98.4 1.5 %shard_map.131 = (f32[24,768]{1,0:T(8,128)}, f32[24,768]{1,0:T(8,128)}, f32[24,768]{1,0:T(8,128)}, f32[24,768]{1,0:T(8,128)}, f32[1,24]{1,0:T(1,128)}) custom-call(s32[3]{0:T(128)S(1)} %copy-done.5, f32[1,24]{1,0:T(1,128)S(1)} %dynamic-slice_bitcast_fusion.refs_1_, bf16[24,768]{1,0:T(8,128)(2,1)S(1)} %copy-done.1, bf16[24,768]{1,0:T(8,128)(2,1)S(1)} %copy-done.2, ...), custom_call_target="tpu_custom_call" | custom-call | flops 1000 | bytes 783564 | tf_op jit(solution)/shard_map/pallas_call | solution.py:459
  (73 shorter events, 9.6 us)
Async XLA Ops:
  0.6 16.1 %collective-permute-start.1 = (bf16[256,768]{1,0:T(8,128)(2,1)}, bf16[256,768]{1,0:T(8,128)(2,1)S(1)}, u32[]{:S(2)}, u32[]{:S(2)}) collective-permute-start(bf16[256,768]{1,0:T(8,128)(2,1)} %bitcast.30), channel_id=1, source_target_pairs={{0,16},{8,24},{16,0},{24,8},{1,17},{9,25},{17,1},{25,9},{2,18},{10... | collective-permute-start | bytes 1179656 | tf_op jit(solution)/shard_map/ppermute | solution.py:166
  3.7 13.1 %collective-permute-start = (bf16[256,768]{1,0:T(8,128)(2,1)}, bf16[256,768]{1,0:T(8,128)(2,1)S(1)}, u32[]{:S(2)}, u32[]{:S(2)}) collective-permute-start(bf16[256,768]{1,0:T(8,128)(2,1)} %bitcast.31), channel_id=1, source_target_pairs={{0,8},{8,0},{16,24},{24,16},{1,9},{9,1},{17,25},{25,17},{2,10},{10... | collective-permute-start | bytes 1179656 | tf_op jit(solution)/shard_map/ppermute | solution.py:166
  15.8 17.9 %copy-start.6 = (bf16[256,1,768]{2,0,1:T(8,128)(2,1)S(1)}, bf16[256,1,768]{2,0,1:T(8,128)(2,1)}, u32[]{:S(2)}) copy-start(bf16[256,1,768]{2,0,1:T(8,128)(2,1)} %param.13) | copy-start | bytes 1179652
  16.8 10.8 %collective-permute-start.2 = (bf16[256,768]{1,0:T(8,128)(2,1)}, bf16[256,768]{1,0:T(8,128)(2,1)S(1)}, u32[]{:S(2)}, u32[]{:S(2)}) collective-permute-start(bf16[256,768]{1,0:T(8,128)(2,1)} %bitcast.32), channel_id=1, source_target_pairs={{0,24},{8,16},{16,8},{24,0},{1,25},{9,17},{17,9},{25,1},{2,26},{10... | collective-permute-start | bytes 1179656 | tf_op jit(solution)/shard_map/ppermute | solution.py:166
  19.2 13.3 %collective-permute-start.5 = (bf16[4,24,768]{2,1,0:T(8,128)(2,1)S(1)}, bf16[4,24,768]{2,1,0:T(8,128)(2,1)S(1)}, u32[]{:S(2)}, u32[]{:S(2)}) collective-permute-start(bf16[4,24,768]{2,1,0:T(8,128)(2,1)S(1)} %pad_maximum_fusion.1), channel_id=1, source_target_pairs={{0,6},{2,4},{4,2},{6,0},{1,7},{3,5},{5,3},{7,1},{8,14},{10,12},{12... | collective-permute-start | bytes 442376 | tf_op jit(solution)/shard_map/ppermute | solution.py:166
  22.8 10.7 %collective-permute-start.4 = (bf16[4,24,768]{2,1,0:T(8,128)(2,1)S(1)}, bf16[4,24,768]{2,1,0:T(8,128)(2,1)S(1)}, u32[]{:S(2)}, u32[]{:S(2)}) collective-permute-start(bf16[4,24,768]{2,1,0:T(8,128)(2,1)S(1)} %pad_maximum_fusion.1), channel_id=1, source_target_pairs={{0,4},{2,6},{4,0},{6,2},{1,5},{3,7},{5,1},{7,3},{8,12},{10,14},{12... | collective-permute-start | bytes 442376 | tf_op jit(solution)/shard_map/ppermute | solution.py:166
  22.8 10.7 %collective-permute-start.3 = (bf16[4,24,768]{2,1,0:T(8,128)(2,1)S(1)}, bf16[4,24,768]{2,1,0:T(8,128)(2,1)S(1)}, u32[]{:S(2)}, u32[]{:S(2)}) collective-permute-start(bf16[4,24,768]{2,1,0:T(8,128)(2,1)S(1)} %pad_maximum_fusion.1), channel_id=1, source_target_pairs={{0,2},{2,0},{4,6},{6,4},{1,3},{3,1},{5,7},{7,5},{8,10},{10,8},{12,... | collective-permute-start | bytes 442376 | tf_op jit(solution)/shard_map/ppermute | solution.py:166
  33.6 3.6 %collective-permute-start.9 = (bf16[4,4,24,768]{3,2,1,0:T(8,128)(2,1)S(1)}, bf16[4,4,24,768]{3,2,1,0:T(8,128)(2,1)S(1)}, u32[]{:S(2)}, u32[]{:S(2)}) collective-permute-start(bf16[4,4,24,768]{3,2,1,0:T(8,128)(2,1)S(1)} %pad_maximum_fusion.refs_1_), channel_id=1, source_target_pairs={{0,1},{1,0},{2,3},{3,2},{4,5},{5,4},{6,7},{7,6},{8,9},{9,8},{10,11... | collective-permute-start | bytes 1769480 | tf_op jit(solution)/shard_map/ppermute | solution.py:166
  33.7 17.1 %collective-permute-start.8 = (bf16[256,768]{1,0:T(8,128)(2,1)S(1)}, bf16[256,768]{1,0:T(8,128)(2,1)S(1)}, u32[]{:S(2)}, u32[]{:S(2)}) collective-permute-start(bf16[256,768]{1,0:T(8,128)(2,1)S(1)} %bitcast.36), channel_id=1, source_target_pairs={{0,24},{8,16},{16,8},{24,0},{1,25},{9,17},{17,9},{25,1},{2,26},{10... | collective-permute-start | bytes 1179656 | tf_op jit(solution)/shard_map/ppermute | solution.py:166
  34.9 19.7 %collective-permute-start.7 = (bf16[256,768]{1,0:T(8,128)(2,1)S(1)}, bf16[256,768]{1,0:T(8,128)(2,1)S(1)}, u32[]{:S(2)}, u32[]{:S(2)}) collective-permute-start(bf16[256,768]{1,0:T(8,128)(2,1)S(1)} %bitcast.37), channel_id=1, source_target_pairs={{0,16},{8,24},{16,0},{24,8},{1,17},{9,25},{17,1},{25,9},{2,18},{10... | collective-permute-start | bytes 1179656 | tf_op jit(solution)/shard_map/ppermute | solution.py:166
  35.4 19.2 %collective-permute-start.6 = (bf16[256,768]{1,0:T(8,128)(2,1)S(1)}, bf16[256,768]{1,0:T(8,128)(2,1)S(1)}, u32[]{:S(2)}, u32[]{:S(2)}) collective-permute-start(bf16[256,768]{1,0:T(8,128)(2,1)S(1)} %bitcast.38), channel_id=1, source_target_pairs={{0,8},{8,0},{16,24},{24,16},{1,9},{9,1},{17,25},{25,17},{2,10},{10... | collective-permute-start | bytes 1179656 | tf_op jit(solution)/shard_map/ppermute | solution.py:166
  49.0 23.3 %collective-permute-start.10 = (bf16[256,768]{1,0:T(8,128)(2,1)}, bf16[256,768]{1,0:T(8,128)(2,1)S(1)}, u32[]{:S(2)}, u32[]{:S(2)}) collective-permute-start(bf16[256,768]{1,0:T(8,128)(2,1)} %get-tuple-element.105), channel_id=1, source_target_pairs={{0,8},{8,0},{16,24},{24,16},{1,9},{9,1},{17,25},{25,17},{2,10},{10... | collective-permute-start | bytes 1179656 | tf_op jit(solution)/shard_map/ppermute | solution.py:166
  49.3 23.0 %collective-permute-start.11 = (bf16[256,768]{1,0:T(8,128)(2,1)}, bf16[256,768]{1,0:T(8,128)(2,1)S(1)}, u32[]{:S(2)}, u32[]{:S(2)}) collective-permute-start(bf16[256,768]{1,0:T(8,128)(2,1)} %get-tuple-element.106), channel_id=1, source_target_pairs={{0,16},{8,24},{16,0},{24,8},{1,17},{9,25},{17,1},{25,9},{2,18},{10... | collective-permute-start | bytes 1179656 | tf_op jit(solution)/shard_map/ppermute | solution.py:166
  50.8 21.5 %collective-permute-start.12 = (bf16[256,768]{1,0:T(8,128)(2,1)}, bf16[256,768]{1,0:T(8,128)(2,1)S(1)}, u32[]{:S(2)}, u32[]{:S(2)}) collective-permute-start(bf16[256,768]{1,0:T(8,128)(2,1)} %get-tuple-element.107), channel_id=1, source_target_pairs={{0,24},{8,16},{16,8},{24,0},{1,25},{9,17},{17,9},{25,1},{2,26},{10... | collective-permute-start | bytes 1179656 | tf_op jit(solution)/shard_map/ppermute | solution.py:166
  72.3 11.8 %copy-start = (bf16[256,1,768]{2,0,1:T(8,128)(2,1)S(1)}, bf16[256,1,768]{2,0,1:T(8,128)(2,1)}, u32[]{:S(2)}) copy-start(bf16[256,1,768]{2,0,1:T(8,128)(2,1)} %param.7) | copy-start | bytes 1179652
  72.3 11.8 %copy-start.10 = (bf16[256,768]{1,0:T(8,128)(2,1)S(1)}, bf16[256,768]{1,0:T(8,128)(2,1)}, u32[]{:S(2)}) copy-start(bf16[256,768]{1,0:T(8,128)(2,1)} %get-tuple-element.120) | copy-start | bytes 1179652
  72.3 12.8 %copy-start.14 = (bf16[256,768]{1,0:T(8,128)(2,1)S(1)}, bf16[256,768]{1,0:T(8,128)(2,1)}, u32[]{:S(2)}) copy-start(bf16[256,768]{1,0:T(8,128)(2,1)} %get-tuple-element.108) | copy-start | bytes 1179652
  72.3 12.8 %copy-start.15 = (bf16[256,768]{1,0:T(8,128)(2,1)S(1)}, bf16[256,768]{1,0:T(8,128)(2,1)}, u32[]{:S(2)}) copy-start(bf16[256,768]{1,0:T(8,128)(2,1)} %get-tuple-element.118) | copy-start | bytes 1179652
  72.3 2.3 %collective-permute-start.13 = (bf16[4,4,24,768]{3,2,1,0:T(8,128)(2,1)}, bf16[4,4,24,768]{3,2,1,0:T(8,128)(2,1)S(1)}, u32[]{:S(2)}, u32[]{:S(2)}) collective-permute-start(bf16[4,4,24,768]{3,2,1,0:T(8,128)(2,1)} %get-tuple-element.110), channel_id=1, source_target_pairs={{0,1},{1,0},{2,3},{3,2},{4,5},{5,4},{6,7},{7,6},{8,9},{9,8},{10,11... | collective-permute-start | bytes 1769480 | tf_op jit(solution)/shard_map/ppermute | solution.py:166
  72.4 7.8 %collective-permute-start.15 = (bf16[128,768]{1,0:T(8,128)(2,1)}, bf16[128,768]{1,0:T(8,128)(2,1)S(1)}, u32[]{:S(2)}, u32[]{:S(2)}) collective-permute-start(bf16[128,768]{1,0:T(8,128)(2,1)} %get-tuple-element.111), channel_id=1, source_target_pairs={{0,8},{8,0},{16,24},{24,16},{1,9},{9,1},{17,25},{25,17},{2,10},{10... | collective-permute-start | bytes 589832 | tf_op jit(solution)/shard_map/ppermute | solution.py:166
  73.0 7.2 %collective-permute-start.16 = (bf16[128,768]{1,0:T(8,128)(2,1)}, bf16[128,768]{1,0:T(8,128)(2,1)S(1)}, u32[]{:S(2)}, u32[]{:S(2)}) collective-permute-start(bf16[128,768]{1,0:T(8,128)(2,1)} %get-tuple-element.112), channel_id=1, source_target_pairs={{0,16},{8,24},{16,0},{24,8},{1,17},{9,25},{17,1},{25,9},{2,18},{10... | collective-permute-start | bytes 589832 | tf_op jit(solution)/shard_map/ppermute | solution.py:166
  75.8 8.3 %collective-permute-start.14 = (bf16[4,24,768]{2,1,0:T(8,128)(2,1)S(1)}, bf16[4,24,768]{2,1,0:T(8,128)(2,1)S(1)}, u32[]{:S(2)}, u32[]{:S(2)}) collective-permute-start(bf16[4,24,768]{2,1,0:T(8,128)(2,1)S(1)} %get-tuple-element.143), channel_id=1, source_target_pairs={{0,2},{2,0},{4,6},{6,4},{1,3},{3,1},{5,7},{7,5},{8,10},{10,8},{12,... | collective-permute-start | bytes 442376 | tf_op jit(solution)/shard_map/ppermute | solution.py:166
  77.0 14.0 %collective-permute-start.19 = (bf16[4,24,768]{2,1,0:T(8,128)(2,1)S(1)}, bf16[4,24,768]{2,1,0:T(8,128)(2,1)S(1)}, u32[]{:S(2)}, u32[]{:S(2)}) collective-permute-start(bf16[4,24,768]{2,1,0:T(8,128)(2,1)S(1)} %get-tuple-element.141), channel_id=1, source_target_pairs={{0,4},{2,6},{4,0},{6,2},{1,5},{3,7},{5,1},{7,3},{8,12},{10,14},{12... | collective-permute-start | bytes 442376 | tf_op jit(solution)/shard_map/ppermute | solution.py:166
  79.6 11.4 %collective-permute-start.20 = (bf16[4,24,768]{2,1,0:T(8,128)(2,1)S(1)}, bf16[4,24,768]{2,1,0:T(8,128)(2,1)S(1)}, u32[]{:S(2)}, u32[]{:S(2)}) collective-permute-start(bf16[4,24,768]{2,1,0:T(8,128)(2,1)S(1)} %get-tuple-element.142), channel_id=1, source_target_pairs={{0,6},{2,4},{4,2},{6,0},{1,7},{3,5},{5,3},{7,1},{8,14},{10,12},{12... | collective-permute-start | bytes 442376 | tf_op jit(solution)/shard_map/ppermute | solution.py:166
  85.1 11.0 %copy-start.4 = (f32[1,768]{1,0:T(1,128)S(1)}, f32[1,768]{1,0:T(1,128)}, u32[]{:S(2)}) copy-start(f32[1,768]{1,0:T(1,128)} %reshape.51.refs_0_.gain) | copy-start | bytes 9220
  85.1 11.0 %copy-start.7 = (bf16[256,1,768]{2,0,1:T(8,128)(2,1)S(1)}, bf16[256,1,768]{2,0,1:T(8,128)(2,1)}, u32[]{:S(2)}) copy-start(bf16[256,1,768]{2,0,1:T(8,128)(2,1)} %param.13) | copy-start | bytes 1179652
  85.1 11.0 %copy-start.8 = (bf16[256,768]{1,0:T(8,128)(2,1)S(1)}, bf16[256,768]{1,0:T(8,128)(2,1)}, u32[]{:S(2)}) copy-start(bf16[256,768]{1,0:T(8,128)(2,1)} %get-tuple-element.125.refs_0_) | copy-start | bytes 1179652
  85.2 10.8 %collective-permute-start.17 = (bf16[256,768]{1,0:T(8,128)(2,1)S(1)}, bf16[256,768]{1,0:T(8,128)(2,1)S(1)}, u32[]{:S(2)}, u32[]{:S(2)}) collective-permute-start(bf16[256,768]{1,0:T(8,128)(2,1)S(1)} %get-tuple-element.126), channel_id=1, source_target_pairs={{0,8},{8,0},{16,24},{24,16},{1,9},{9,1},{17,25},{25,17},{2,10},{10... | collective-permute-start | bytes 1179656 | tf_op jit(solution)/shard_map/ppermute | solution.py:166
  85.9 10.2 %collective-permute-start.18 = (bf16[256,768]{1,0:T(8,128)(2,1)S(1)}, bf16[256,768]{1,0:T(8,128)(2,1)S(1)}, u32[]{:S(2)}, u32[]{:S(2)}) collective-permute-start(bf16[256,768]{1,0:T(8,128)(2,1)S(1)} %get-tuple-element.127), channel_id=1, source_target_pairs={{0,16},{8,24},{16,0},{24,8},{1,17},{9,25},{17,1},{25,9},{2,18},{10... | collective-permute-start | bytes 1179656 | tf_op jit(solution)/shard_map/ppermute | solution.py:166
  92.0 5.5 %collective-permute-start.23 = (bf16[24,576]{1,0:T(8,128)(2,1)S(1)}, bf16[24,576]{1,0:T(8,128)(2,1)S(1)}, u32[]{:S(2)}, u32[]{:S(2)}) collective-permute-start(bf16[24,576]{1,0:T(8,128)(2,1)S(1)} %get-tuple-element.144), channel_id=1, source_target_pairs={{0,24},{8,16},{16,8},{24,0},{1,25},{9,17},{17,9},{25,1},{2,26},{10... | collective-permute-start | bytes 82952 | tf_op jit(solution)/shard_map/ppermute | solution.py:166
  93.6 3.9 %collective-permute-start.22 = (bf16[24,576]{1,0:T(8,128)(2,1)S(1)}, bf16[24,576]{1,0:T(8,128)(2,1)S(1)}, u32[]{:S(2)}, u32[]{:S(2)}) collective-permute-start(bf16[24,576]{1,0:T(8,128)(2,1)S(1)} %get-tuple-element.145), channel_id=1, source_target_pairs={{0,16},{8,24},{16,0},{24,8},{1,17},{9,25},{17,1},{25,9},{2,18},{10... | collective-permute-start | bytes 82952 | tf_op jit(solution)/shard_map/ppermute | solution.py:166
  94.5 3.9 %collective-permute-start.21 = (bf16[24,576]{1,0:T(8,128)(2,1)S(1)}, bf16[24,576]{1,0:T(8,128)(2,1)S(1)}, u32[]{:S(2)}, u32[]{:S(2)}) collective-permute-start(bf16[24,576]{1,0:T(8,128)(2,1)S(1)} %get-tuple-element.146), channel_id=1, source_target_pairs={{0,8},{8,0},{16,24},{24,16},{1,9},{9,1},{17,25},{25,17},{2,10},{10... | collective-permute-start | bytes 82952 | tf_op jit(solution)/shard_map/ppermute | solution.py:166
  (12 other events, 58.1 us)

commit v2 on v1

--- a/solution.py
+++ b/solution.py
@@ -265,10 +265,10 @@
     query[...] = (SCALE * dot(normed[...], wq[...])).astype(BF16)
     key = dot(normed[...], wk[...])
     keys[...] = key.astype(BF16)
-    keys_t[...] = jnp.transpose(key).astype(BF16)
+    keys_t[...] = jnp.transpose(key.astype(BF16))
     value = dot(normed[...], wv[...])
     values[...] = value.astype(BF16)
-    values_t[...] = jnp.transpose(value).astype(BF16)
+    values_t[...] = jnp.transpose(value.astype(BF16))
     for src, dst in ((query, query_h), (keys, keys_h), (values, values_h), (keys_t, keys_t_h)):
         sender.send(src, dst)
 
@@ -328,8 +328,6 @@
     )
     loaded, later = 7 + depth, copies[7 + depth :]
 
-    d_keys[...] = jnp.zeros_like(d_keys)
-    d_values[...] = jnp.zeros_like(d_values)
     for copy in copies[: 2 + depth]:
         copy.wait()
     part = dot(gs[...], w_out[...], (1, 1)).astype(BF16)
@@ -341,33 +339,38 @@
         copy.wait()
     masks = head_masks(span)
 
-    def step(j, _):
-        cols = pl.ds(pl.multiple_of(j * block, block), block)
-        q_block, g_block = query[cols, :], d_att[cols, :]
-        qs = [q_block * m for m in masks]
-        ds = [g_block * m for m in masks]
-
-        def pair(h):
-            return dot(keys[...], qs[h], (1, 1)), dot(values[...], ds[h], (1, 1))
-
-        pairs = [pair(h) for h in range(min(2, heads))]
-        for h in range(heads):
-            scores, d_probs = pairs[h]
-            probs = jnp.exp(scores - lse[h, :, cols])
-            d_scores = (probs * (d_probs - delta[h, :, cols])).astype(BF16)
-            if h + 2 < heads:
-                pairs.append(pair(h + 2))
-            values_add = dot(probs.astype(BF16), ds[h])
-            keys_add = dot(d_scores, qs[h])
-            value_part = values_add if h == 0 else value_part + values_add
-            key_part = keys_add if h == 0 else key_part + keys_add
-            lanes = slice(h * HEAD_DIM, (h + 1) * HEAD_DIM)
-            d_query_t[lanes, cols] = SCALE * dot(keys_t[lanes, :], d_scores)
-        d_values[...] += value_part.astype(BF16).astype(F32)
-        d_keys[...] += key_part.astype(BF16).astype(F32)
-        return 0
-
-    lax.fori_loop(0, depth, step, 0)
+    units = [(j, h) for j in range(depth) for h in range(heads)]
+
+    def pair(j, h):
+        rows = slice(j * block, (j + 1) * block)
+        q_head, g_head = query[rows, :] * masks[h], d_att[rows, :] * masks[h]
+        scores, d_probs = dot(keys[...], q_head, (1, 1)), dot(values[...], g_head, (1, 1))
+        return q_head, g_head, scores, d_probs
+
+    def add_block(j, parts):
+        probs, d_scores, qs, ds = (list(p) for p in zip(*parts))
+        value_part = dot(jnp.concatenate(probs, axis=1), jnp.concatenate(ds, axis=0))
+        key_part = dot(jnp.concatenate(d_scores, axis=1), jnp.concatenate(qs, axis=0))
+        d_values[...] = value_part if j == 0 else d_values[...] + value_part
+        d_keys[...] = key_part if j == 0 else d_keys[...] + key_part
+
+    ready = [pair(*unit) for unit in units[:2]]
+    parts, waiting = [], None
+    for i, (j, h) in enumerate(units):
+        cols, lanes = slice(j * block, (j + 1) * block), slice(h * HEAD_DIM, (h + 1) * HEAD_DIM)
+        q_head, g_head, scores, d_probs = ready.pop(0)
+        probs = jnp.exp(scores - lse[h, :, cols])
+        d_scores = (probs * (d_probs - delta[h, :, cols])).astype(BF16)
+        if i + 2 < len(units):
+            ready.append(pair(*units[i + 2]))
+        parts.append((probs.astype(BF16), d_scores, q_head, g_head))
+        d_query_t[lanes, cols] = SCALE * dot(keys_t[lanes, :], d_scores)
+        if waiting is not None:
+            add_block(*waiting)
+            waiting = None
+        if h == heads - 1:
+            parts, waiting = [], (j, parts)
+    add_block(*waiting)
     for copy in later:
         copy.wait()
     d_query = jnp.transpose(d_query_t[...]).astype(BF16)

time: 100 us -> 101 us (1.010)
  no operation moved by 1% of the time
where the time goes in v2:
time: 101 us
  Pallas kernels  37 us (37%)
  starting transfers between devices  30.2 us (30%)
  waiting for transfers between devices  14.2 us (14%)
  blocking collectives  9.04 us (9%)
  other arithmetic  4.9 us (5%)
  local copies, waits for them, and re-layouts  4.64 us (5%)
    pallas_call x6, Pallas kernels, call(): pl.pallas_call(functools.partial(kernel, dims), out_shape=shapes, in_spec...  37 us
    ppermute x24, starting transfers between devices, swap(): return lax.ppermute(value, axis, [(i, i ^ bits) for i in range(size)])  30.2 us
    ppermute x24, waiting for transfers between devices, swap(): return lax.ppermute(value, axis, [(i, i ^ bits) for i in range(size)])  14.2 us
    all_to_all x1, blocking collectives, head_body(): mine = lax.all_to_all(packed, 'depth', 0, 0, tiled=True)  9.04 us
    unnamed x40, local copies, waits for them, and re-layouts  2.6 us
  transfers between devices with their start and end apart: 24, of which 9 were waited for; matrix products, arithmetic and copies ran while one was open for 7% of the time, Pallas kernels for 35%

profile of v2, /device:TPU:0, one launch (start us, length us, event | category | flops | bytes accessed | tf_op | source)
XLA Modules:
  0.0 100.9 jit_solution(17436290068350653714)
XLA Ops:
  0.6 3.0 %collective-permute-start.1 = (bf16[256,768]{1,0:T(8,128)(2,1)}, bf16[256,768]{1,0:T(8,128)(2,1)S(1)}, u32[]{:S(2)}, u32[]{:S(2)}) collective-permute-start(bf16[256,768]{1,0:T(8,128)(2,1)} %bitcast.30), channel_id=1, source_target_pairs={{0,16},{8,24},{16,0},{24,8},{1,17},{9,25},{17,1},{25,9},{2,18},{10... | collective-permute-start | bytes 1179656 | tf_op jit(solution)/shard_map/ppermute | solution.py:166
  3.7 1.5 %collective-permute-start = (bf16[256,768]{1,0:T(8,128)(2,1)}, bf16[256,768]{1,0:T(8,128)(2,1)S(1)}, u32[]{:S(2)}, u32[]{:S(2)}) collective-permute-start(bf16[256,768]{1,0:T(8,128)(2,1)} %bitcast.31), channel_id=1, source_target_pairs={{0,8},{8,0},{16,24},{24,16},{1,9},{9,1},{17,25},{25,17},{2,10},{10... | collective-permute-start | bytes 1179656 | tf_op jit(solution)/shard_map/ppermute | solution.py:166
  5.2 1.6 %shard_map.126 = (bf16[4,24,576]{2,1,0:T(8,128)(2,1)}, bf16[4,24,192]{2,1,0:T(8,128)(2,1)}) custom-call(bf16[24,768]{1,0:T(8,128)(2,1)} %refs_2_.1, bf16[24,768]{1,0:T(8,128)(2,1)} %refs_3_.1, bf16[24,768]{1,0:T(8,128)(2,1)} %refs_4_.1, bf16[24,768]{1,0:T(8,128)(2,1)} %w_out.1), custom_call_target="tpu_custom_call" | custom-call | flops 1000 | bytes 294912 | tf_op jit(solution)/shard_map/pallas_call | solution.py:462
  6.7 9.0 %all_to_all.5 = bf16[4,24,576]{2,1,0:T(8,128)(2,1)S(1)} all-to-all(bf16[4,24,576]{2,1,0:T(8,128)(2,1)} %get-tuple-element.73), channel_id=1, replica_groups=mesh['depth'=4,'z'=4,'core'=2] {'depth'}, dimensions={0} | all-to-all | bytes 221184 | tf_op jit(solution)/shard_map/all_to_all | solution.py:497
  15.8 0.9 pad_maximum_fusion.1
  16.8 2.5 %collective-permute-start.2 = (bf16[256,768]{1,0:T(8,128)(2,1)}, bf16[256,768]{1,0:T(8,128)(2,1)S(1)}, u32[]{:S(2)}, u32[]{:S(2)}) collective-permute-start(bf16[256,768]{1,0:T(8,128)(2,1)} %bitcast.32), channel_id=1, source_target_pairs={{0,24},{8,16},{16,8},{24,0},{1,25},{9,17},{17,9},{25,1},{2,26},{10... | collective-permute-start | bytes 1179656 | tf_op jit(solution)/shard_map/ppermute | solution.py:166
  19.2 3.6 %collective-permute-start.5 = (bf16[4,24,768]{2,1,0:T(8,128)(2,1)S(1)}, bf16[4,24,768]{2,1,0:T(8,128)(2,1)S(1)}, u32[]{:S(2)}, u32[]{:S(2)}) collective-permute-start(bf16[4,24,768]{2,1,0:T(8,128)(2,1)S(1)} %pad_maximum_fusion.1), channel_id=1, source_target_pairs={{0,6},{2,4},{4,2},{6,0},{1,7},{3,5},{5,3},{7,1},{8,14},{10,12},{12... | collective-permute-start | bytes 442376 | tf_op jit(solution)/shard_map/ppermute | solution.py:166
  24.4 1.3 %reshape.51.refs_0_.gain = f32[1,768]{1,0:T(1,128)} reshape(f32[768]{0:T(1024)} %param.8) | data formatting | bytes 6144 | tf_op jit(solution)/shard_map/reshape | solution.py:483
  26.2 1.4 %collective-permute-done.2.refs_4_ = bf16[256,768]{1,0:T(8,128)(2,1)S(1)} collective-permute-done((bf16[256,768]{1,0:T(8,128)(2,1)}, bf16[256,768]{1,0:T(8,128)(2,1)S(1)}, u32[]{:S(2)}, u32[]{:S(2)}) %collective-permute-start.2) | collective-permute-done | bytes 393248 | tf_op jit(solution)/shard_map/ppermute | solution.py:166
  28.3 4.2 %shard_map.127 = (bf16[1024,768]{1,0:T(8,128)(2,1)}, bf16[768,1024]{1,0:T(8,128)(2,1)}) custom-call(f32[1,768]{1,0:T(1,128)} %reshape.51.refs_0_.gain, bf16[256,768]{1,0:T(8,128)(2,1)} %bitcast.33, bf16[256,768]{1,0:T(8,128)(2,1)} %copy-done.12, bf16[256,768]{1,0:T(8,128)(2,1)} %copy-done.11, bf16[256,768]{1,0:T(8,128)(2,1)} %copy-done.13), custom_call_target="tpu_custom_call" | custom-call | flops 1000 | bytes 4721664 | tf_op jit(solution)/shard_map/pallas_call | solution.py:462
  32.6 1.0 collective-permute-done.4
  33.7 1.2 %collective-permute-start.8 = (bf16[256,768]{1,0:T(8,128)(2,1)S(1)}, bf16[256,768]{1,0:T(8,128)(2,1)S(1)}, u32[]{:S(2)}, u32[]{:S(2)}) collective-permute-start(bf16[256,768]{1,0:T(8,128)(2,1)S(1)} %bitcast.36), channel_id=1, source_target_pairs={{0,24},{8,16},{16,8},{24,0},{1,25},{9,17},{17,9},{25,1},{2,26},{10... | collective-permute-start | bytes 1179656 | tf_op jit(solution)/shard_map/ppermute | solution.py:166
  35.4 1.8 %collective-permute-start.6 = (bf16[256,768]{1,0:T(8,128)(2,1)S(1)}, bf16[256,768]{1,0:T(8,128)(2,1)S(1)}, u32[]{:S(2)}, u32[]{:S(2)}) collective-permute-start(bf16[256,768]{1,0:T(8,128)(2,1)S(1)} %bitcast.38), channel_id=1, source_target_pairs={{0,8},{8,0},{16,24},{24,16},{1,9},{9,1},{17,25},{25,17},{2,10},{10... | collective-permute-start | bytes 1179656 | tf_op jit(solution)/shard_map/ppermute | solution.py:166
  37.3 0.9 copy-done.16
  38.1 10.7 %shard_map.128 = (bf16[1024,192]{1,0:T(8,128)(2,1)}, bf16[1024,192]{1,0:T(8,128)(2,1)}, bf16[1024,192]{1,0:T(8,128)(2,1)}, bf16[192,1024]{1,0:T(8,128)(2,1)}, f3...) custom-call(s32[3]{0:T(128)} %pad_add_fusion.refs_0_, ...), custom_call_target="tpu_custom_call" | custom-call | flops 3221225472 | bytes 7876620 | tf_op jit(solution)/shard_map/pallas_call | solution.py:462
  49.1 1.5 %collective-permute-start.11 = (bf16[256,768]{1,0:T(8,128)(2,1)}, bf16[256,768]{1,0:T(8,128)(2,1)S(1)}, u32[]{:S(2)}, u32[]{:S(2)}) collective-permute-start(bf16[256,768]{1,0:T(8,128)(2,1)} %get-tuple-element.106), channel_id=1, source_target_pairs={{0,16},{8,24},{16,0},{24,8},{1,17},{9,25},{17,1},{25,9},{2,18},{10... | collective-permute-start | bytes 1179656 | tf_op jit(solution)/shard_map/ppermute | solution.py:166
  50.7 1.8 %collective-permute-start.12 = (bf16[256,768]{1,0:T(8,128)(2,1)}, bf16[256,768]{1,0:T(8,128)(2,1)S(1)}, u32[]{:S(2)}, u32[]{:S(2)}) collective-permute-start(bf16[256,768]{1,0:T(8,128)(2,1)} %get-tuple-element.107), channel_id=1, source_target_pairs={{0,24},{8,16},{16,8},{24,0},{1,25},{9,17},{17,9},{25,1},{2,26},{10... | collective-permute-start | bytes 1179656 | tf_op jit(solution)/shard_map/ppermute | solution.py:166
  52.4 2.2 %collective-permute-done.7.refs_3_ = bf16[256,768]{1,0:T(8,128)(2,1)S(1)} collective-permute-done((bf16[256,768]{1,0:T(8,128)(2,1)S(1)}, bf16[256,768]{1,0:T(8,128)(2,1)S(1)}, u32[]{:S(2)}, u32[]{:S(2)}) %collective-permute-start.7) | collective-permute-done | bytes 393248 | tf_op jit(solution)/shard_map/ppermute | solution.py:166
  55.6 17.7 %shard_map.129 = (bf16[4,4,24,768]{3,2,1,0:T(8,128)(2,1)}, bf16[4,4,24,768]{3,2,1,0:T(8,128)(2,1)}, bf16[256,768]{1,0:T(8,128)(2,1)}, bf16[256,768]{1,0:T(8,128)...) custom-call(s32[3]{0:T(128)} %pad_add_fusion.refs_0_, ...), custom_call_target="tpu_custom_call" | custom-call | flops 9663676416 | bytes 9449484 | tf_op jit(solution)/shard_map/pallas_call | solution.py:462
  74.0 1.2 %collective-permute-start.16 = (bf16[128,768]{1,0:T(8,128)(2,1)}, bf16[128,768]{1,0:T(8,128)(2,1)S(1)}, u32[]{:S(2)}, u32[]{:S(2)}) collective-permute-start(bf16[128,768]{1,0:T(8,128)(2,1)} %get-tuple-element.112), channel_id=1, source_target_pairs={{0,16},{8,24},{16,0},{24,8},{1,17},{9,25},{17,1},{25,9},{2,18},{10... | collective-permute-start | bytes 589832 | tf_op jit(solution)/shard_map/ppermute | solution.py:166
  75.6 1.2 %fusion.1 = (bf16[4,24,768]{2,1,0:T(8,128)(2,1)S(1)}, bf16[4,24,768]{2,1,0:T(8,128)(2,1)S(1)}, bf16[4,24,768]{2,1,0:T(8,128)(2,1)S(1)}) fusion(bf16[4,4,24,768]{3,2,1,0:T(8,128)(2,1)S(1)} %collective-permute-done.13, bf16[4,4,24,768]{3,2,1,0:T(8,128)(2,1)} %get-tuple-element.109), kind=kLoop, calls=%fused_computation.9 | loop fusion | flops 884736 | bytes 1327104 | tf_op jit(solution)/shard_map/convert_element_type | solution.py:564
  76.8 1.2 %collective-permute-start.14 = (bf16[4,24,768]{2,1,0:T(8,128)(2,1)S(1)}, bf16[4,24,768]{2,1,0:T(8,128)(2,1)S(1)}, u32[]{:S(2)}, u32[]{:S(2)}) collective-permute-start(bf16[4,24,768]{2,1,0:T(8,128)(2,1)S(1)} %get-tuple-element.143), channel_id=1, source_target_pairs={{0,2},{2,0},{4,6},{6,4},{1,3},{3,1},{5,7},{7,5},{8,10},{10,8},{12,... | collective-permute-start | bytes 442376 | tf_op jit(solution)/shard_map/ppermute | solution.py:166
  78.0 2.6 %collective-permute-start.19 = (bf16[4,24,768]{2,1,0:T(8,128)(2,1)S(1)}, bf16[4,24,768]{2,1,0:T(8,128)(2,1)S(1)}, u32[]{:S(2)}, u32[]{:S(2)}) collective-permute-start(bf16[4,24,768]{2,1,0:T(8,128)(2,1)S(1)} %get-tuple-element.141), channel_id=1, source_target_pairs={{0,4},{2,6},{4,0},{6,2},{1,5},{3,7},{5,1},{7,3},{8,12},{10,14},{12... | collective-permute-start | bytes 442376 | tf_op jit(solution)/shard_map/ppermute | solution.py:166
  81.2 3.8 %collective-permute-done.14 = bf16[4,24,768]{2,1,0:T(8,128)(2,1)S(1)} collective-permute-done((bf16[4,24,768]{2,1,0:T(8,128)(2,1)S(1)}, bf16[4,24,768]{2,1,0:T(8,128)(2,1)S(1)}, u32[]{:S(2)}, u32[]{:S(2)}) %collective-permute-start.14) | collective-permute-done | bytes 147488 | tf_op jit(solution)/shard_map/ppermute | solution.py:166
  85.1 1.0 %add_convert_fusion = bf16[256,768]{1,0:T(8,128)(2,1)} fusion(bf16[256,768]{1,0:T(8,128)(2,1)S(1)} %collective-permute-done.12, bf16[256,768]{1,0:T(8,128)(2,1)S(1)} %collective-permute-done.11, bf16[256,768]{1,0:T(8,128)(2,1)S(1)} %collective-permute-done.10, bf16[256,768]{1,0:T(8,128)(2,1)S(1)} %copy-done.10, bf16[256,1,768]{2,0,1:T(8,128)(2,1)S(1)} %copy-done), kind=kLoop, calls=%fused_computation | loop fusion | flops 1966080 | bytes 2359296 | tf_op jit(solution)/shard_map/convert_element_type | solution.py:568
  86.9 1.2 %collective-permute-start.18 = (bf16[256,768]{1,0:T(8,128)(2,1)S(1)}, bf16[256,768]{1,0:T(8,128)(2,1)S(1)}, u32[]{:S(2)}, u32[]{:S(2)}) collective-permute-start(bf16[256,768]{1,0:T(8,128)(2,1)S(1)} %get-tuple-element.127), channel_id=1, source_target_pairs={{0,16},{8,24},{16,0},{24,8},{1,17},{9,25},{17,1},{25,9},{2,18},{10... | collective-permute-start | bytes 1179656 | tf_op jit(solution)/shard_map/ppermute | solution.py:166
  88.0 3.9 %collective-permute-done.19 = bf16[4,24,768]{2,1,0:T(8,128)(2,1)S(1)} collective-permute-done((bf16[4,24,768]{2,1,0:T(8,128)(2,1)S(1)}, bf16[4,24,768]{2,1,0:T(8,128)(2,1)S(1)}, u32[]{:S(2)}, u32[]{:S(2)}) %collective-permute-start.19) | collective-permute-done | bytes 147488 | tf_op jit(solution)/shard_map/ppermute | solution.py:166
  91.9 1.0 %fusion.3 = (bf16[4,24,768]{2,1,0:T(8,128)(2,1)S(1)}, f32[4,24,768]{2,1,0:T(8,128)S(1)}) fusion(bf16[4,24,768]{2,1,0:T(8,128)(2,1)S(1)} %collective-permute-done.20, bf16[4,24,768]{2,1,0:T(8,128)(2,1)S(1)} %collective-permute-done.19, bf16[4,24,768]{2,1,0:T(8,128)(2,1)S(1)} %collective-permute-done.14, ...), kind=kLoop, calls=%fused_computation.17 | loop fusion | flops 737280 | bytes 1179648 | tf_op jit(solution)/shard_map/convert.2
  93.0 1.6 %collective-permute-start.23 = (bf16[24,576]{1,0:T(8,128)(2,1)S(1)}, bf16[24,576]{1,0:T(8,128)(2,1)S(1)}, u32[]{:S(2)}, u32[]{:S(2)}) collective-permute-start(bf16[24,576]{1,0:T(8,128)(2,1)S(1)} %get-tuple-element.144), channel_id=1, source_target_pairs={{0,24},{8,16},{16,8},{24,0},{1,25},{9,17},{17,9},{25,1},{2,26},{10... | collective-permute-start | bytes 82952 | tf_op jit(solution)/shard_map/ppermute | solution.py:166
  95.5 1.1 %collective-permute-start.21 = (bf16[24,576]{1,0:T(8,128)(2,1)S(1)}, bf16[24,576]{1,0:T(8,128)(2,1)S(1)}, u32[]{:S(2)}, u32[]{:S(2)}) collective-permute-start(bf16[24,576]{1,0:T(8,128)(2,1)S(1)} %get-tuple-element.146), channel_id=1, source_target_pairs={{0,8},{8,0},{16,24},{24,16},{1,9},{9,1},{17,25},{25,17},{2,10},{10... | collective-permute-start | bytes 82952 | tf_op jit(solution)/shard_map/ppermute | solution.py:166
  97.1 1.4 %shard_map.130 = bf16[256,768]{1,0:T(8,128)(2,1)} custom-call(f32[1,768]{1,0:T(1,128)S(1)} %copy-done.4, bf16[256,768]{1,0:T(8,128)(2,1)S(1)} %bitcast.34, bf16[256,768]{1,0:T(8,128)(2,1)S(1)} %bitcast.39, bf16[256,768]{1,0:T(8,128)(2,1)S(1)} %copy-done.8, bf16[256,768]{1,0:T(8,128)(2,1)S(1)} %collective-permute-done.17.refs_1_, ...), custom_call_target="tpu_custom_call" | custom-call | flops 786432000 | bytes 2362368 | tf_op jit(solution)/shard_map/pallas_call | solution.py:462
  99.4 1.5 %shard_map.131 = (f32[24,768]{1,0:T(8,128)}, f32[24,768]{1,0:T(8,128)}, f32[24,768]{1,0:T(8,128)}, f32[24,768]{1,0:T(8,128)}, f32[1,24]{1,0:T(1,128)}) custom-call(s32[3]{0:T(128)S(1)} %copy-done.5, f32[1,24]{1,0:T(1,128)S(1)} %dynamic-slice_bitcast_fusion.refs_1_, bf16[24,768]{1,0:T(8,128)(2,1)S(1)} %copy-done.1, bf16[24,768]{1,0:T(8,128)(2,1)S(1)} %copy-done.2, ...), custom_call_target="tpu_custom_call" | custom-call | flops 1000 | bytes 783564 | tf_op jit(solution)/shard_map/pallas_call | solution.py:462
  (73 shorter events, 9.6 us)
Async XLA Ops:
  0.6 16.1 %collective-permute-start.1 = (bf16[256,768]{1,0:T(8,128)(2,1)}, bf16[256,768]{1,0:T(8,128)(2,1)S(1)}, u32[]{:S(2)}, u32[]{:S(2)}) collective-permute-start(bf16[256,768]{1,0:T(8,128)(2,1)} %bitcast.30), channel_id=1, source_target_pairs={{0,16},{8,24},{16,0},{24,8},{1,17},{9,25},{17,1},{25,9},{2,18},{10... | collective-permute-start | bytes 1179656 | tf_op jit(solution)/shard_map/ppermute | solution.py:166
  3.7 13.1 %collective-permute-start = (bf16[256,768]{1,0:T(8,128)(2,1)}, bf16[256,768]{1,0:T(8,128)(2,1)S(1)}, u32[]{:S(2)}, u32[]{:S(2)}) collective-permute-start(bf16[256,768]{1,0:T(8,128)(2,1)} %bitcast.31), channel_id=1, source_target_pairs={{0,8},{8,0},{16,24},{24,16},{1,9},{9,1},{17,25},{25,17},{2,10},{10... | collective-permute-start | bytes 1179656 | tf_op jit(solution)/shard_map/ppermute | solution.py:166
  15.8 17.9 %copy-start.6 = (bf16[256,1,768]{2,0,1:T(8,128)(2,1)S(1)}, bf16[256,1,768]{2,0,1:T(8,128)(2,1)}, u32[]{:S(2)}) copy-start(bf16[256,1,768]{2,0,1:T(8,128)(2,1)} %param.13) | copy-start | bytes 1179652
  16.8 10.8 %collective-permute-start.2 = (bf16[256,768]{1,0:T(8,128)(2,1)}, bf16[256,768]{1,0:T(8,128)(2,1)S(1)}, u32[]{:S(2)}, u32[]{:S(2)}) collective-permute-start(bf16[256,768]{1,0:T(8,128)(2,1)} %bitcast.32), channel_id=1, source_target_pairs={{0,24},{8,16},{16,8},{24,0},{1,25},{9,17},{17,9},{25,1},{2,26},{10... | collective-permute-start | bytes 1179656 | tf_op jit(solution)/shard_map/ppermute | solution.py:166
  19.2 13.3 %collective-permute-start.5 = (bf16[4,24,768]{2,1,0:T(8,128)(2,1)S(1)}, bf16[4,24,768]{2,1,0:T(8,128)(2,1)S(1)}, u32[]{:S(2)}, u32[]{:S(2)}) collective-permute-start(bf16[4,24,768]{2,1,0:T(8,128)(2,1)S(1)} %pad_maximum_fusion.1), channel_id=1, source_target_pairs={{0,6},{2,4},{4,2},{6,0},{1,7},{3,5},{5,3},{7,1},{8,14},{10,12},{12... | collective-permute-start | bytes 442376 | tf_op jit(solution)/shard_map/ppermute | solution.py:166
  22.8 10.7 %collective-permute-start.4 = (bf16[4,24,768]{2,1,0:T(8,128)(2,1)S(1)}, bf16[4,24,768]{2,1,0:T(8,128)(2,1)S(1)}, u32[]{:S(2)}, u32[]{:S(2)}) collective-permute-start(bf16[4,24,768]{2,1,0:T(8,128)(2,1)S(1)} %pad_maximum_fusion.1), channel_id=1, source_target_pairs={{0,4},{2,6},{4,0},{6,2},{1,5},{3,7},{5,1},{7,3},{8,12},{10,14},{12... | collective-permute-start | bytes 442376 | tf_op jit(solution)/shard_map/ppermute | solution.py:166
  22.8 10.7 %collective-permute-start.3 = (bf16[4,24,768]{2,1,0:T(8,128)(2,1)S(1)}, bf16[4,24,768]{2,1,0:T(8,128)(2,1)S(1)}, u32[]{:S(2)}, u32[]{:S(2)}) collective-permute-start(bf16[4,24,768]{2,1,0:T(8,128)(2,1)S(1)} %pad_maximum_fusion.1), channel_id=1, source_target_pairs={{0,2},{2,0},{4,6},{6,4},{1,3},{3,1},{5,7},{7,5},{8,10},{10,8},{12,... | collective-permute-start | bytes 442376 | tf_op jit(solution)/shard_map/ppermute | solution.py:166
  33.6 3.6 %collective-permute-start.9 = (bf16[4,4,24,768]{3,2,1,0:T(8,128)(2,1)S(1)}, bf16[4,4,24,768]{3,2,1,0:T(8,128)(2,1)S(1)}, u32[]{:S(2)}, u32[]{:S(2)}) collective-permute-start(bf16[4,4,24,768]{3,2,1,0:T(8,128)(2,1)S(1)} %pad_maximum_fusion.refs_1_), channel_id=1, source_target_pairs={{0,1},{1,0},{2,3},{3,2},{4,5},{5,4},{6,7},{7,6},{8,9},{9,8},{10,11... | collective-permute-start | bytes 1769480 | tf_op jit(solution)/shard_map/ppermute | solution.py:166
  33.7 17.0 %collective-permute-start.8 = (bf16[256,768]{1,0:T(8,128)(2,1)S(1)}, bf16[256,768]{1,0:T(8,128)(2,1)S(1)}, u32[]{:S(2)}, u32[]{:S(2)}) collective-permute-start(bf16[256,768]{1,0:T(8,128)(2,1)S(1)} %bitcast.36), channel_id=1, source_target_pairs={{0,24},{8,16},{16,8},{24,0},{1,25},{9,17},{17,9},{25,1},{2,26},{10... | collective-permute-start | bytes 1179656 | tf_op jit(solution)/shard_map/ppermute | solution.py:166
  34.9 19.7 %collective-permute-start.7 = (bf16[256,768]{1,0:T(8,128)(2,1)S(1)}, bf16[256,768]{1,0:T(8,128)(2,1)S(1)}, u32[]{:S(2)}, u32[]{:S(2)}) collective-permute-start(bf16[256,768]{1,0:T(8,128)(2,1)S(1)} %bitcast.37), channel_id=1, source_target_pairs={{0,16},{8,24},{16,0},{24,8},{1,17},{9,25},{17,1},{25,9},{2,18},{10... | collective-permute-start | bytes 1179656 | tf_op jit(solution)/shard_map/ppermute | solution.py:166
  35.4 19.2 %collective-permute-start.6 = (bf16[256,768]{1,0:T(8,128)(2,1)S(1)}, bf16[256,768]{1,0:T(8,128)(2,1)S(1)}, u32[]{:S(2)}, u32[]{:S(2)}) collective-permute-start(bf16[256,768]{1,0:T(8,128)(2,1)S(1)} %bitcast.38), channel_id=1, source_target_pairs={{0,8},{8,0},{16,24},{24,16},{1,9},{9,1},{17,25},{25,17},{2,10},{10... | collective-permute-start | bytes 1179656 | tf_op jit(solution)/shard_map/ppermute | solution.py:166
  48.9 24.4 %collective-permute-start.10 = (bf16[256,768]{1,0:T(8,128)(2,1)}, bf16[256,768]{1,0:T(8,128)(2,1)S(1)}, u32[]{:S(2)}, u32[]{:S(2)}) collective-permute-start(bf16[256,768]{1,0:T(8,128)(2,1)} %get-tuple-element.105), channel_id=1, source_target_pairs={{0,8},{8,0},{16,24},{24,16},{1,9},{9,1},{17,25},{25,17},{2,10},{10... | collective-permute-start | bytes 1179656 | tf_op jit(solution)/shard_map/ppermute | solution.py:166
  49.1 24.2 %collective-permute-start.11 = (bf16[256,768]{1,0:T(8,128)(2,1)}, bf16[256,768]{1,0:T(8,128)(2,1)S(1)}, u32[]{:S(2)}, u32[]{:S(2)}) collective-permute-start(bf16[256,768]{1,0:T(8,128)(2,1)} %get-tuple-element.106), channel_id=1, source_target_pairs={{0,16},{8,24},{16,0},{24,8},{1,17},{9,25},{17,1},{25,9},{2,18},{10... | collective-permute-start | bytes 1179656 | tf_op jit(solution)/shard_map/ppermute | solution.py:166
  50.7 22.6 %collective-permute-start.12 = (bf16[256,768]{1,0:T(8,128)(2,1)}, bf16[256,768]{1,0:T(8,128)(2,1)S(1)}, u32[]{:S(2)}, u32[]{:S(2)}) collective-permute-start(bf16[256,768]{1,0:T(8,128)(2,1)} %get-tuple-element.107), channel_id=1, source_target_pairs={{0,24},{8,16},{16,8},{24,0},{1,25},{9,17},{17,9},{25,1},{2,26},{10... | collective-permute-start | bytes 1179656 | tf_op jit(solution)/shard_map/ppermute | solution.py:166
  73.3 11.8 %copy-start = (bf16[256,1,768]{2,0,1:T(8,128)(2,1)S(1)}, bf16[256,1,768]{2,0,1:T(8,128)(2,1)}, u32[]{:S(2)}) copy-start(bf16[256,1,768]{2,0,1:T(8,128)(2,1)} %param.7) | copy-start | bytes 1179652
  73.3 11.8 %copy-start.10 = (bf16[256,768]{1,0:T(8,128)(2,1)S(1)}, bf16[256,768]{1,0:T(8,128)(2,1)}, u32[]{:S(2)}) copy-start(bf16[256,768]{1,0:T(8,128)(2,1)} %get-tuple-element.120) | copy-start | bytes 1179652
  73.3 12.8 %copy-start.14 = (bf16[256,768]{1,0:T(8,128)(2,1)S(1)}, bf16[256,768]{1,0:T(8,128)(2,1)}, u32[]{:S(2)}) copy-start(bf16[256,768]{1,0:T(8,128)(2,1)} %get-tuple-element.108) | copy-start | bytes 1179652
  73.3 12.8 %copy-start.15 = (bf16[256,768]{1,0:T(8,128)(2,1)S(1)}, bf16[256,768]{1,0:T(8,128)(2,1)}, u32[]{:S(2)}) copy-start(bf16[256,768]{1,0:T(8,128)(2,1)} %get-tuple-element.118) | copy-start | bytes 1179652
  73.3 2.3 %collective-permute-start.13 = (bf16[4,4,24,768]{3,2,1,0:T(8,128)(2,1)}, bf16[4,4,24,768]{3,2,1,0:T(8,128)(2,1)S(1)}, u32[]{:S(2)}, u32[]{:S(2)}) collective-permute-start(bf16[4,4,24,768]{3,2,1,0:T(8,128)(2,1)} %get-tuple-element.110), channel_id=1, source_target_pairs={{0,1},{1,0},{2,3},{3,2},{4,5},{5,4},{6,7},{7,6},{8,9},{9,8},{10,11... | collective-permute-start | bytes 1769480 | tf_op jit(solution)/shard_map/ppermute | solution.py:166
  73.4 7.8 %collective-permute-start.15 = (bf16[128,768]{1,0:T(8,128)(2,1)}, bf16[128,768]{1,0:T(8,128)(2,1)S(1)}, u32[]{:S(2)}, u32[]{:S(2)}) collective-permute-start(bf16[128,768]{1,0:T(8,128)(2,1)} %get-tuple-element.111), channel_id=1, source_target_pairs={{0,8},{8,0},{16,24},{24,16},{1,9},{9,1},{17,25},{25,17},{2,10},{10... | collective-permute-start | bytes 589832 | tf_op jit(solution)/shard_map/ppermute | solution.py:166
  74.0 7.3 %collective-permute-start.16 = (bf16[128,768]{1,0:T(8,128)(2,1)}, bf16[128,768]{1,0:T(8,128)(2,1)S(1)}, u32[]{:S(2)}, u32[]{:S(2)}) collective-permute-start(bf16[128,768]{1,0:T(8,128)(2,1)} %get-tuple-element.112), channel_id=1, source_target_pairs={{0,16},{8,24},{16,0},{24,8},{1,17},{9,25},{17,1},{25,9},{2,18},{10... | collective-permute-start | bytes 589832 | tf_op jit(solution)/shard_map/ppermute | solution.py:166
  76.8 8.3 %collective-permute-start.14 = (bf16[4,24,768]{2,1,0:T(8,128)(2,1)S(1)}, bf16[4,24,768]{2,1,0:T(8,128)(2,1)S(1)}, u32[]{:S(2)}, u32[]{:S(2)}) collective-permute-start(bf16[4,24,768]{2,1,0:T(8,128)(2,1)S(1)} %get-tuple-element.143), channel_id=1, source_target_pairs={{0,2},{2,0},{4,6},{6,4},{1,3},{3,1},{5,7},{7,5},{8,10},{10,8},{12,... | collective-permute-start | bytes 442376 | tf_op jit(solution)/shard_map/ppermute | solution.py:166
  78.0 14.0 %collective-permute-start.19 = (bf16[4,24,768]{2,1,0:T(8,128)(2,1)S(1)}, bf16[4,24,768]{2,1,0:T(8,128)(2,1)S(1)}, u32[]{:S(2)}, u32[]{:S(2)}) collective-permute-start(bf16[4,24,768]{2,1,0:T(8,128)(2,1)S(1)} %get-tuple-element.141), channel_id=1, source_target_pairs={{0,4},{2,6},{4,0},{6,2},{1,5},{3,7},{5,1},{7,3},{8,12},{10,14},{12... | collective-permute-start | bytes 442376 | tf_op jit(solution)/shard_map/ppermute | solution.py:166
  80.5 11.4 %collective-permute-start.20 = (bf16[4,24,768]{2,1,0:T(8,128)(2,1)S(1)}, bf16[4,24,768]{2,1,0:T(8,128)(2,1)S(1)}, u32[]{:S(2)}, u32[]{:S(2)}) collective-permute-start(bf16[4,24,768]{2,1,0:T(8,128)(2,1)S(1)} %get-tuple-element.142), channel_id=1, source_target_pairs={{0,6},{2,4},{4,2},{6,0},{1,7},{3,5},{5,3},{7,1},{8,14},{10,12},{12... | collective-permute-start | bytes 442376 | tf_op jit(solution)/shard_map/ppermute | solution.py:166
  86.1 11.0 %copy-start.4 = (f32[1,768]{1,0:T(1,128)S(1)}, f32[1,768]{1,0:T(1,128)}, u32[]{:S(2)}) copy-start(f32[1,768]{1,0:T(1,128)} %reshape.51.refs_0_.gain) | copy-start | bytes 9220
  86.1 11.0 %copy-start.7 = (bf16[256,1,768]{2,0,1:T(8,128)(2,1)S(1)}, bf16[256,1,768]{2,0,1:T(8,128)(2,1)}, u32[]{:S(2)}) copy-start(bf16[256,1,768]{2,0,1:T(8,128)(2,1)} %param.13) | copy-start | bytes 1179652
  86.1 11.0 %copy-start.8 = (bf16[256,768]{1,0:T(8,128)(2,1)S(1)}, bf16[256,768]{1,0:T(8,128)(2,1)}, u32[]{:S(2)}) copy-start(bf16[256,768]{1,0:T(8,128)(2,1)} %get-tuple-element.125.refs_0_) | copy-start | bytes 1179652
  86.2 10.8 %collective-permute-start.17 = (bf16[256,768]{1,0:T(8,128)(2,1)S(1)}, bf16[256,768]{1,0:T(8,128)(2,1)S(1)}, u32[]{:S(2)}, u32[]{:S(2)}) collective-permute-start(bf16[256,768]{1,0:T(8,128)(2,1)S(1)} %get-tuple-element.126), channel_id=1, source_target_pairs={{0,8},{8,0},{16,24},{24,16},{1,9},{9,1},{17,25},{25,17},{2,10},{10... | collective-permute-start | bytes 1179656 | tf_op jit(solution)/shard_map/ppermute | solution.py:166
  86.9 10.2 %collective-permute-start.18 = (bf16[256,768]{1,0:T(8,128)(2,1)S(1)}, bf16[256,768]{1,0:T(8,128)(2,1)S(1)}, u32[]{:S(2)}, u32[]{:S(2)}) collective-permute-start(bf16[256,768]{1,0:T(8,128)(2,1)S(1)} %get-tuple-element.127), channel_id=1, source_target_pairs={{0,16},{8,24},{16,0},{24,8},{1,17},{9,25},{17,1},{25,9},{2,18},{10... | collective-permute-start | bytes 1179656 | tf_op jit(solution)/shard_map/ppermute | solution.py:166
  93.0 5.5 %collective-permute-start.23 = (bf16[24,576]{1,0:T(8,128)(2,1)S(1)}, bf16[24,576]{1,0:T(8,128)(2,1)S(1)}, u32[]{:S(2)}, u32[]{:S(2)}) collective-permute-start(bf16[24,576]{1,0:T(8,128)(2,1)S(1)} %get-tuple-element.144), channel_id=1, source_target_pairs={{0,24},{8,16},{16,8},{24,0},{1,25},{9,17},{17,9},{25,1},{2,26},{10... | collective-permute-start | bytes 82952 | tf_op jit(solution)/shard_map/ppermute | solution.py:166
  94.6 3.9 %collective-permute-start.22 = (bf16[24,576]{1,0:T(8,128)(2,1)S(1)}, bf16[24,576]{1,0:T(8,128)(2,1)S(1)}, u32[]{:S(2)}, u32[]{:S(2)}) collective-permute-start(bf16[24,576]{1,0:T(8,128)(2,1)S(1)} %get-tuple-element.145), channel_id=1, source_target_pairs={{0,16},{8,24},{16,0},{24,8},{1,17},{9,25},{17,1},{25,9},{2,18},{10... | collective-permute-start | bytes 82952 | tf_op jit(solution)/shard_map/ppermute | solution.py:166
  95.5 3.9 %collective-permute-start.21 = (bf16[24,576]{1,0:T(8,128)(2,1)S(1)}, bf16[24,576]{1,0:T(8,128)(2,1)S(1)}, u32[]{:S(2)}, u32[]{:S(2)}) collective-permute-start(bf16[24,576]{1,0:T(8,128)(2,1)S(1)} %get-tuple-element.146), channel_id=1, source_target_pairs={{0,8},{8,0},{16,24},{24,16},{1,9},{9,1},{17,25},{25,17},{2,10},{10... | collective-permute-start | bytes 82952 | tf_op jit(solution)/shard_map/ppermute | solution.py:166
  (12 other events, 58.3 us)

commit v3 on v1

--- a/solution.py
+++ b/solution.py
@@ -185,6 +185,15 @@
         ((lane >= at) & (lane < at + HEAD_DIM)).astype(F32)[0:1].astype(BF16)
         for at in range(0, span, HEAD_DIM)
     ]
+
+
+def only_head(turned, h):
+    low, high = h * HEAD_DIM, (h + 1) * HEAD_DIM
+    parts = [jnp.zeros((low, turned.shape[1]), turned.dtype)] if low else []
+    parts.append(turned[low:high])
+    if high < turned.shape[0]:
+        parts.append(jnp.zeros((turned.shape[0] - high, turned.shape[1]), turned.dtype))
+    return jnp.concatenate(parts, axis=0)
 
 
 def fetch(pairs, sems):
@@ -239,10 +248,11 @@
     depth, zs, shard, block, span = dims
     heads = span // HEAD_DIM
     pos, w_near, w_far, normed_h = refs[:4]
-    query_h, keys_h, values_h, keys_t_h, att_t_h, lse_h, wq_h, wk_h, wv_h, w_out_h = refs[4:14]
-    outs_h, refs = refs[14 : 14 + depth], refs[14 + depth :]
-    normed, query, keys, values, keys_t, values_t, att_t, lse = refs[:8]
-    wq, wk, wv, w_out, outs, in_sems, out_sems = refs[8:]
+    (query_h, query_t_h, keys_h, values_h, keys_t_h, att_t_h, lse_h) = refs[4:11]
+    (wq_t_h, wk_t_h, wv_t_h, w_out_t_h), outs_h = refs[11:15], refs[15 : 15 + depth]
+    refs = refs[15 + depth :]
+    normed, query, query_t, keys, values, keys_t, values_t, att_t, lse = refs[:9]
+    wq, wk, wv, w_out, wq_t, wk_t, wv_t, w_out_t, outs, in_sems, out_sems = refs[9:]
     copies = fetch([(normed_h, normed)], in_sems)
     sender = Sender(out_sems)
 
@@ -258,26 +268,33 @@
                 w[rows, :] = both[:, i * span : (i + 1) * span]
             rows = slice(z * 2 * shard, (z + 1) * 2 * shard)
             w_out[rows, d * span : (d + 1) * span] = both[:, 3 * span :]
-    for src, dst in ((wq, wq_h), (wk, wk_h), (wv, wv_h), (w_out, w_out_h)):
-        sender.send(src, dst)
     copies[0].wait()
 
-    query[...] = (SCALE * dot(normed[...], wq[...])).astype(BF16)
-    key = dot(normed[...], wk[...])
-    keys[...] = key.astype(BF16)
-    keys_t[...] = jnp.transpose(key).astype(BF16)
-    value = dot(normed[...], wv[...])
-    values[...] = value.astype(BF16)
-    values_t[...] = jnp.transpose(value).astype(BF16)
-    for src, dst in ((query, query_h), (keys, keys_h), (values, values_h), (keys_t, keys_t_h)):
-        sender.send(src, dst)
-
-    masks = head_masks(span)
+    for scale, w, full, turned, full_h, turned_h in (
+        (SCALE, wq, query, query_t, query_h, query_t_h),
+        (1.0, wk, keys, keys_t, keys_h, keys_t_h),
+        (1.0, wv, values, values_t, values_h, None),
+    ):
+        rows = (scale * dot(normed[...], w[...])).astype(BF16)
+        full[...] = rows
+        turned[...] = jnp.transpose(rows)
+        sender.send(full, full_h)
+        if turned_h is not None:
+            sender.send(turned, turned_h)
+    for w, turned, turned_h in (
+        (wq, wq_t, wq_t_h),
+        (wk, wk_t, wk_t_h),
+        (wv, wv_t, wv_t_h),
+        (w_out, w_out_t, w_out_t_h),
+    ):
+        turned[...] = jnp.transpose(w[...])
+        sender.send(turned, turned_h)
+
 
     units = [(j, h) for j in range(depth) for h in range(heads)]
 
     def score(j, h):
-        return dot(keys[...], query[j * block : (j + 1) * block, :] * masks[h], (1, 1))
+        return dot(keys[...], only_head(query_t[:, j * block : (j + 1) * block], h))
 
     ready = [score(*unit) for unit in units[:2]]
     for i, (j, h) in enumerate(units):
@@ -304,37 +321,41 @@
     heads = span // HEAD_DIM
     pos, refs = refs[0], refs[1:]
     gs_h, refs = refs[:depth], refs[depth:]
-    (w_out_h, query_h, keys_h, values_h, keys_t_h, lse_h, normed_t_h, att_t_h) = refs[:8]
-    (wq_h, wk_h, wv_h, near, far), refs = refs[8:13], refs[13:]
+    (w_out_t_h, query_h, query_t_h, keys_h, values_h, keys_t_h, lse_h, normed_t_h) = refs[:8]
+    (att_t_h, wq_t_h, wk_t_h, wv_t_h, near, far), refs = refs[8:14], refs[14:]
     dns_h, refs = refs[: depth + 1], refs[depth + 1 :]
-    (gs, w_out, query, keys, values, keys_t, lse, normed_t, att_t, wq, wk, wv) = refs[:12]
-    (d_att, delta, d_query_t, d_keys, d_values, grad_out, dns, in_sems, out_sems) = refs[12:]
+    (gs, w_out_t, query, query_t, keys, values, keys_t, lse, normed_t, att_t) = refs[:10]
+    (wq_t, wk_t, wv_t, d_att, d_att_t, delta, d_query_t, d_keys, d_values) = refs[10:19]
+    grad_out, dns, in_sems, out_sems = refs[19:]
     copies = fetch(
-        [(w_out_h, w_out)]
+        [(w_out_t_h, w_out_t)]
         + [(gs_h[j], gs.at[pl.ds(j * block, block)]) for j in range(depth)]
         + [
             (att_t_h, att_t),
             (keys_h, keys),
             (query_h, query),
+            (query_t_h, query_t),
             (values_h, values),
             (lse_h, lse),
             (keys_t_h, keys_t),
             (normed_t_h, normed_t),
-            (wq_h, wq),
-            (wk_h, wk),
-            (wv_h, wv),
+            (wq_t_h, wq_t),
+            (wk_t_h, wk_t),
+            (wv_t_h, wv_t),
         ],
         in_sems,
     )
-    loaded, later = 7 + depth, copies[7 + depth :]
+    loaded, later = 8 + depth, copies[8 + depth :]
 
     d_keys[...] = jnp.zeros_like(d_keys)
     d_values[...] = jnp.zeros_like(d_values)
     for copy in copies[: 2 + depth]:
         copy.wait()
-    part = dot(gs[...], w_out[...], (1, 1)).astype(BF16)
+    part = dot(gs[...], w_out_t[...]).astype(BF16)
     d_att[...] = part
-    product = jnp.transpose(part.astype(F32)) * att_t[...]
+    part = jnp.transpose(part)
+    d_att_t[...] = part
+    product = part.astype(F32) * att_t[...]
     for h in range(heads):
         delta[h] = jnp.sum(product[h * HEAD_DIM : (h + 1) * HEAD_DIM], axis=0, keepdims=True)
     for copy in copies[2 + depth : loaded]:
@@ -348,7 +369,9 @@
         ds = [g_block * m for m in masks]
 
         def pair(h):
-            return dot(keys[...], qs[h], (1, 1)), dot(values[...], ds[h], (1, 1))
+            q_turned = only_head(query_t[:, cols], h)
+            d_turned = only_head(d_att_t[:, cols], h)
+            return dot(keys[...], q_turned), dot(values[...], d_turned)
 
         pairs = [pair(h) for h in range(min(2, heads))]
         for h in range(heads):
@@ -370,14 +393,14 @@
     lax.fori_loop(0, depth, step, 0)
     for copy in later:
         copy.wait()
-    d_query = jnp.transpose(d_query_t[...]).astype(BF16)
+    d_query = jnp.transpose(d_query_t[...].astype(BF16))
     d_key, d_value = d_keys[...].astype(BF16), d_values[...].astype(BF16)
     sender = Sender(out_sems)
     for i in range(0, depth, 2):
         rows = slice(i * block, (i + 2) * block)
-        d_normed = dot(d_query[rows], wq[...], (1, 1))
-        d_normed = d_normed + dot(d_key[rows], wk[...], (1, 1))
-        d_normed = d_normed + dot(d_value[rows], wv[...], (1, 1))
+        d_normed = dot(d_query[rows], wq_t[...])
+        d_normed = d_normed + dot(d_key[rows], wk_t[...])
+        d_normed = d_normed + dot(d_value[rows], wv_t[...])
         dns[rows, :] = d_normed.astype(BF16)
         for j in (i, i + 1):
             if j < depth - 1:
@@ -521,15 +544,17 @@
     w_far = swap(w_near, "core", 2, 1)
 
     turned_f32 = ((span, total), F32)
-    saved = [rows, rows, rows, turned, turned_f32, stats] + [in_weights] * 3 + [out_weights]
-    query, keys, values, keys_t, att_t, lse, wq, wk, wv, wo, *outs = call(
+    saved = [rows, turned, rows, rows, turned, turned_f32, stats]
+    saved = saved + [out_weights] * 3 + [in_weights]
+    query, query_t, keys, values, keys_t, att_t, lse, wq_t, wk_t, wv_t, wo_t, *outs = call(
         forward_kernel,
         dims,
         [(pos, SMEM), (w_near, VMEM), (w_far, VMEM), (normed, ANY)],
         [s + (ANY,) for s in saved + [block] * depth],
-        [norm, rows, rows, rows, turned, turned, turned_f32, stats]
+        [norm, rows, turned, rows, rows, turned, turned, turned_f32, stats]
         + [in_weights] * 3
-        + [out_weights, blocks],
+        + [out_weights] * 4
+        + [in_weights, blocks],
         [1, len(saved) + depth],
         8 * pass_flops,
     )
@@ -539,15 +564,15 @@
         backward_kernel,
         dims,
         [(pos, SMEM)]
-        + [(a, ANY) for a in gs + [wo, query, keys, values, keys_t, lse, normed_t]]
-        + [(a, ANY) for a in (att_t, wq, wk, wv)],
+        + [(a, ANY) for a in gs + [wo_t, query, query_t, keys, values, keys_t, lse, normed_t]]
+        + [(a, ANY) for a in (att_t, wq_t, wk_t, wv_t)],
         [(packed, BF16, VMEM)] * 2 + [s + (ANY,) for s in [block] * 3 + [halved] * 2],
-        [norm, out_weights, rows, rows, rows, turned, stats, ((width, total), BF16)]
-        + [turned_f32, in_weights, in_weights, in_weights]
-        + [rows, stats, turned_f32]
+        [norm, in_weights, rows, turned, rows, rows, turned, stats, ((width, total), BF16)]
+        + [turned_f32, out_weights, out_weights, out_weights]
+        + [rows, turned, stats, turned_f32]
         + [((total, span), F32)] * 2
         + [((span, width), F32), norm],
-        [depth + 11, depth + 1],
+        [depth + 12, depth + 1],
         24 * pass_flops,
     )
 
@@ -563,11 +588,12 @@
     dn2 = dn2.astype(F32) + jnp.concatenate([top, jnp.zeros_like(top)], axis=0).astype(F32)
     dn1 = dn1.astype(F32) + jnp.concatenate([jnp.zeros_like(bottom), bottom], axis=0).astype(F32)
     final_result = (x.astype(F32) + sum(o.astype(F32) for o in outs)).astype(BF16)
-    dn1, dn2, final_result = lax.optimization_barrier(
-        (dn1.astype(BF16), dn2.astype(BF16), final_result)
+    own = near[0].astype(F32) + far[0].astype(F32)
+    dn1, dn2, final_result, own = lax.optimization_barrier(
+        (dn1.astype(BF16), dn2.astype(BF16), final_result, own)
     )
     dn1, dn2 = swap(dn1, "depth", depth, 1), swap(dn2, "depth", depth, 2)
-    acc = near[0].astype(F32) + far[0].astype(F32) + sum(p.astype(F32) for p in low)
+    acc = own + sum(p.astype(F32) for p in low)
     parts = [
         swap(acc[k, :, : 3 * span].astype(BF16), "depth", depth, k) for k in range(1, depth)
     ]

time: 100 us -> 99.4 us (level)
  Pallas kernels: 36.2 us -> 35.2 us
    pallas_call x6, Pallas kernels: 36.2 us -> 35.2 us  [call(): pl.pallas_call(functools.partial(kernel, dims), out_shape=shapes, in_spec...]
  transfers between devices with their start and end apart: 24 -> 24, of which waited for: 9 -> 8; matrix products, arithmetic and copies ran while one was open for 7% -> 6% of each run, Pallas kernels for 35% -> 34%
where the time goes in v3:
time: 99.4 us; the launch traced here: 98.9 us
  Pallas kernels  35.2 us (35%)
  starting transfers between devices  30.2 us (30%)
  waiting for transfers between devices  14.9 us (15%)
  blocking collectives  9.04 us (9%)
  local copies, waits for them, and re-layouts  4.66 us (5%)
  other arithmetic  4.05 us (4%)
    pallas_call x6, Pallas kernels, call(): pl.pallas_call(functools.partial(kernel, dims), out_shape=shapes, in_spec...  35.2 us
    ppermute x24, starting transfers between devices, swap(): return lax.ppermute(value, axis, [(i, i ^ bits) for i in range(size)])  30.2 us
    ppermute x24, waiting for transfers between devices, swap(): return lax.ppermute(value, axis, [(i, i ^ bits) for i in range(size)])  14.9 us
    all_to_all x1, blocking collectives, head_body(): mine = lax.all_to_all(packed, 'depth', 0, 0, tiled=True)  9.04 us
    unnamed x40, local copies, waits for them, and re-layouts  2.63 us
  transfers between devices with their start and end apart: 24, of which 8 were waited for; matrix products, arithmetic and copies ran while one was open for 6% of the time, Pallas kernels for 34%

profile of v3, /device:TPU:0, one launch (start us, length us, event | category | flops | bytes accessed | tf_op | source)
XLA Modules:
  0.0 98.9 jit_solution(8288099716237429190)
XLA Ops:
  0.6 3.0 %collective-permute-start.1 = (bf16[256,768]{1,0:T(8,128)(2,1)}, bf16[256,768]{1,0:T(8,128)(2,1)S(1)}, u32[]{:S(2)}, u32[]{:S(2)}) collective-permute-start(bf16[256,768]{1,0:T(8,128)(2,1)} %bitcast.29), channel_id=1, source_target_pairs={{0,16},{8,24},{16,0},{24,8},{1,17},{9,25},{17,1},{25,9},{2,18},{10... | collective-permute-start | bytes 1179656 | tf_op jit(solution)/shard_map/ppermute | solution.py:166
  3.7 1.5 %collective-permute-start = (bf16[256,768]{1,0:T(8,128)(2,1)}, bf16[256,768]{1,0:T(8,128)(2,1)S(1)}, u32[]{:S(2)}, u32[]{:S(2)}) collective-permute-start(bf16[256,768]{1,0:T(8,128)(2,1)} %bitcast.30), channel_id=1, source_target_pairs={{0,8},{8,0},{16,24},{24,16},{1,9},{9,1},{17,25},{25,17},{2,10},{10... | collective-permute-start | bytes 1179656 | tf_op jit(solution)/shard_map/ppermute | solution.py:166
  5.2 1.6 %shard_map.126 = (bf16[4,24,576]{2,1,0:T(8,128)(2,1)}, bf16[4,24,192]{2,1,0:T(8,128)(2,1)}) custom-call(bf16[24,768]{1,0:T(8,128)(2,1)} %refs_2_.1, bf16[24,768]{1,0:T(8,128)(2,1)} %refs_3_.1, bf16[24,768]{1,0:T(8,128)(2,1)} %refs_4_.1, bf16[24,768]{1,0:T(8,128)(2,1)} %w_out.1), custom_call_target="tpu_custom_call" | custom-call | flops 1000 | bytes 294912 | tf_op jit(solution)/shard_map/pallas_call | solution.py:482
  6.7 9.0 %all_to_all.5 = bf16[4,24,576]{2,1,0:T(8,128)(2,1)S(1)} all-to-all(bf16[4,24,576]{2,1,0:T(8,128)(2,1)} %get-tuple-element.75), channel_id=1, replica_groups=mesh['depth'=4,'z'=4,'core'=2] {'depth'}, dimensions={0} | all-to-all | bytes 221184 | tf_op jit(solution)/shard_map/all_to_all | solution.py:517
  15.8 0.9 pad_maximum_fusion.1
  16.8 2.5 %collective-permute-start.2 = (bf16[256,768]{1,0:T(8,128)(2,1)}, bf16[256,768]{1,0:T(8,128)(2,1)S(1)}, u32[]{:S(2)}, u32[]{:S(2)}) collective-permute-start(bf16[256,768]{1,0:T(8,128)(2,1)} %bitcast.31), channel_id=1, source_target_pairs={{0,24},{8,16},{16,8},{24,0},{1,25},{9,17},{17,9},{25,1},{2,26},{10... | collective-permute-start | bytes 1179656 | tf_op jit(solution)/shard_map/ppermute | solution.py:166
  19.2 3.6 %collective-permute-start.5 = (bf16[4,24,768]{2,1,0:T(8,128)(2,1)S(1)}, bf16[4,24,768]{2,1,0:T(8,128)(2,1)S(1)}, u32[]{:S(2)}, u32[]{:S(2)}) collective-permute-start(bf16[4,24,768]{2,1,0:T(8,128)(2,1)S(1)} %pad_maximum_fusion.1), channel_id=1, source_target_pairs={{0,6},{2,4},{4,2},{6,0},{1,7},{3,5},{5,3},{7,1},{8,14},{10,12},{12... | collective-permute-start | bytes 442376 | tf_op jit(solution)/shard_map/ppermute | solution.py:166
  24.4 1.3 %reshape.51.refs_0_.gain = f32[1,768]{1,0:T(1,128)} reshape(f32[768]{0:T(1024)} %param.8) | data formatting | bytes 6144 | tf_op jit(solution)/shard_map/reshape | solution.py:503
  26.2 1.4 %collective-permute-done.2.refs_4_ = bf16[256,768]{1,0:T(8,128)(2,1)S(1)} collective-permute-done((bf16[256,768]{1,0:T(8,128)(2,1)}, bf16[256,768]{1,0:T(8,128)(2,1)S(1)}, u32[]{:S(2)}, u32[]{:S(2)}) %collective-permute-start.2) | collective-permute-done | bytes 393248 | tf_op jit(solution)/shard_map/ppermute | solution.py:166
  28.3 4.2 %shard_map.127 = (bf16[1024,768]{1,0:T(8,128)(2,1)}, bf16[768,1024]{1,0:T(8,128)(2,1)}) custom-call(f32[1,768]{1,0:T(1,128)} %reshape.51.refs_0_.gain, bf16[256,768]{1,0:T(8,128)(2,1)} %bitcast.32, bf16[256,768]{1,0:T(8,128)(2,1)} %copy-done.12, bf16[256,768]{1,0:T(8,128)(2,1)} %copy-done.11, bf16[256,768]{1,0:T(8,128)(2,1)} %copy-done.13), custom_call_target="tpu_custom_call" | custom-call | flops 1000 | bytes 4721664 | tf_op jit(solution)/shard_map/pallas_call | solution.py:482
  32.6 1.0 collective-permute-done.4
  33.7 1.2 %collective-permute-start.8 = (bf16[256,768]{1,0:T(8,128)(2,1)S(1)}, bf16[256,768]{1,0:T(8,128)(2,1)S(1)}, u32[]{:S(2)}, u32[]{:S(2)}) collective-permute-start(bf16[256,768]{1,0:T(8,128)(2,1)S(1)} %bitcast.35), channel_id=1, source_target_pairs={{0,24},{8,16},{16,8},{24,0},{1,25},{9,17},{17,9},{25,1},{2,26},{10... | collective-permute-start | bytes 1179656 | tf_op jit(solution)/shard_map/ppermute | solution.py:166
  35.4 1.8 %collective-permute-start.6 = (bf16[256,768]{1,0:T(8,128)(2,1)S(1)}, bf16[256,768]{1,0:T(8,128)(2,1)S(1)}, u32[]{:S(2)}, u32[]{:S(2)}) collective-permute-start(bf16[256,768]{1,0:T(8,128)(2,1)S(1)} %bitcast.37), channel_id=1, source_target_pairs={{0,8},{8,0},{16,24},{24,16},{1,9},{9,1},{17,25},{25,17},{2,10},{10... | collective-permute-start | bytes 1179656 | tf_op jit(solution)/shard_map/ppermute | solution.py:166
  37.3 0.9 copy-done.16
  38.1 10.1 %shard_map.128 = (bf16[1024,192]{1,0:T(8,128)(2,1)}, bf16[192,1024]{1,0:T(8,128)(2,1)}, bf16[1024,192]{1,0:T(8,128)(2,1)}, bf16[1024,192]{1,0:T(8,128)(2,1)}, bf...) custom-call(s32[3]{0:T(128)} %pad_add_fusion.refs_0_, ...), custom_call_target="tpu_custom_call" | custom-call | flops 3221225472 | bytes 8269836 | tf_op jit(solution)/shard_map/pallas_call | solution.py:482
  48.5 1.5 %collective-permute-start.11 = (bf16[256,768]{1,0:T(8,128)(2,1)}, bf16[256,768]{1,0:T(8,128)(2,1)S(1)}, u32[]{:S(2)}, u32[]{:S(2)}) collective-permute-start(bf16[256,768]{1,0:T(8,128)(2,1)} %get-tuple-element.109), channel_id=1, source_target_pairs={{0,16},{8,24},{16,0},{24,8},{1,17},{9,25},{17,1},{25,9},{2,18},{10... | collective-permute-start | bytes 1179656 | tf_op jit(solution)/shard_map/ppermute | solution.py:166
  50.0 1.8 %collective-permute-start.12 = (bf16[256,768]{1,0:T(8,128)(2,1)}, bf16[256,768]{1,0:T(8,128)(2,1)S(1)}, u32[]{:S(2)}, u32[]{:S(2)}) collective-permute-start(bf16[256,768]{1,0:T(8,128)(2,1)} %get-tuple-element.110), channel_id=1, source_target_pairs={{0,24},{8,16},{16,8},{24,0},{1,25},{9,17},{17,9},{25,1},{2,26},{10... | collective-permute-start | bytes 1179656 | tf_op jit(solution)/shard_map/ppermute | solution.py:166
  51.8 2.9 %collective-permute-done.7.refs_3_ = bf16[256,768]{1,0:T(8,128)(2,1)S(1)} collective-permute-done((bf16[256,768]{1,0:T(8,128)(2,1)S(1)}, bf16[256,768]{1,0:T(8,128)(2,1)S(1)}, u32[]{:S(2)}, u32[]{:S(2)}) %collective-permute-start.7) | collective-permute-done | bytes 393248 | tf_op jit(solution)/shard_map/ppermute | solution.py:166
  55.6 16.4 %shard_map.129 = (bf16[4,4,24,768]{3,2,1,0:T(8,128)(2,1)}, bf16[4,4,24,768]{3,2,1,0:T(8,128)(2,1)}, bf16[256,768]{1,0:T(8,128)(2,1)}, bf16[256,768]{1,0:T(8,128)...) custom-call(s32[3]{0:T(128)} %pad_add_fusion.refs_0_, ...), custom_call_target="tpu_custom_call" | custom-call | flops 9663676416 | bytes 9842700 | tf_op jit(solution)/shard_map/pallas_call | solution.py:482
  72.7 1.2 %collective-permute-start.16 = (bf16[128,768]{1,0:T(8,128)(2,1)}, bf16[128,768]{1,0:T(8,128)(2,1)S(1)}, u32[]{:S(2)}, u32[]{:S(2)}) collective-permute-start(bf16[128,768]{1,0:T(8,128)(2,1)} %get-tuple-element.115), channel_id=1, source_target_pairs={{0,16},{8,24},{16,0},{24,8},{1,17},{9,25},{17,1},{25,9},{2,18},{10... | collective-permute-start | bytes 589832 | tf_op jit(solution)/shard_map/ppermute | solution.py:166
  74.4 1.3 %fusion.1 = (bf16[4,24,768]{2,1,0:T(8,128)(2,1)S(1)}, bf16[4,24,768]{2,1,0:T(8,128)(2,1)S(1)}, f32[4,24,768]{2,1,0:T(8,128)S(1)}, bf16[4,24,768]{2,1,0:T(8,128)(2,1)S(1)}) fusion(bf16[4,4,24,768]{3,2,1,0:T(8,128)(2,1)S(1)} %collective-permute-done.13, bf16[4,4,24,768]{3,2,1,0:T(8,128)(2,1)} %get-tuple-element.112), kind=kLoop, calls=%fused_computation.10 | loop fusion | flops 1105920 | bytes 1916928 | tf_op jit(solution)/shard_map/convert_element_type | solution.py:586
  75.6 1.2 %collective-permute-start.14 = (bf16[4,24,768]{2,1,0:T(8,128)(2,1)S(1)}, bf16[4,24,768]{2,1,0:T(8,128)(2,1)S(1)}, u32[]{:S(2)}, u32[]{:S(2)}) collective-permute-start(bf16[4,24,768]{2,1,0:T(8,128)(2,1)S(1)} %get-tuple-element.148), channel_id=1, source_target_pairs={{0,2},{2,0},{4,6},{6,4},{1,3},{3,1},{5,7},{7,5},{8,10},{10,8},{12,... | collective-permute-start | bytes 442376 | tf_op jit(solution)/shard_map/ppermute | solution.py:166
  76.8 2.6 %collective-permute-start.19 = (bf16[4,24,768]{2,1,0:T(8,128)(2,1)S(1)}, bf16[4,24,768]{2,1,0:T(8,128)(2,1)S(1)}, u32[]{:S(2)}, u32[]{:S(2)}) collective-permute-start(bf16[4,24,768]{2,1,0:T(8,128)(2,1)S(1)} %get-tuple-element.145), channel_id=1, source_target_pairs={{0,4},{2,6},{4,0},{6,2},{1,5},{3,7},{5,1},{7,3},{8,12},{10,14},{12... | collective-permute-start | bytes 442376 | tf_op jit(solution)/shard_map/ppermute | solution.py:166
  80.1 3.8 %collective-permute-done.14 = bf16[4,24,768]{2,1,0:T(8,128)(2,1)S(1)} collective-permute-done((bf16[4,24,768]{2,1,0:T(8,128)(2,1)S(1)}, bf16[4,24,768]{2,1,0:T(8,128)(2,1)S(1)}, u32[]{:S(2)}, u32[]{:S(2)}) %collective-permute-start.14) | collective-permute-done | bytes 147488 | tf_op jit(solution)/shard_map/ppermute | solution.py:166
  84.0 1.0 %add_convert_fusion = bf16[256,768]{1,0:T(8,128)(2,1)} fusion(bf16[256,768]{1,0:T(8,128)(2,1)S(1)} %collective-permute-done.12, bf16[256,768]{1,0:T(8,128)(2,1)S(1)} %collective-permute-done.11, bf16[256,768]{1,0:T(8,128)(2,1)S(1)} %collective-permute-done.10, bf16[256,768]{1,0:T(8,128)(2,1)S(1)} %copy-done.10, bf16[256,1,768]{2,0,1:T(8,128)(2,1)S(1)} %copy-done), kind=kLoop, calls=%fused_computation | loop fusion | flops 1966080 | bytes 2359296 | tf_op jit(solution)/shard_map/convert_element_type | solution.py:590
  85.7 1.2 %collective-permute-start.18 = (bf16[256,768]{1,0:T(8,128)(2,1)S(1)}, bf16[256,768]{1,0:T(8,128)(2,1)S(1)}, u32[]{:S(2)}, u32[]{:S(2)}) collective-permute-start(bf16[256,768]{1,0:T(8,128)(2,1)S(1)} %get-tuple-element.130), channel_id=1, source_target_pairs={{0,16},{8,24},{16,0},{24,8},{1,17},{9,25},{17,1},{25,9},{2,18},{10... | collective-permute-start | bytes 1179656 | tf_op jit(solution)/shard_map/ppermute | solution.py:166
  86.9 3.9 %collective-permute-done.19 = bf16[4,24,768]{2,1,0:T(8,128)(2,1)S(1)} collective-permute-done((bf16[4,24,768]{2,1,0:T(8,128)(2,1)S(1)}, bf16[4,24,768]{2,1,0:T(8,128)(2,1)S(1)}, u32[]{:S(2)}, u32[]{:S(2)}) %collective-permute-start.19) | collective-permute-done | bytes 147488 | tf_op jit(solution)/shard_map/ppermute | solution.py:166
  91.0 1.6 %collective-permute-start.23 = (bf16[24,576]{1,0:T(8,128)(2,1)S(1)}, bf16[24,576]{1,0:T(8,128)(2,1)S(1)}, u32[]{:S(2)}, u32[]{:S(2)}) collective-permute-start(bf16[24,576]{1,0:T(8,128)(2,1)S(1)} %get-tuple-element.149), channel_id=1, source_target_pairs={{0,24},{8,16},{16,8},{24,0},{1,25},{9,17},{17,9},{25,1},{2,26},{10... | collective-permute-start | bytes 82952 | tf_op jit(solution)/shard_map/ppermute | solution.py:166
  93.4 1.1 %collective-permute-start.21 = (bf16[24,576]{1,0:T(8,128)(2,1)S(1)}, bf16[24,576]{1,0:T(8,128)(2,1)S(1)}, u32[]{:S(2)}, u32[]{:S(2)}) collective-permute-start(bf16[24,576]{1,0:T(8,128)(2,1)S(1)} %get-tuple-element.151), channel_id=1, source_target_pairs={{0,8},{8,0},{16,24},{24,16},{1,9},{9,1},{17,25},{25,17},{2,10},{10... | collective-permute-start | bytes 82952 | tf_op jit(solution)/shard_map/ppermute | solution.py:166
  94.5 1.4 %collective-permute-done.17.refs_1_ = bf16[256,768]{1,0:T(8,128)(2,1)S(1)} collective-permute-done((bf16[256,768]{1,0:T(8,128)(2,1)S(1)}, bf16[256,768]{1,0:T(8,128)(2,1)S(1)}, u32[]{:S(2)}, u32[]{:S(2)}) %collective-permute-start.17) | collective-permute-done | bytes 393248 | tf_op jit(solution)/shard_map/ppermute | solution.py:166
  96.0 1.4 %shard_map.130 = bf16[256,768]{1,0:T(8,128)(2,1)} custom-call(f32[1,768]{1,0:T(1,128)S(1)} %copy-done.4, bf16[256,768]{1,0:T(8,128)(2,1)S(1)} %bitcast.33, bf16[256,768]{1,0:T(8,128)(2,1)S(1)} %bitcast.38, bf16[256,768]{1,0:T(8,128)(2,1)S(1)} %copy-done.8, bf16[256,768]{1,0:T(8,128)(2,1)S(1)} %collective-permute-done.17.refs_1_, ...), custom_call_target="tpu_custom_call" | custom-call | flops 786432000 | bytes 2362368 | tf_op jit(solution)/shard_map/pallas_call | solution.py:482
  97.4 1.5 %shard_map.131 = (f32[24,768]{1,0:T(8,128)}, f32[24,768]{1,0:T(8,128)}, f32[24,768]{1,0:T(8,128)}, f32[24,768]{1,0:T(8,128)}, f32[1,24]{1,0:T(1,128)}) custom-call(s32[3]{0:T(128)S(1)} %copy-done.5, f32[1,24]{1,0:T(1,128)S(1)} %dynamic-slice_bitcast_fusion.refs_1_, bf16[24,768]{1,0:T(8,128)(2,1)S(1)} %copy-done.1, bf16[24,768]{1,0:T(8,128)(2,1)S(1)} %copy-done.2, ...), custom_call_target="tpu_custom_call" | custom-call | flops 1000 | bytes 783564 | tf_op jit(solution)/shard_map/pallas_call | solution.py:482
  (73 shorter events, 8.3 us)
Async XLA Ops:
  0.6 16.1 %collective-permute-start.1 = (bf16[256,768]{1,0:T(8,128)(2,1)}, bf16[256,768]{1,0:T(8,128)(2,1)S(1)}, u32[]{:S(2)}, u32[]{:S(2)}) collective-permute-start(bf16[256,768]{1,0:T(8,128)(2,1)} %bitcast.29), channel_id=1, source_target_pairs={{0,16},{8,24},{16,0},{24,8},{1,17},{9,25},{17,1},{25,9},{2,18},{10... | collective-permute-start | bytes 1179656 | tf_op jit(solution)/shard_map/ppermute | solution.py:166
  3.7 13.1 %collective-permute-start = (bf16[256,768]{1,0:T(8,128)(2,1)}, bf16[256,768]{1,0:T(8,128)(2,1)S(1)}, u32[]{:S(2)}, u32[]{:S(2)}) collective-permute-start(bf16[256,768]{1,0:T(8,128)(2,1)} %bitcast.30), channel_id=1, source_target_pairs={{0,8},{8,0},{16,24},{24,16},{1,9},{9,1},{17,25},{25,17},{2,10},{10... | collective-permute-start | bytes 1179656 | tf_op jit(solution)/shard_map/ppermute | solution.py:166
  15.8 17.9 %copy-start.6 = (bf16[256,1,768]{2,0,1:T(8,128)(2,1)S(1)}, bf16[256,1,768]{2,0,1:T(8,128)(2,1)}, u32[]{:S(2)}) copy-start(bf16[256,1,768]{2,0,1:T(8,128)(2,1)} %param.13) | copy-start | bytes 1179652
  16.7 10.9 %copy-start.11 = (bf16[256,768]{1,0:T(8,128)(2,1)}, bf16[256,768]{1,0:T(8,128)(2,1)S(1)}, u32[]{:S(2)}) copy-start(bf16[256,768]{1,0:T(8,128)(2,1)S(1)} %collective-permute-done.1.refs_3_) | copy-start | bytes 1179652
  16.7 10.9 %copy-start.12 = (bf16[256,768]{1,0:T(8,128)(2,1)}, bf16[256,768]{1,0:T(8,128)(2,1)S(1)}, u32[]{:S(2)}) copy-start(bf16[256,768]{1,0:T(8,128)(2,1)S(1)} %collective-permute-done.refs_2_) | copy-start | bytes 1179652
  16.8 10.8 %collective-permute-start.2 = (bf16[256,768]{1,0:T(8,128)(2,1)}, bf16[256,768]{1,0:T(8,128)(2,1)S(1)}, u32[]{:S(2)}, u32[]{:S(2)}) collective-permute-start(bf16[256,768]{1,0:T(8,128)(2,1)} %bitcast.31), channel_id=1, source_target_pairs={{0,24},{8,16},{16,8},{24,0},{1,25},{9,17},{17,9},{25,1},{2,26},{10... | collective-permute-start | bytes 1179656 | tf_op jit(solution)/shard_map/ppermute | solution.py:166
  19.2 13.3 %collective-permute-start.5 = (bf16[4,24,768]{2,1,0:T(8,128)(2,1)S(1)}, bf16[4,24,768]{2,1,0:T(8,128)(2,1)S(1)}, u32[]{:S(2)}, u32[]{:S(2)}) collective-permute-start(bf16[4,24,768]{2,1,0:T(8,128)(2,1)S(1)} %pad_maximum_fusion.1), channel_id=1, source_target_pairs={{0,6},{2,4},{4,2},{6,0},{1,7},{3,5},{5,3},{7,1},{8,14},{10,12},{12... | collective-permute-start | bytes 442376 | tf_op jit(solution)/shard_map/ppermute | solution.py:166
  22.8 10.7 %collective-permute-start.4 = (bf16[4,24,768]{2,1,0:T(8,128)(2,1)S(1)}, bf16[4,24,768]{2,1,0:T(8,128)(2,1)S(1)}, u32[]{:S(2)}, u32[]{:S(2)}) collective-permute-start(bf16[4,24,768]{2,1,0:T(8,128)(2,1)S(1)} %pad_maximum_fusion.1), channel_id=1, source_target_pairs={{0,4},{2,6},{4,0},{6,2},{1,5},{3,7},{5,1},{7,3},{8,12},{10,14},{12... | collective-permute-start | bytes 442376 | tf_op jit(solution)/shard_map/ppermute | solution.py:166
  22.8 10.7 %collective-permute-start.3 = (bf16[4,24,768]{2,1,0:T(8,128)(2,1)S(1)}, bf16[4,24,768]{2,1,0:T(8,128)(2,1)S(1)}, u32[]{:S(2)}, u32[]{:S(2)}) collective-permute-start(bf16[4,24,768]{2,1,0:T(8,128)(2,1)S(1)} %pad_maximum_fusion.1), channel_id=1, source_target_pairs={{0,2},{2,0},{4,6},{6,4},{1,3},{3,1},{5,7},{7,5},{8,10},{10,8},{12,... | collective-permute-start | bytes 442376 | tf_op jit(solution)/shard_map/ppermute | solution.py:166
  33.6 3.6 %collective-permute-start.9 = (bf16[4,4,24,768]{3,2,1,0:T(8,128)(2,1)S(1)}, bf16[4,4,24,768]{3,2,1,0:T(8,128)(2,1)S(1)}, u32[]{:S(2)}, u32[]{:S(2)}) collective-permute-start(bf16[4,4,24,768]{3,2,1,0:T(8,128)(2,1)S(1)} %pad_maximum_fusion.refs_1_), channel_id=1, source_target_pairs={{0,1},{1,0},{2,3},{3,2},{4,5},{5,4},{6,7},{7,6},{8,9},{9,8},{10,11... | collective-permute-start | bytes 1769480 | tf_op jit(solution)/shard_map/ppermute | solution.py:166
  33.7 16.3 %collective-permute-start.8 = (bf16[256,768]{1,0:T(8,128)(2,1)S(1)}, bf16[256,768]{1,0:T(8,128)(2,1)S(1)}, u32[]{:S(2)}, u32[]{:S(2)}) collective-permute-start(bf16[256,768]{1,0:T(8,128)(2,1)S(1)} %bitcast.35), channel_id=1, source_target_pairs={{0,24},{8,16},{16,8},{24,0},{1,25},{9,17},{17,9},{25,1},{2,26},{10... | collective-permute-start | bytes 1179656 | tf_op jit(solution)/shard_map/ppermute | solution.py:166
  34.9 19.7 %collective-permute-start.7 = (bf16[256,768]{1,0:T(8,128)(2,1)S(1)}, bf16[256,768]{1,0:T(8,128)(2,1)S(1)}, u32[]{:S(2)}, u32[]{:S(2)}) collective-permute-start(bf16[256,768]{1,0:T(8,128)(2,1)S(1)} %bitcast.36), channel_id=1, source_target_pairs={{0,16},{8,24},{16,0},{24,8},{1,17},{9,25},{17,1},{25,9},{2,18},{10... | collective-permute-start | bytes 1179656 | tf_op jit(solution)/shard_map/ppermute | solution.py:166
  35.4 19.2 %collective-permute-start.6 = (bf16[256,768]{1,0:T(8,128)(2,1)S(1)}, bf16[256,768]{1,0:T(8,128)(2,1)S(1)}, u32[]{:S(2)}, u32[]{:S(2)}) collective-permute-start(bf16[256,768]{1,0:T(8,128)(2,1)S(1)} %bitcast.37), channel_id=1, source_target_pairs={{0,8},{8,0},{16,24},{24,16},{1,9},{9,1},{17,25},{25,17},{2,10},{10... | collective-permute-start | bytes 1179656 | tf_op jit(solution)/shard_map/ppermute | solution.py:166
  48.2 23.8 %collective-permute-start.10 = (bf16[256,768]{1,0:T(8,128)(2,1)}, bf16[256,768]{1,0:T(8,128)(2,1)S(1)}, u32[]{:S(2)}, u32[]{:S(2)}) collective-permute-start(bf16[256,768]{1,0:T(8,128)(2,1)} %get-tuple-element.108), channel_id=1, source_target_pairs={{0,8},{8,0},{16,24},{24,16},{1,9},{9,1},{17,25},{25,17},{2,10},{10... | collective-permute-start | bytes 1179656 | tf_op jit(solution)/shard_map/ppermute | solution.py:166
  48.5 23.6 %collective-permute-start.11 = (bf16[256,768]{1,0:T(8,128)(2,1)}, bf16[256,768]{1,0:T(8,128)(2,1)S(1)}, u32[]{:S(2)}, u32[]{:S(2)}) collective-permute-start(bf16[256,768]{1,0:T(8,128)(2,1)} %get-tuple-element.109), channel_id=1, source_target_pairs={{0,16},{8,24},{16,0},{24,8},{1,17},{9,25},{17,1},{25,9},{2,18},{10... | collective-permute-start | bytes 1179656 | tf_op jit(solution)/shard_map/ppermute | solution.py:166
  50.0 22.1 %collective-permute-start.12 = (bf16[256,768]{1,0:T(8,128)(2,1)}, bf16[256,768]{1,0:T(8,128)(2,1)S(1)}, u32[]{:S(2)}, u32[]{:S(2)}) collective-permute-start(bf16[256,768]{1,0:T(8,128)(2,1)} %get-tuple-element.110), channel_id=1, source_target_pairs={{0,24},{8,16},{16,8},{24,0},{1,25},{9,17},{17,9},{25,1},{2,26},{10... | collective-permute-start | bytes 1179656 | tf_op jit(solution)/shard_map/ppermute | solution.py:166
  72.0 11.9 %copy-start = (bf16[256,1,768]{2,0,1:T(8,128)(2,1)S(1)}, bf16[256,1,768]{2,0,1:T(8,128)(2,1)}, u32[]{:S(2)}) copy-start(bf16[256,1,768]{2,0,1:T(8,128)(2,1)} %param.7) | copy-start | bytes 1179652
  72.0 11.9 %copy-start.10 = (bf16[256,768]{1,0:T(8,128)(2,1)S(1)}, bf16[256,768]{1,0:T(8,128)(2,1)}, u32[]{:S(2)}) copy-start(bf16[256,768]{1,0:T(8,128)(2,1)} %get-tuple-element.123) | copy-start | bytes 1179652
  72.1 2.3 %collective-permute-start.13 = (bf16[4,4,24,768]{3,2,1,0:T(8,128)(2,1)}, bf16[4,4,24,768]{3,2,1,0:T(8,128)(2,1)S(1)}, u32[]{:S(2)}, u32[]{:S(2)}) collective-permute-start(bf16[4,4,24,768]{3,2,1,0:T(8,128)(2,1)} %get-tuple-element.113), channel_id=1, source_target_pairs={{0,1},{1,0},{2,3},{3,2},{4,5},{5,4},{6,7},{7,6},{8,9},{9,8},{10,11... | collective-permute-start | bytes 1769480 | tf_op jit(solution)/shard_map/ppermute | solution.py:166
  72.2 7.9 %collective-permute-start.15 = (bf16[128,768]{1,0:T(8,128)(2,1)}, bf16[128,768]{1,0:T(8,128)(2,1)S(1)}, u32[]{:S(2)}, u32[]{:S(2)}) collective-permute-start(bf16[128,768]{1,0:T(8,128)(2,1)} %get-tuple-element.114), channel_id=1, source_target_pairs={{0,8},{8,0},{16,24},{24,16},{1,9},{9,1},{17,25},{25,17},{2,10},{10... | collective-permute-start | bytes 589832 | tf_op jit(solution)/shard_map/ppermute | solution.py:166
  72.7 7.4 %collective-permute-start.16 = (bf16[128,768]{1,0:T(8,128)(2,1)}, bf16[128,768]{1,0:T(8,128)(2,1)S(1)}, u32[]{:S(2)}, u32[]{:S(2)}) collective-permute-start(bf16[128,768]{1,0:T(8,128)(2,1)} %get-tuple-element.115), channel_id=1, source_target_pairs={{0,16},{8,24},{16,0},{24,8},{1,17},{9,25},{17,1},{25,9},{2,18},{10... | collective-permute-start | bytes 589832 | tf_op jit(solution)/shard_map/ppermute | solution.py:166
  75.6 8.3 %collective-permute-start.14 = (bf16[4,24,768]{2,1,0:T(8,128)(2,1)S(1)}, bf16[4,24,768]{2,1,0:T(8,128)(2,1)S(1)}, u32[]{:S(2)}, u32[]{:S(2)}) collective-permute-start(bf16[4,24,768]{2,1,0:T(8,128)(2,1)S(1)} %get-tuple-element.148), channel_id=1, source_target_pairs={{0,2},{2,0},{4,6},{6,4},{1,3},{3,1},{5,7},{7,5},{8,10},{10,8},{12,... | collective-permute-start | bytes 442376 | tf_op jit(solution)/shard_map/ppermute | solution.py:166
  76.8 14.0 %collective-permute-start.19 = (bf16[4,24,768]{2,1,0:T(8,128)(2,1)S(1)}, bf16[4,24,768]{2,1,0:T(8,128)(2,1)S(1)}, u32[]{:S(2)}, u32[]{:S(2)}) collective-permute-start(bf16[4,24,768]{2,1,0:T(8,128)(2,1)S(1)} %get-tuple-element.145), channel_id=1, source_target_pairs={{0,4},{2,6},{4,0},{6,2},{1,5},{3,7},{5,1},{7,3},{8,12},{10,14},{12... | collective-permute-start | bytes 442376 | tf_op jit(solution)/shard_map/ppermute | solution.py:166
  79.4 11.4 %collective-permute-start.20 = (bf16[4,24,768]{2,1,0:T(8,128)(2,1)S(1)}, bf16[4,24,768]{2,1,0:T(8,128)(2,1)S(1)}, u32[]{:S(2)}, u32[]{:S(2)}) collective-permute-start(bf16[4,24,768]{2,1,0:T(8,128)(2,1)S(1)} %get-tuple-element.146), channel_id=1, source_target_pairs={{0,6},{2,4},{4,2},{6,0},{1,7},{3,5},{5,3},{7,1},{8,14},{10,12},{12... | collective-permute-start | bytes 442376 | tf_op jit(solution)/shard_map/ppermute | solution.py:166
  85.0 11.0 %copy-start.4 = (f32[1,768]{1,0:T(1,128)S(1)}, f32[1,768]{1,0:T(1,128)}, u32[]{:S(2)}) copy-start(f32[1,768]{1,0:T(1,128)} %reshape.51.refs_0_.gain) | copy-start | bytes 9220
  85.0 11.0 %copy-start.7 = (bf16[256,1,768]{2,0,1:T(8,128)(2,1)S(1)}, bf16[256,1,768]{2,0,1:T(8,128)(2,1)}, u32[]{:S(2)}) copy-start(bf16[256,1,768]{2,0,1:T(8,128)(2,1)} %param.13) | copy-start | bytes 1179652
  85.0 11.0 %copy-start.8 = (bf16[256,768]{1,0:T(8,128)(2,1)S(1)}, bf16[256,768]{1,0:T(8,128)(2,1)}, u32[]{:S(2)}) copy-start(bf16[256,768]{1,0:T(8,128)(2,1)} %get-tuple-element.128.refs_0_) | copy-start | bytes 1179652
  85.1 10.8 %collective-permute-start.17 = (bf16[256,768]{1,0:T(8,128)(2,1)S(1)}, bf16[256,768]{1,0:T(8,128)(2,1)S(1)}, u32[]{:S(2)}, u32[]{:S(2)}) collective-permute-start(bf16[256,768]{1,0:T(8,128)(2,1)S(1)} %get-tuple-element.129), channel_id=1, source_target_pairs={{0,8},{8,0},{16,24},{24,16},{1,9},{9,1},{17,25},{25,17},{2,10},{10... | collective-permute-start | bytes 1179656 | tf_op jit(solution)/shard_map/ppermute | solution.py:166
  85.7 10.3 %collective-permute-start.18 = (bf16[256,768]{1,0:T(8,128)(2,1)S(1)}, bf16[256,768]{1,0:T(8,128)(2,1)S(1)}, u32[]{:S(2)}, u32[]{:S(2)}) collective-permute-start(bf16[256,768]{1,0:T(8,128)(2,1)S(1)} %get-tuple-element.130), channel_id=1, source_target_pairs={{0,16},{8,24},{16,0},{24,8},{1,17},{9,25},{17,1},{25,9},{2,18},{10... | collective-permute-start | bytes 1179656 | tf_op jit(solution)/shard_map/ppermute | solution.py:166
  91.0 6.4 %collective-permute-start.23 = (bf16[24,576]{1,0:T(8,128)(2,1)S(1)}, bf16[24,576]{1,0:T(8,128)(2,1)S(1)}, u32[]{:S(2)}, u32[]{:S(2)}) collective-permute-start(bf16[24,576]{1,0:T(8,128)(2,1)S(1)} %get-tuple-element.149), channel_id=1, source_target_pairs={{0,24},{8,16},{16,8},{24,0},{1,25},{9,17},{17,9},{25,1},{2,26},{10... | collective-permute-start | bytes 82952 | tf_op jit(solution)/shard_map/ppermute | solution.py:166
  92.6 4.8 %collective-permute-start.22 = (bf16[24,576]{1,0:T(8,128)(2,1)S(1)}, bf16[24,576]{1,0:T(8,128)(2,1)S(1)}, u32[]{:S(2)}, u32[]{:S(2)}) collective-permute-start(bf16[24,576]{1,0:T(8,128)(2,1)S(1)} %get-tuple-element.150), channel_id=1, source_target_pairs={{0,16},{8,24},{16,0},{24,8},{1,17},{9,25},{17,1},{25,9},{2,18},{10... | collective-permute-start | bytes 82952 | tf_op jit(solution)/shard_map/ppermute | solution.py:166
  93.4 4.0 %collective-permute-start.21 = (bf16[24,576]{1,0:T(8,128)(2,1)S(1)}, bf16[24,576]{1,0:T(8,128)(2,1)S(1)}, u32[]{:S(2)}, u32[]{:S(2)}) collective-permute-start(bf16[24,576]{1,0:T(8,128)(2,1)S(1)} %get-tuple-element.151), channel_id=1, source_target_pairs={{0,8},{8,0},{16,24},{24,16},{1,9},{9,1},{17,25},{25,17},{2,10},{10... | collective-permute-start | bytes 82952 | tf_op jit(solution)/shard_map/ppermute | solution.py:166
  (12 other events, 56.3 us)

commit v4 on v3

--- a/solution.py
+++ b/solution.py
@@ -249,10 +249,10 @@
     heads = span // HEAD_DIM
     pos, w_near, w_far, normed_h = refs[:4]
     (query_h, query_t_h, keys_h, values_h, keys_t_h, att_t_h, lse_h) = refs[4:11]
-    (wq_t_h, wk_t_h, wv_t_h, w_out_t_h), outs_h = refs[11:15], refs[15 : 15 + depth]
-    refs = refs[15 + depth :]
+    (weights_t_h, w_out_t_h), outs_h = refs[11:13], refs[13 : 13 + depth]
+    refs = refs[13 + depth :]
     normed, query, query_t, keys, values, keys_t, values_t, att_t, lse = refs[:9]
-    wq, wk, wv, w_out, wq_t, wk_t, wv_t, w_out_t, outs, in_sems, out_sems = refs[9:]
+    wq, wk, wv, w_out, weights_t, w_out_t, outs, in_sems, out_sems = refs[9:]
     copies = fetch([(normed_h, normed)], in_sems)
     sender = Sender(out_sems)
 
@@ -281,14 +281,11 @@
         sender.send(full, full_h)
         if turned_h is not None:
             sender.send(turned, turned_h)
-    for w, turned, turned_h in (
-        (wq, wq_t, wq_t_h),
-        (wk, wk_t, wk_t_h),
-        (wv, wv_t, wv_t_h),
-        (w_out, w_out_t, w_out_t_h),
-    ):
-        turned[...] = jnp.transpose(w[...])
-        sender.send(turned, turned_h)
+    for i, w in enumerate((wq, wk, wv)):
+        weights_t[i * span : (i + 1) * span, :] = jnp.transpose(w[...])
+    sender.send(weights_t, weights_t_h)
+    w_out_t[...] = jnp.transpose(w_out[...])
+    sender.send(w_out_t, w_out_t_h)
 
 
     units = [(j, h) for j in range(depth) for h in range(heads)]
@@ -322,35 +319,32 @@
     pos, refs = refs[0], refs[1:]
     gs_h, refs = refs[:depth], refs[depth:]
     (w_out_t_h, query_h, query_t_h, keys_h, values_h, keys_t_h, lse_h, normed_t_h) = refs[:8]
-    (att_t_h, wq_t_h, wk_t_h, wv_t_h, near, far), refs = refs[8:14], refs[14:]
+    (att_t_h, weights_t_h, near, far), refs = refs[8:12], refs[12:]
     dns_h, refs = refs[: depth + 1], refs[depth + 1 :]
     (gs, w_out_t, query, query_t, keys, values, keys_t, lse, normed_t, att_t) = refs[:10]
-    (wq_t, wk_t, wv_t, d_att, d_att_t, delta, d_query_t, d_keys, d_values) = refs[10:19]
-    grad_out, dns, in_sems, out_sems = refs[19:]
-    copies = fetch(
+    (weights_t, d_att, d_att_t, delta, d_query_t, d_keys, d_values, d_qkv) = refs[10:18]
+    grad_out, dns, in_sems, out_sems = refs[18:]
+    first = fetch(
         [(w_out_t_h, w_out_t)]
         + [(gs_h[j], gs.at[pl.ds(j * block, block)]) for j in range(depth)]
-        + [
-            (att_t_h, att_t),
-            (keys_h, keys),
-            (query_h, query),
-            (query_t_h, query_t),
-            (values_h, values),
-            (lse_h, lse),
-            (keys_t_h, keys_t),
-            (normed_t_h, normed_t),
-            (wq_t_h, wq_t),
-            (wk_t_h, wk_t),
-            (wv_t_h, wv_t),
-        ],
-        in_sems,
-    )
-    loaded, later = 8 + depth, copies[8 + depth :]
+        + [(att_t_h, att_t)],
+        in_sems.at[pl.ds(0, 2 + depth)],
+    )
+    second = [
+        (keys_h, keys),
+        (query_t_h, query_t),
+        (values_h, values),
+        (lse_h, lse),
+        (query_h, query),
+        (keys_t_h, keys_t),
+    ]
+    third = [(normed_t_h, normed_t), (weights_t_h, weights_t)]
 
     d_keys[...] = jnp.zeros_like(d_keys)
     d_values[...] = jnp.zeros_like(d_values)
-    for copy in copies[: 2 + depth]:
+    for copy in first:
         copy.wait()
+    second = fetch(second, in_sems.at[pl.ds(2 + depth, 6)])
     part = dot(gs[...], w_out_t[...]).astype(BF16)
     d_att[...] = part
     part = jnp.transpose(part)
@@ -358,8 +352,9 @@
     product = part.astype(F32) * att_t[...]
     for h in range(heads):
         delta[h] = jnp.sum(product[h * HEAD_DIM : (h + 1) * HEAD_DIM], axis=0, keepdims=True)
-    for copy in copies[2 + depth : loaded]:
+    for copy in second:
         copy.wait()
+    third = fetch(third, in_sems.at[pl.ds(8 + depth, 2)])
     masks = head_masks(span)
 
     def step(j, _):
@@ -391,17 +386,15 @@
         return 0
 
     lax.fori_loop(0, depth, step, 0)
-    for copy in later:
+    d_qkv[:, :span] = jnp.transpose(d_query_t[...].astype(BF16))
+    d_qkv[:, span : 2 * span] = d_keys[...].astype(BF16)
+    d_qkv[:, 2 * span :] = d_values[...].astype(BF16)
+    for copy in third:
         copy.wait()
-    d_query = jnp.transpose(d_query_t[...].astype(BF16))
-    d_key, d_value = d_keys[...].astype(BF16), d_values[...].astype(BF16)
     sender = Sender(out_sems)
     for i in range(0, depth, 2):
         rows = slice(i * block, (i + 2) * block)
-        d_normed = dot(d_query[rows], wq_t[...])
-        d_normed = d_normed + dot(d_key[rows], wk_t[...])
-        d_normed = d_normed + dot(d_value[rows], wv_t[...])
-        dns[rows, :] = d_normed.astype(BF16)
+        dns[rows, :] = dot(d_qkv[rows, :], weights_t[...]).astype(BF16)
         for j in (i, i + 1):
             if j < depth - 1:
                 sender.send(dns.at[pl.ds(j * block, block)], dns_h[j])
@@ -411,7 +404,7 @@
                 sender.send(dns.at[pl.ds(j * block + half, half)], dns_h[j + 1])
 
     grad_out[...] = dot(att_t[...].astype(BF16), gs[...])
-    grads = [dot(normed_t[...], d) for d in (d_query, d_key, d_value)]
+    grads = dot(normed_t[...], d_qkv[...])
     own_z, first, own_d = pos[0], pos[1] == 0, pos[2]
     for d in range(depth):
         for z in range(zs):
@@ -419,8 +412,10 @@
             for c in range(2):
                 row, row_out = ((d * zs + z) * 2 + c) * shard, (z * 2 + c) * shard
                 sides.append(
-                    [g[row : row + shard] for g in grads]
-                    + [grad_out[row_out : row_out + shard, d * span : (d + 1) * span]]
+                    (
+                        grads[row : row + shard],
+                        grad_out[row_out : row_out + shard, d * span : (d + 1) * span],
+                    )
                 )
             at = 0
             for one, two in zip(*sides):
@@ -545,16 +540,16 @@
 
     turned_f32 = ((span, total), F32)
     saved = [rows, turned, rows, rows, turned, turned_f32, stats]
-    saved = saved + [out_weights] * 3 + [in_weights]
-    query, query_t, keys, values, keys_t, att_t, lse, wq_t, wk_t, wv_t, wo_t, *outs = call(
+    weights_shape = ((3 * span, width), BF16)
+    saved = saved + [weights_shape, in_weights]
+    query, query_t, keys, values, keys_t, att_t, lse, weights_t, wo_t, *outs = call(
         forward_kernel,
         dims,
         [(pos, SMEM), (w_near, VMEM), (w_far, VMEM), (normed, ANY)],
         [s + (ANY,) for s in saved + [block] * depth],
         [norm, rows, turned, rows, rows, turned, turned, turned_f32, stats]
         + [in_weights] * 3
-        + [out_weights] * 4
-        + [in_weights, blocks],
+        + [out_weights, weights_shape, in_weights, blocks],
         [1, len(saved) + depth],
         8 * pass_flops,
     )
@@ -565,14 +560,13 @@
         dims,
         [(pos, SMEM)]
         + [(a, ANY) for a in gs + [wo_t, query, query_t, keys, values, keys_t, lse, normed_t]]
-        + [(a, ANY) for a in (att_t, wq_t, wk_t, wv_t)],
+        + [(a, ANY) for a in (att_t, weights_t)],
         [(packed, BF16, VMEM)] * 2 + [s + (ANY,) for s in [block] * 3 + [halved] * 2],
         [norm, in_weights, rows, turned, rows, rows, turned, stats, ((width, total), BF16)]
-        + [turned_f32, out_weights, out_weights, out_weights]
-        + [rows, turned, stats, turned_f32]
+        + [turned_f32, weights_shape, rows, turned, stats, turned_f32]
         + [((total, span), F32)] * 2
-        + [((span, width), F32), norm],
-        [depth + 12, depth + 1],
+        + [((total, 3 * span), BF16), ((span, width), F32), norm],
+        [depth + 10, depth + 1],
         24 * pass_flops,
     )
 

time: 99.4 us -> 101 us (1.016)
  Pallas kernels: 35.2 us -> 36.5 us
    pallas_call x6, Pallas kernels: 35.2 us -> 36.5 us  [call(): pl.pallas_call(functools.partial(kernel, dims), out_shape=shapes, in_spec...]
  transfers between devices with their start and end apart: 24 -> 24, of which waited for: 8 -> 8; matrix products, arithmetic and copies ran while one was open for 6% -> 6% of each run, Pallas kernels for 34% -> 35%
where the time goes in v4:
time: 101 us; the launch traced here: 100 us
  Pallas kernels  36.5 us (36%)
  starting transfers between devices  30.1 us (30%)
  waiting for transfers between devices  14.9 us (15%)
  blocking collectives  9.04 us (9%)
  local copies, waits for them, and re-layouts  4.6 us (5%)
  other arithmetic  4.05 us (4%)
    pallas_call x6, Pallas kernels, call(): pl.pallas_call(functools.partial(kernel, dims), out_shape=shapes, in_spec...  36.5 us
    ppermute x24, starting transfers between devices, swap(): return lax.ppermute(value, axis, [(i, i ^ bits) for i in range(size)])  30.1 us
    ppermute x24, waiting for transfers between devices, swap(): return lax.ppermute(value, axis, [(i, i ^ bits) for i in range(size)])  14.9 us
    all_to_all x1, blocking collectives, head_body(): mine = lax.all_to_all(packed, 'depth', 0, 0, tiled=True)  9.04 us
    unnamed x40, local copies, waits for them, and re-layouts  2.56 us
  transfers between devices with their start and end apart: 24, of which 8 were waited for; matrix products, arithmetic and copies ran while one was open for 6% of the time, Pallas kernels for 35%

profile of v4, /device:TPU:0, one launch (start us, length us, event | category | flops | bytes accessed | tf_op | source)
XLA Modules:
  0.0 100.1 jit_solution(4438091533537585784)
XLA Ops:
  0.6 3.0 %collective-permute-start.1 = (bf16[256,768]{1,0:T(8,128)(2,1)}, bf16[256,768]{1,0:T(8,128)(2,1)S(1)}, u32[]{:S(2)}, u32[]{:S(2)}) collective-permute-start(bf16[256,768]{1,0:T(8,128)(2,1)} %bitcast.29), channel_id=1, source_target_pairs={{0,16},{8,24},{16,0},{24,8},{1,17},{9,25},{17,1},{25,9},{2,18},{10... | collective-permute-start | bytes 1179656 | tf_op jit(solution)/shard_map/ppermute | solution.py:166
  3.7 1.5 %collective-permute-start = (bf16[256,768]{1,0:T(8,128)(2,1)}, bf16[256,768]{1,0:T(8,128)(2,1)S(1)}, u32[]{:S(2)}, u32[]{:S(2)}) collective-permute-start(bf16[256,768]{1,0:T(8,128)(2,1)} %bitcast.30), channel_id=1, source_target_pairs={{0,8},{8,0},{16,24},{24,16},{1,9},{9,1},{17,25},{25,17},{2,10},{10... | collective-permute-start | bytes 1179656 | tf_op jit(solution)/shard_map/ppermute | solution.py:166
  5.2 1.6 %shard_map.126 = (bf16[4,24,576]{2,1,0:T(8,128)(2,1)}, bf16[4,24,192]{2,1,0:T(8,128)(2,1)}) custom-call(bf16[24,768]{1,0:T(8,128)(2,1)} %refs_2_.1, bf16[24,768]{1,0:T(8,128)(2,1)} %refs_3_.1, bf16[24,768]{1,0:T(8,128)(2,1)} %refs_4_.1, bf16[24,768]{1,0:T(8,128)(2,1)} %w_out.1), custom_call_target="tpu_custom_call" | custom-call | flops 1000 | bytes 294912 | tf_op jit(solution)/shard_map/pallas_call | solution.py:477
  6.7 9.0 %all_to_all.5 = bf16[4,24,576]{2,1,0:T(8,128)(2,1)S(1)} all-to-all(bf16[4,24,576]{2,1,0:T(8,128)(2,1)} %get-tuple-element.73), channel_id=1, replica_groups=mesh['depth'=4,'z'=4,'core'=2] {'depth'}, dimensions={0} | all-to-all | bytes 221184 | tf_op jit(solution)/shard_map/all_to_all | solution.py:512
  15.8 0.9 pad_maximum_fusion.1
  16.8 2.5 %collective-permute-start.2 = (bf16[256,768]{1,0:T(8,128)(2,1)}, bf16[256,768]{1,0:T(8,128)(2,1)S(1)}, u32[]{:S(2)}, u32[]{:S(2)}) collective-permute-start(bf16[256,768]{1,0:T(8,128)(2,1)} %bitcast.31), channel_id=1, source_target_pairs={{0,24},{8,16},{16,8},{24,0},{1,25},{9,17},{17,9},{25,1},{2,26},{10... | collective-permute-start | bytes 1179656 | tf_op jit(solution)/shard_map/ppermute | solution.py:166
  19.2 3.6 %collective-permute-start.5 = (bf16[4,24,768]{2,1,0:T(8,128)(2,1)S(1)}, bf16[4,24,768]{2,1,0:T(8,128)(2,1)S(1)}, u32[]{:S(2)}, u32[]{:S(2)}) collective-permute-start(bf16[4,24,768]{2,1,0:T(8,128)(2,1)S(1)} %pad_maximum_fusion.1), channel_id=1, source_target_pairs={{0,6},{2,4},{4,2},{6,0},{1,7},{3,5},{5,3},{7,1},{8,14},{10,12},{12... | collective-permute-start | bytes 442376 | tf_op jit(solution)/shard_map/ppermute | solution.py:166
  24.4 1.3 %reshape.51.refs_0_.gain = f32[1,768]{1,0:T(1,128)} reshape(f32[768]{0:T(1024)} %param.8) | data formatting | bytes 6144 | tf_op jit(solution)/shard_map/reshape | solution.py:498
  26.2 1.4 %collective-permute-done.2.refs_4_ = bf16[256,768]{1,0:T(8,128)(2,1)S(1)} collective-permute-done((bf16[256,768]{1,0:T(8,128)(2,1)}, bf16[256,768]{1,0:T(8,128)(2,1)S(1)}, u32[]{:S(2)}, u32[]{:S(2)}) %collective-permute-start.2) | collective-permute-done | bytes 393248 | tf_op jit(solution)/shard_map/ppermute | solution.py:166
  28.3 4.2 %shard_map.127 = (bf16[1024,768]{1,0:T(8,128)(2,1)}, bf16[768,1024]{1,0:T(8,128)(2,1)}) custom-call(f32[1,768]{1,0:T(1,128)} %reshape.51.refs_0_.gain, bf16[256,768]{1,0:T(8,128)(2,1)} %bitcast.32, bf16[256,768]{1,0:T(8,128)(2,1)} %copy-done.12, bf16[256,768]{1,0:T(8,128)(2,1)} %copy-done.11, bf16[256,768]{1,0:T(8,128)(2,1)} %copy-done.13), custom_call_target="tpu_custom_call" | custom-call | flops 1000 | bytes 4721664 | tf_op jit(solution)/shard_map/pallas_call | solution.py:477
  32.6 1.0 collective-permute-done.4
  33.7 1.2 %collective-permute-start.8 = (bf16[256,768]{1,0:T(8,128)(2,1)S(1)}, bf16[256,768]{1,0:T(8,128)(2,1)S(1)}, u32[]{:S(2)}, u32[]{:S(2)}) collective-permute-start(bf16[256,768]{1,0:T(8,128)(2,1)S(1)} %bitcast.35), channel_id=1, source_target_pairs={{0,24},{8,16},{16,8},{24,0},{1,25},{9,17},{17,9},{25,1},{2,26},{10... | collective-permute-start | bytes 1179656 | tf_op jit(solution)/shard_map/ppermute | solution.py:166
  35.4 1.8 %collective-permute-start.6 = (bf16[256,768]{1,0:T(8,128)(2,1)S(1)}, bf16[256,768]{1,0:T(8,128)(2,1)S(1)}, u32[]{:S(2)}, u32[]{:S(2)}) collective-permute-start(bf16[256,768]{1,0:T(8,128)(2,1)S(1)} %bitcast.37), channel_id=1, source_target_pairs={{0,8},{8,0},{16,24},{24,16},{1,9},{9,1},{17,25},{25,17},{2,10},{10... | collective-permute-start | bytes 1179656 | tf_op jit(solution)/shard_map/ppermute | solution.py:166
  38.1 10.2 %shard_map.128 = (bf16[1024,192]{1,0:T(8,128)(2,1)}, bf16[192,1024]{1,0:T(8,128)(2,1)}, bf16[1024,192]{1,0:T(8,128)(2,1)}, bf16[1024,192]{1,0:T(8,128)(2,1)}, bf...) custom-call(s32[3]{0:T(128)} %pad_add_fusion.refs_0_, ...), custom_call_target="tpu_custom_call" | custom-call | flops 3221225472 | bytes 8269836 | tf_op jit(solution)/shard_map/pallas_call | solution.py:477
  48.6 1.5 %collective-permute-start.11 = (bf16[256,768]{1,0:T(8,128)(2,1)}, bf16[256,768]{1,0:T(8,128)(2,1)S(1)}, u32[]{:S(2)}, u32[]{:S(2)}) collective-permute-start(bf16[256,768]{1,0:T(8,128)(2,1)} %get-tuple-element.105), channel_id=1, source_target_pairs={{0,16},{8,24},{16,0},{24,8},{1,17},{9,25},{17,1},{25,9},{2,18},{10... | collective-permute-start | bytes 1179656 | tf_op jit(solution)/shard_map/ppermute | solution.py:166
  50.1 1.8 %collective-permute-start.12 = (bf16[256,768]{1,0:T(8,128)(2,1)}, bf16[256,768]{1,0:T(8,128)(2,1)S(1)}, u32[]{:S(2)}, u32[]{:S(2)}) collective-permute-start(bf16[256,768]{1,0:T(8,128)(2,1)} %get-tuple-element.106), channel_id=1, source_target_pairs={{0,24},{8,16},{16,8},{24,0},{1,25},{9,17},{17,9},{25,1},{2,26},{10... | collective-permute-start | bytes 1179656 | tf_op jit(solution)/shard_map/ppermute | solution.py:166
  51.9 2.8 %collective-permute-done.7.refs_3_ = bf16[256,768]{1,0:T(8,128)(2,1)S(1)} collective-permute-done((bf16[256,768]{1,0:T(8,128)(2,1)S(1)}, bf16[256,768]{1,0:T(8,128)(2,1)S(1)}, u32[]{:S(2)}, u32[]{:S(2)}) %collective-permute-start.7) | collective-permute-done | bytes 393248 | tf_op jit(solution)/shard_map/ppermute | solution.py:166
  55.6 17.6 %shard_map.129 = (bf16[4,4,24,768]{3,2,1,0:T(8,128)(2,1)}, bf16[4,4,24,768]{3,2,1,0:T(8,128)(2,1)}, bf16[256,768]{1,0:T(8,128)(2,1)}, bf16[256,768]{1,0:T(8,128)...) custom-call(s32[3]{0:T(128)} %pad_add_fusion.refs_0_, ...), custom_call_target="tpu_custom_call" | custom-call | flops 9663676416 | bytes 9842700 | tf_op jit(solution)/shard_map/pallas_call | solution.py:477
  73.9 1.2 %collective-permute-start.16 = (bf16[128,768]{1,0:T(8,128)(2,1)}, bf16[128,768]{1,0:T(8,128)(2,1)S(1)}, u32[]{:S(2)}, u32[]{:S(2)}) collective-permute-start(bf16[128,768]{1,0:T(8,128)(2,1)} %get-tuple-element.111), channel_id=1, source_target_pairs={{0,16},{8,24},{16,0},{24,8},{1,17},{9,25},{17,1},{25,9},{2,18},{10... | collective-permute-start | bytes 589832 | tf_op jit(solution)/shard_map/ppermute | solution.py:166
  75.6 1.3 %fusion.1 = (bf16[4,24,768]{2,1,0:T(8,128)(2,1)S(1)}, bf16[4,24,768]{2,1,0:T(8,128)(2,1)S(1)}, f32[4,24,768]{2,1,0:T(8,128)S(1)}, bf16[4,24,768]{2,1,0:T(8,128)(2,1)S(1)}) fusion(bf16[4,4,24,768]{3,2,1,0:T(8,128)(2,1)S(1)} %collective-permute-done.13, bf16[4,4,24,768]{3,2,1,0:T(8,128)(2,1)} %get-tuple-element.108), kind=kLoop, calls=%fused_computation.10 | loop fusion | flops 1105920 | bytes 1916928 | tf_op jit(solution)/shard_map/convert_element_type | solution.py:580
  76.8 1.2 %collective-permute-start.14 = (bf16[4,24,768]{2,1,0:T(8,128)(2,1)S(1)}, bf16[4,24,768]{2,1,0:T(8,128)(2,1)S(1)}, u32[]{:S(2)}, u32[]{:S(2)}) collective-permute-start(bf16[4,24,768]{2,1,0:T(8,128)(2,1)S(1)} %get-tuple-element.144), channel_id=1, source_target_pairs={{0,2},{2,0},{4,6},{6,4},{1,3},{3,1},{5,7},{7,5},{8,10},{10,8},{12,... | collective-permute-start | bytes 442376 | tf_op jit(solution)/shard_map/ppermute | solution.py:166
  78.0 2.6 %collective-permute-start.19 = (bf16[4,24,768]{2,1,0:T(8,128)(2,1)S(1)}, bf16[4,24,768]{2,1,0:T(8,128)(2,1)S(1)}, u32[]{:S(2)}, u32[]{:S(2)}) collective-permute-start(bf16[4,24,768]{2,1,0:T(8,128)(2,1)S(1)} %get-tuple-element.141), channel_id=1, source_target_pairs={{0,4},{2,6},{4,0},{6,2},{1,5},{3,7},{5,1},{7,3},{8,12},{10,14},{12... | collective-permute-start | bytes 442376 | tf_op jit(solution)/shard_map/ppermute | solution.py:166
  81.3 3.8 %collective-permute-done.14 = bf16[4,24,768]{2,1,0:T(8,128)(2,1)S(1)} collective-permute-done((bf16[4,24,768]{2,1,0:T(8,128)(2,1)S(1)}, bf16[4,24,768]{2,1,0:T(8,128)(2,1)S(1)}, u32[]{:S(2)}, u32[]{:S(2)}) %collective-permute-start.14) | collective-permute-done | bytes 147488 | tf_op jit(solution)/shard_map/ppermute | solution.py:166
  85.2 1.0 %add_convert_fusion = bf16[256,768]{1,0:T(8,128)(2,1)} fusion(bf16[256,768]{1,0:T(8,128)(2,1)S(1)} %collective-permute-done.12, bf16[256,768]{1,0:T(8,128)(2,1)S(1)} %collective-permute-done.11, bf16[256,768]{1,0:T(8,128)(2,1)S(1)} %collective-permute-done.10, bf16[256,768]{1,0:T(8,128)(2,1)S(1)} %copy-done.10, bf16[256,1,768]{2,0,1:T(8,128)(2,1)S(1)} %copy-done), kind=kLoop, calls=%fused_computation | loop fusion | flops 1966080 | bytes 2359296 | tf_op jit(solution)/shard_map/convert_element_type | solution.py:584
  86.9 1.2 %collective-permute-start.18 = (bf16[256,768]{1,0:T(8,128)(2,1)S(1)}, bf16[256,768]{1,0:T(8,128)(2,1)S(1)}, u32[]{:S(2)}, u32[]{:S(2)}) collective-permute-start(bf16[256,768]{1,0:T(8,128)(2,1)S(1)} %get-tuple-element.126), channel_id=1, source_target_pairs={{0,16},{8,24},{16,0},{24,8},{1,17},{9,25},{17,1},{25,9},{2,18},{10... | collective-permute-start | bytes 1179656 | tf_op jit(solution)/shard_map/ppermute | solution.py:166
  88.1 3.9 %collective-permute-done.19 = bf16[4,24,768]{2,1,0:T(8,128)(2,1)S(1)} collective-permute-done((bf16[4,24,768]{2,1,0:T(8,128)(2,1)S(1)}, bf16[4,24,768]{2,1,0:T(8,128)(2,1)S(1)}, u32[]{:S(2)}, u32[]{:S(2)}) %collective-permute-start.19) | collective-permute-done | bytes 147488 | tf_op jit(solution)/shard_map/ppermute | solution.py:166
  92.2 1.6 %collective-permute-start.23 = (bf16[24,576]{1,0:T(8,128)(2,1)S(1)}, bf16[24,576]{1,0:T(8,128)(2,1)S(1)}, u32[]{:S(2)}, u32[]{:S(2)}) collective-permute-start(bf16[24,576]{1,0:T(8,128)(2,1)S(1)} %get-tuple-element.145), channel_id=1, source_target_pairs={{0,24},{8,16},{16,8},{24,0},{1,25},{9,17},{17,9},{25,1},{2,26},{10... | collective-permute-start | bytes 82952 | tf_op jit(solution)/shard_map/ppermute | solution.py:166
  93.8 0.8 collective-permute-start.22
  94.6 1.1 %collective-permute-start.21 = (bf16[24,576]{1,0:T(8,128)(2,1)S(1)}, bf16[24,576]{1,0:T(8,128)(2,1)S(1)}, u32[]{:S(2)}, u32[]{:S(2)}) collective-permute-start(bf16[24,576]{1,0:T(8,128)(2,1)S(1)} %get-tuple-element.147), channel_id=1, source_target_pairs={{0,8},{8,0},{16,24},{24,16},{1,9},{9,1},{17,25},{25,17},{2,10},{10... | collective-permute-start | bytes 82952 | tf_op jit(solution)/shard_map/ppermute | solution.py:166
  95.7 1.4 %collective-permute-done.17.refs_1_ = bf16[256,768]{1,0:T(8,128)(2,1)S(1)} collective-permute-done((bf16[256,768]{1,0:T(8,128)(2,1)S(1)}, bf16[256,768]{1,0:T(8,128)(2,1)S(1)}, u32[]{:S(2)}, u32[]{:S(2)}) %collective-permute-start.17) | collective-permute-done | bytes 393248 | tf_op jit(solution)/shard_map/ppermute | solution.py:166
  97.2 1.4 %shard_map.130 = bf16[256,768]{1,0:T(8,128)(2,1)} custom-call(f32[1,768]{1,0:T(1,128)S(1)} %copy-done.4, bf16[256,768]{1,0:T(8,128)(2,1)S(1)} %bitcast.33, bf16[256,768]{1,0:T(8,128)(2,1)S(1)} %bitcast.38, bf16[256,768]{1,0:T(8,128)(2,1)S(1)} %copy-done.8, bf16[256,768]{1,0:T(8,128)(2,1)S(1)} %collective-permute-done.17.refs_1_, ...), custom_call_target="tpu_custom_call" | custom-call | flops 786432000 | bytes 2362368 | tf_op jit(solution)/shard_map/pallas_call | solution.py:477
  98.6 1.5 %shard_map.131 = (f32[24,768]{1,0:T(8,128)}, f32[24,768]{1,0:T(8,128)}, f32[24,768]{1,0:T(8,128)}, f32[24,768]{1,0:T(8,128)}, f32[1,24]{1,0:T(1,128)}) custom-call(s32[3]{0:T(128)S(1)} %copy-done.5, f32[1,24]{1,0:T(1,128)S(1)} %dynamic-slice_bitcast_fusion.refs_1_, bf16[24,768]{1,0:T(8,128)(2,1)S(1)} %copy-done.1, bf16[24,768]{1,0:T(8,128)(2,1)S(1)} %copy-done.2, ...), custom_call_target="tpu_custom_call" | custom-call | flops 1000 | bytes 783564 | tf_op jit(solution)/shard_map/pallas_call | solution.py:477
  (73 shorter events, 8.3 us)
Async XLA Ops:
  0.6 16.1 %collective-permute-start.1 = (bf16[256,768]{1,0:T(8,128)(2,1)}, bf16[256,768]{1,0:T(8,128)(2,1)S(1)}, u32[]{:S(2)}, u32[]{:S(2)}) collective-permute-start(bf16[256,768]{1,0:T(8,128)(2,1)} %bitcast.29), channel_id=1, source_target_pairs={{0,16},{8,24},{16,0},{24,8},{1,17},{9,25},{17,1},{25,9},{2,18},{10... | collective-permute-start | bytes 1179656 | tf_op jit(solution)/shard_map/ppermute | solution.py:166
  3.7 13.1 %collective-permute-start = (bf16[256,768]{1,0:T(8,128)(2,1)}, bf16[256,768]{1,0:T(8,128)(2,1)S(1)}, u32[]{:S(2)}, u32[]{:S(2)}) collective-permute-start(bf16[256,768]{1,0:T(8,128)(2,1)} %bitcast.30), channel_id=1, source_target_pairs={{0,8},{8,0},{16,24},{24,16},{1,9},{9,1},{17,25},{25,17},{2,10},{10... | collective-permute-start | bytes 1179656 | tf_op jit(solution)/shard_map/ppermute | solution.py:166
  15.8 17.9 %copy-start.6 = (bf16[256,1,768]{2,0,1:T(8,128)(2,1)S(1)}, bf16[256,1,768]{2,0,1:T(8,128)(2,1)}, u32[]{:S(2)}) copy-start(bf16[256,1,768]{2,0,1:T(8,128)(2,1)} %param.13) | copy-start | bytes 1179652
  16.7 10.9 %copy-start.11 = (bf16[256,768]{1,0:T(8,128)(2,1)}, bf16[256,768]{1,0:T(8,128)(2,1)S(1)}, u32[]{:S(2)}) copy-start(bf16[256,768]{1,0:T(8,128)(2,1)S(1)} %collective-permute-done.1.refs_3_) | copy-start | bytes 1179652
  16.7 10.9 %copy-start.12 = (bf16[256,768]{1,0:T(8,128)(2,1)}, bf16[256,768]{1,0:T(8,128)(2,1)S(1)}, u32[]{:S(2)}) copy-start(bf16[256,768]{1,0:T(8,128)(2,1)S(1)} %collective-permute-done.refs_2_) | copy-start | bytes 1179652
  16.8 10.8 %collective-permute-start.2 = (bf16[256,768]{1,0:T(8,128)(2,1)}, bf16[256,768]{1,0:T(8,128)(2,1)S(1)}, u32[]{:S(2)}, u32[]{:S(2)}) collective-permute-start(bf16[256,768]{1,0:T(8,128)(2,1)} %bitcast.31), channel_id=1, source_target_pairs={{0,24},{8,16},{16,8},{24,0},{1,25},{9,17},{17,9},{25,1},{2,26},{10... | collective-permute-start | bytes 1179656 | tf_op jit(solution)/shard_map/ppermute | solution.py:166
  19.2 13.3 %collective-permute-start.5 = (bf16[4,24,768]{2,1,0:T(8,128)(2,1)S(1)}, bf16[4,24,768]{2,1,0:T(8,128)(2,1)S(1)}, u32[]{:S(2)}, u32[]{:S(2)}) collective-permute-start(bf16[4,24,768]{2,1,0:T(8,128)(2,1)S(1)} %pad_maximum_fusion.1), channel_id=1, source_target_pairs={{0,6},{2,4},{4,2},{6,0},{1,7},{3,5},{5,3},{7,1},{8,14},{10,12},{12... | collective-permute-start | bytes 442376 | tf_op jit(solution)/shard_map/ppermute | solution.py:166
  22.8 10.7 %collective-permute-start.4 = (bf16[4,24,768]{2,1,0:T(8,128)(2,1)S(1)}, bf16[4,24,768]{2,1,0:T(8,128)(2,1)S(1)}, u32[]{:S(2)}, u32[]{:S(2)}) collective-permute-start(bf16[4,24,768]{2,1,0:T(8,128)(2,1)S(1)} %pad_maximum_fusion.1), channel_id=1, source_target_pairs={{0,4},{2,6},{4,0},{6,2},{1,5},{3,7},{5,1},{7,3},{8,12},{10,14},{12... | collective-permute-start | bytes 442376 | tf_op jit(solution)/shard_map/ppermute | solution.py:166
  22.8 10.7 %collective-permute-start.3 = (bf16[4,24,768]{2,1,0:T(8,128)(2,1)S(1)}, bf16[4,24,768]{2,1,0:T(8,128)(2,1)S(1)}, u32[]{:S(2)}, u32[]{:S(2)}) collective-permute-start(bf16[4,24,768]{2,1,0:T(8,128)(2,1)S(1)} %pad_maximum_fusion.1), channel_id=1, source_target_pairs={{0,2},{2,0},{4,6},{6,4},{1,3},{3,1},{5,7},{7,5},{8,10},{10,8},{12,... | collective-permute-start | bytes 442376 | tf_op jit(solution)/shard_map/ppermute | solution.py:166
  33.6 3.6 %collective-permute-start.9 = (bf16[4,4,24,768]{3,2,1,0:T(8,128)(2,1)S(1)}, bf16[4,4,24,768]{3,2,1,0:T(8,128)(2,1)S(1)}, u32[]{:S(2)}, u32[]{:S(2)}) collective-permute-start(bf16[4,4,24,768]{3,2,1,0:T(8,128)(2,1)S(1)} %pad_maximum_fusion.refs_1_), channel_id=1, source_target_pairs={{0,1},{1,0},{2,3},{3,2},{4,5},{5,4},{6,7},{7,6},{8,9},{9,8},{10,11... | collective-permute-start | bytes 1769480 | tf_op jit(solution)/shard_map/ppermute | solution.py:166
  33.7 16.4 %collective-permute-start.8 = (bf16[256,768]{1,0:T(8,128)(2,1)S(1)}, bf16[256,768]{1,0:T(8,128)(2,1)S(1)}, u32[]{:S(2)}, u32[]{:S(2)}) collective-permute-start(bf16[256,768]{1,0:T(8,128)(2,1)S(1)} %bitcast.35), channel_id=1, source_target_pairs={{0,24},{8,16},{16,8},{24,0},{1,25},{9,17},{17,9},{25,1},{2,26},{10... | collective-permute-start | bytes 1179656 | tf_op jit(solution)/shard_map/ppermute | solution.py:166
  34.9 19.7 %collective-permute-start.7 = (bf16[256,768]{1,0:T(8,128)(2,1)S(1)}, bf16[256,768]{1,0:T(8,128)(2,1)S(1)}, u32[]{:S(2)}, u32[]{:S(2)}) collective-permute-start(bf16[256,768]{1,0:T(8,128)(2,1)S(1)} %bitcast.36), channel_id=1, source_target_pairs={{0,16},{8,24},{16,0},{24,8},{1,17},{9,25},{17,1},{25,9},{2,18},{10... | collective-permute-start | bytes 1179656 | tf_op jit(solution)/shard_map/ppermute | solution.py:166
  35.4 19.2 %collective-permute-start.6 = (bf16[256,768]{1,0:T(8,128)(2,1)S(1)}, bf16[256,768]{1,0:T(8,128)(2,1)S(1)}, u32[]{:S(2)}, u32[]{:S(2)}) collective-permute-start(bf16[256,768]{1,0:T(8,128)(2,1)S(1)} %bitcast.37), channel_id=1, source_target_pairs={{0,8},{8,0},{16,24},{24,16},{1,9},{9,1},{17,25},{25,17},{2,10},{10... | collective-permute-start | bytes 1179656 | tf_op jit(solution)/shard_map/ppermute | solution.py:166
  48.3 24.9 %collective-permute-start.10 = (bf16[256,768]{1,0:T(8,128)(2,1)}, bf16[256,768]{1,0:T(8,128)(2,1)S(1)}, u32[]{:S(2)}, u32[]{:S(2)}) collective-permute-start(bf16[256,768]{1,0:T(8,128)(2,1)} %get-tuple-element.104), channel_id=1, source_target_pairs={{0,8},{8,0},{16,24},{24,16},{1,9},{9,1},{17,25},{25,17},{2,10},{10... | collective-permute-start | bytes 1179656 | tf_op jit(solution)/shard_map/ppermute | solution.py:166
  48.6 24.7 %collective-permute-start.11 = (bf16[256,768]{1,0:T(8,128)(2,1)}, bf16[256,768]{1,0:T(8,128)(2,1)S(1)}, u32[]{:S(2)}, u32[]{:S(2)}) collective-permute-start(bf16[256,768]{1,0:T(8,128)(2,1)} %get-tuple-element.105), channel_id=1, source_target_pairs={{0,16},{8,24},{16,0},{24,8},{1,17},{9,25},{17,1},{25,9},{2,18},{10... | collective-permute-start | bytes 1179656 | tf_op jit(solution)/shard_map/ppermute | solution.py:166
  50.1 23.2 %collective-permute-start.12 = (bf16[256,768]{1,0:T(8,128)(2,1)}, bf16[256,768]{1,0:T(8,128)(2,1)S(1)}, u32[]{:S(2)}, u32[]{:S(2)}) collective-permute-start(bf16[256,768]{1,0:T(8,128)(2,1)} %get-tuple-element.106), channel_id=1, source_target_pairs={{0,24},{8,16},{16,8},{24,0},{1,25},{9,17},{17,9},{25,1},{2,26},{10... | collective-permute-start | bytes 1179656 | tf_op jit(solution)/shard_map/ppermute | solution.py:166
  73.2 11.9 %copy-start = (bf16[256,1,768]{2,0,1:T(8,128)(2,1)S(1)}, bf16[256,1,768]{2,0,1:T(8,128)(2,1)}, u32[]{:S(2)}) copy-start(bf16[256,1,768]{2,0,1:T(8,128)(2,1)} %param.7) | copy-start | bytes 1179652
  73.2 11.9 %copy-start.10 = (bf16[256,768]{1,0:T(8,128)(2,1)S(1)}, bf16[256,768]{1,0:T(8,128)(2,1)}, u32[]{:S(2)}) copy-start(bf16[256,768]{1,0:T(8,128)(2,1)} %get-tuple-element.119) | copy-start | bytes 1179652
  73.3 2.3 %collective-permute-start.13 = (bf16[4,4,24,768]{3,2,1,0:T(8,128)(2,1)}, bf16[4,4,24,768]{3,2,1,0:T(8,128)(2,1)S(1)}, u32[]{:S(2)}, u32[]{:S(2)}) collective-permute-start(bf16[4,4,24,768]{3,2,1,0:T(8,128)(2,1)} %get-tuple-element.109), channel_id=1, source_target_pairs={{0,1},{1,0},{2,3},{3,2},{4,5},{5,4},{6,7},{7,6},{8,9},{9,8},{10,11... | collective-permute-start | bytes 1769480 | tf_op jit(solution)/shard_map/ppermute | solution.py:166
  73.4 7.9 %collective-permute-start.15 = (bf16[128,768]{1,0:T(8,128)(2,1)}, bf16[128,768]{1,0:T(8,128)(2,1)S(1)}, u32[]{:S(2)}, u32[]{:S(2)}) collective-permute-start(bf16[128,768]{1,0:T(8,128)(2,1)} %get-tuple-element.110), channel_id=1, source_target_pairs={{0,8},{8,0},{16,24},{24,16},{1,9},{9,1},{17,25},{25,17},{2,10},{10... | collective-permute-start | bytes 589832 | tf_op jit(solution)/shard_map/ppermute | solution.py:166
  73.9 7.4 %collective-permute-start.16 = (bf16[128,768]{1,0:T(8,128)(2,1)}, bf16[128,768]{1,0:T(8,128)(2,1)S(1)}, u32[]{:S(2)}, u32[]{:S(2)}) collective-permute-start(bf16[128,768]{1,0:T(8,128)(2,1)} %get-tuple-element.111), channel_id=1, source_target_pairs={{0,16},{8,24},{16,0},{24,8},{1,17},{9,25},{17,1},{25,9},{2,18},{10... | collective-permute-start | bytes 589832 | tf_op jit(solution)/shard_map/ppermute | solution.py:166
  76.8 8.3 %collective-permute-start.14 = (bf16[4,24,768]{2,1,0:T(8,128)(2,1)S(1)}, bf16[4,24,768]{2,1,0:T(8,128)(2,1)S(1)}, u32[]{:S(2)}, u32[]{:S(2)}) collective-permute-start(bf16[4,24,768]{2,1,0:T(8,128)(2,1)S(1)} %get-tuple-element.144), channel_id=1, source_target_pairs={{0,2},{2,0},{4,6},{6,4},{1,3},{3,1},{5,7},{7,5},{8,10},{10,8},{12,... | collective-permute-start | bytes 442376 | tf_op jit(solution)/shard_map/ppermute | solution.py:166
  78.0 14.0 %collective-permute-start.19 = (bf16[4,24,768]{2,1,0:T(8,128)(2,1)S(1)}, bf16[4,24,768]{2,1,0:T(8,128)(2,1)S(1)}, u32[]{:S(2)}, u32[]{:S(2)}) collective-permute-start(bf16[4,24,768]{2,1,0:T(8,128)(2,1)S(1)} %get-tuple-element.141), channel_id=1, source_target_pairs={{0,4},{2,6},{4,0},{6,2},{1,5},{3,7},{5,1},{7,3},{8,12},{10,14},{12... | collective-permute-start | bytes 442376 | tf_op jit(solution)/shard_map/ppermute | solution.py:166
  80.6 11.4 %collective-permute-start.20 = (bf16[4,24,768]{2,1,0:T(8,128)(2,1)S(1)}, bf16[4,24,768]{2,1,0:T(8,128)(2,1)S(1)}, u32[]{:S(2)}, u32[]{:S(2)}) collective-permute-start(bf16[4,24,768]{2,1,0:T(8,128)(2,1)S(1)} %get-tuple-element.142), channel_id=1, source_target_pairs={{0,6},{2,4},{4,2},{6,0},{1,7},{3,5},{5,3},{7,1},{8,14},{10,12},{12... | collective-permute-start | bytes 442376 | tf_op jit(solution)/shard_map/ppermute | solution.py:166
  86.2 11.0 %copy-start.4 = (f32[1,768]{1,0:T(1,128)S(1)}, f32[1,768]{1,0:T(1,128)}, u32[]{:S(2)}) copy-start(f32[1,768]{1,0:T(1,128)} %reshape.51.refs_0_.gain) | copy-start | bytes 9220
  86.2 11.0 %copy-start.7 = (bf16[256,1,768]{2,0,1:T(8,128)(2,1)S(1)}, bf16[256,1,768]{2,0,1:T(8,128)(2,1)}, u32[]{:S(2)}) copy-start(bf16[256,1,768]{2,0,1:T(8,128)(2,1)} %param.13) | copy-start | bytes 1179652
  86.2 11.0 %copy-start.8 = (bf16[256,768]{1,0:T(8,128)(2,1)S(1)}, bf16[256,768]{1,0:T(8,128)(2,1)}, u32[]{:S(2)}) copy-start(bf16[256,768]{1,0:T(8,128)(2,1)} %get-tuple-element.124.refs_0_) | copy-start | bytes 1179652
  86.3 10.8 %collective-permute-start.17 = (bf16[256,768]{1,0:T(8,128)(2,1)S(1)}, bf16[256,768]{1,0:T(8,128)(2,1)S(1)}, u32[]{:S(2)}, u32[]{:S(2)}) collective-permute-start(bf16[256,768]{1,0:T(8,128)(2,1)S(1)} %get-tuple-element.125), channel_id=1, source_target_pairs={{0,8},{8,0},{16,24},{24,16},{1,9},{9,1},{17,25},{25,17},{2,10},{10... | collective-permute-start | bytes 1179656 | tf_op jit(solution)/shard_map/ppermute | solution.py:166
  86.9 10.3 %collective-permute-start.18 = (bf16[256,768]{1,0:T(8,128)(2,1)S(1)}, bf16[256,768]{1,0:T(8,128)(2,1)S(1)}, u32[]{:S(2)}, u32[]{:S(2)}) collective-permute-start(bf16[256,768]{1,0:T(8,128)(2,1)S(1)} %get-tuple-element.126), channel_id=1, source_target_pairs={{0,16},{8,24},{16,0},{24,8},{1,17},{9,25},{17,1},{25,9},{2,18},{10... | collective-permute-start | bytes 1179656 | tf_op jit(solution)/shard_map/ppermute | solution.py:166
  92.2 6.4 %collective-permute-start.23 = (bf16[24,576]{1,0:T(8,128)(2,1)S(1)}, bf16[24,576]{1,0:T(8,128)(2,1)S(1)}, u32[]{:S(2)}, u32[]{:S(2)}) collective-permute-start(bf16[24,576]{1,0:T(8,128)(2,1)S(1)} %get-tuple-element.145), channel_id=1, source_target_pairs={{0,24},{8,16},{16,8},{24,0},{1,25},{9,17},{17,9},{25,1},{2,26},{10... | collective-permute-start | bytes 82952 | tf_op jit(solution)/shard_map/ppermute | solution.py:166
  93.8 4.8 %collective-permute-start.22 = (bf16[24,576]{1,0:T(8,128)(2,1)S(1)}, bf16[24,576]{1,0:T(8,128)(2,1)S(1)}, u32[]{:S(2)}, u32[]{:S(2)}) collective-permute-start(bf16[24,576]{1,0:T(8,128)(2,1)S(1)} %get-tuple-element.146), channel_id=1, source_target_pairs={{0,16},{8,24},{16,0},{24,8},{1,17},{9,25},{17,1},{25,9},{2,18},{10... | collective-permute-start | bytes 82952 | tf_op jit(solution)/shard_map/ppermute | solution.py:166
  94.6 4.0 %collective-permute-start.21 = (bf16[24,576]{1,0:T(8,128)(2,1)S(1)}, bf16[24,576]{1,0:T(8,128)(2,1)S(1)}, u32[]{:S(2)}, u32[]{:S(2)}) collective-permute-start(bf16[24,576]{1,0:T(8,128)(2,1)S(1)} %get-tuple-element.147), channel_id=1, source_target_pairs={{0,8},{8,0},{16,24},{24,16},{1,9},{9,1},{17,25},{25,17},{2,10},{10... | collective-permute-start | bytes 82952 | tf_op jit(solution)/shard_map/ppermute | solution.py:166
  (12 other events, 56.1 us)

commit v5 on v3

--- a/solution.py
+++ b/solution.py
@@ -223,6 +223,7 @@
         lanes = slice(d * span, (d + 1) * span)
         for i, w in enumerate((w_query, w_key, w_value)):
             out[d, :, i * span : (i + 1) * span] = w[:, lanes]
+        out[d, :, 3 * span :] = w_out[:, lanes]
         out_cut[d] = w_out[:, lanes]
 
 
@@ -509,13 +510,13 @@
         pack_kernel,
         dims,
         [(w, VMEM) for w in (w_query, w_key, w_value, w_out)],
-        [((depth, shard, 3 * span), BF16, VMEM), ((depth, shard, span), BF16, VMEM)],
+        [((depth, shard, 4 * span), BF16, VMEM), ((depth, shard, span), BF16, VMEM)],
         [],
         [],
         1000,
     )
     mine = lax.all_to_all(packed, "depth", 0, 0, tiled=True)
-    mine = jnp.concatenate([mine, out_cut], axis=2)
+    mine = lax.dynamic_update_slice(mine, out_cut, (0, 0, 3 * span))
     mine, *xs = lax.optimization_barrier([mine] + xs)
     xs.append(swap(xs[0], "depth", depth, depth - 1))
     parts = [mine] + [swap(mine, "z", zs, k) for k in range(1, zs)]
@@ -574,6 +575,7 @@
         + [((span, width), F32), norm],
         [depth + 12, depth + 1],
         24 * pass_flops,
+        50,
     )
 
     outs = [outs[0]] + [swap(outs[k], "depth", depth, k) for k in range(1, depth)]

time: 99.4 us -> 105 us (1.056)
  local copies, waits for them, and re-layouts: 4.66 us -> 8.84 us
  Pallas kernels: 35.2 us -> 37.1 us
    unnamed x40 -> x34, local copies, waits for them, and re-layouts: 2.63 us -> 5.24 us
    pallas_call x6, Pallas kernels: 35.2 us -> 37.1 us  [call(): pl.pallas_call(functools.partial(kernel, dims), out_shape=shapes, in_spec...]
    dynamic_update_slice x0 -> x1, local copies, waits for them, and re-layouts: none -> 1.57 us  [head_body(): mine = lax.dynamic_update_slice(mine, out_cut, (0, 0, 3 * span))]
  transfers between devices with their start and end apart: 24 -> 24, of which waited for: 8 -> 9; matrix products, arithmetic and copies ran while one was open for 6% -> 6% of each run, Pallas kernels for 34% -> 34%
where the time goes in v5:
time: 105 us; the launch traced here: 104 us
  Pallas kernels  37.1 us (35%)
  starting transfers between devices  30.1 us (29%)
  waiting for transfers between devices  15.1 us (14%)
  blocking collectives  9.28 us (9%)
  local copies, waits for them, and re-layouts  8.84 us (8%)
  other arithmetic  3.09 us (3%)
    pallas_call x6, Pallas kernels, call(): pl.pallas_call(functools.partial(kernel, dims), out_shape=shapes, in_spec...  37.1 us
    ppermute x24, starting transfers between devices, swap(): return lax.ppermute(value, axis, [(i, i ^ bits) for i in range(size)])  30.1 us
    ppermute x24, waiting for transfers between devices, swap(): return lax.ppermute(value, axis, [(i, i ^ bits) for i in range(size)])  15.1 us
    all_to_all x1, blocking collectives, head_body(): mine = lax.all_to_all(packed, 'depth', 0, 0, tiled=True)  9.28 us
    unnamed x34, local copies, waits for them, and re-layouts  5.24 us
  transfers between devices with their start and end apart: 24, of which 9 were waited for; matrix products, arithmetic and copies ran while one was open for 6% of the time, Pallas kernels for 34%

profile of v5, /device:TPU:0, one launch (start us, length us, event | category | flops | bytes accessed | tf_op | source)
XLA Modules:
  0.0 104.4 jit_solution(11315690677860140750)
XLA Ops:
  0.6 3.0 %collective-permute-start.1 = (bf16[256,768]{1,0:T(8,128)(2,1)}, bf16[256,768]{1,0:T(8,128)(2,1)S(1)}, u32[]{:S(2)}, u32[]{:S(2)}) collective-permute-start(bf16[256,768]{1,0:T(8,128)(2,1)} %bitcast.29), channel_id=1, source_target_pairs={{0,16},{8,24},{16,0},{24,8},{1,17},{9,25},{17,1},{25,9},{2,18},{10... | collective-permute-start | bytes 1179656 | tf_op jit(solution)/shard_map/ppermute | solution.py:166
  3.7 1.5 %collective-permute-start = (bf16[256,768]{1,0:T(8,128)(2,1)}, bf16[256,768]{1,0:T(8,128)(2,1)S(1)}, u32[]{:S(2)}, u32[]{:S(2)}) collective-permute-start(bf16[256,768]{1,0:T(8,128)(2,1)} %bitcast.30), channel_id=1, source_target_pairs={{0,8},{8,0},{16,24},{24,16},{1,9},{9,1},{17,25},{25,17},{2,10},{10... | collective-permute-start | bytes 1179656 | tf_op jit(solution)/shard_map/ppermute | solution.py:166
  5.2 1.6 %shard_map.126 = (bf16[4,24,768]{2,1,0:T(8,128)(2,1)}, bf16[4,24,192]{2,1,0:T(8,128)(2,1)}) custom-call(bf16[24,768]{1,0:T(8,128)(2,1)} %refs_2_.1, bf16[24,768]{1,0:T(8,128)(2,1)} %refs_3_.1, bf16[24,768]{1,0:T(8,128)(2,1)} %refs_4_.1, bf16[24,768]{1,0:T(8,128)(2,1)} %w_out.1), custom_call_target="tpu_custom_call" | custom-call | flops 1000 | bytes 331776 | tf_op jit(solution)/shard_map/pallas_call | solution.py:483
  6.7 9.3 %all_to_all.5 = bf16[4,24,768]{2,1,0:T(8,128)(2,1)S(1)} all-to-all(bf16[4,24,768]{2,1,0:T(8,128)(2,1)} %get-tuple-element.75), channel_id=1, replica_groups=mesh['depth'=4,'z'=4,'core'=2] {'depth'}, dimensions={0} | all-to-all | bytes 294912 | tf_op jit(solution)/shard_map/all_to_all | solution.py:518
  16.0 1.6 %dynamic_update_slice.3 = bf16[4,24,768]{2,1,0:T(8,128)(2,1)S(1)} dynamic-update-slice(bf16[4,24,768]{2,1,0:T(8,128)(2,1)S(1)} %all_to_all.5, bf16[4,24,192]{2,1,0:T(8,128)(2,1)} %get-tuple-element.76, s32[]{:T(128)} %constant.9.clone.1, s32[]{:T(128)} %constant.9.clone.1, s32[]{:T(128)} %constant.10.clone.1) | dynamic-update-slice | bytes 73732 | tf_op jit(solution)/shard_map/dynamic_update_slice | solution.py:519
  17.6 2.5 %collective-permute-start.2 = (bf16[256,768]{1,0:T(8,128)(2,1)}, bf16[256,768]{1,0:T(8,128)(2,1)S(1)}, u32[]{:S(2)}, u32[]{:S(2)}) collective-permute-start(bf16[256,768]{1,0:T(8,128)(2,1)} %bitcast.31), channel_id=1, source_target_pairs={{0,24},{8,16},{16,8},{24,0},{1,25},{9,17},{17,9},{25,1},{2,26},{10... | collective-permute-start | bytes 1179656 | tf_op jit(solution)/shard_map/ppermute | solution.py:166
  20.1 3.6 %collective-permute-start.5 = (bf16[4,24,768]{2,1,0:T(8,128)(2,1)S(1)}, bf16[4,24,768]{2,1,0:T(8,128)(2,1)S(1)}, u32[]{:S(2)}, u32[]{:S(2)}) collective-permute-start(bf16[4,24,768]{2,1,0:T(8,128)(2,1)S(1)} %dynamic_update_slice.3), channel_id=1, source_target_pairs={{0,6},{2,4},{4,2},{6,0},{1,7},{3,5},{5,3},{7,1},{8,14},{10,12},{12... | collective-permute-start | bytes 442376 | tf_op jit(solution)/shard_map/ppermute | solution.py:166
  25.3 1.3 %reshape.51.refs_0_.gain = f32[1,768]{1,0:T(1,128)} reshape(f32[768]{0:T(1024)} %param.8) | data formatting | bytes 6144 | tf_op jit(solution)/shard_map/reshape | solution.py:504
  27.1 1.4 %collective-permute-done.2.refs_4_ = bf16[256,768]{1,0:T(8,128)(2,1)S(1)} collective-permute-done((bf16[256,768]{1,0:T(8,128)(2,1)}, bf16[256,768]{1,0:T(8,128)(2,1)S(1)}, u32[]{:S(2)}, u32[]{:S(2)}) %collective-permute-start.2) | collective-permute-done | bytes 393248 | tf_op jit(solution)/shard_map/ppermute | solution.py:166
  29.2 4.2 %shard_map.127 = (bf16[1024,768]{1,0:T(8,128)(2,1)}, bf16[768,1024]{1,0:T(8,128)(2,1)}) custom-call(f32[1,768]{1,0:T(1,128)} %reshape.51.refs_0_.gain, bf16[256,768]{1,0:T(8,128)(2,1)} %bitcast.32, bf16[256,768]{1,0:T(8,128)(2,1)} %copy-done.14, bf16[256,768]{1,0:T(8,128)(2,1)} %copy-done.13, bf16[256,768]{1,0:T(8,128)(2,1)} %copy-done.15), custom_call_target="tpu_custom_call" | custom-call | flops 1000 | bytes 4721664 | tf_op jit(solution)/shard_map/pallas_call | solution.py:483
  33.4 1.0 collective-permute-done.4
  34.6 1.2 %collective-permute-start.8 = (bf16[256,768]{1,0:T(8,128)(2,1)S(1)}, bf16[256,768]{1,0:T(8,128)(2,1)S(1)}, u32[]{:S(2)}, u32[]{:S(2)}) collective-permute-start(bf16[256,768]{1,0:T(8,128)(2,1)S(1)} %bitcast.34), channel_id=1, source_target_pairs={{0,24},{8,16},{16,8},{24,0},{1,25},{9,17},{17,9},{25,1},{2,26},{10... | collective-permute-start | bytes 1179656 | tf_op jit(solution)/shard_map/ppermute | solution.py:166
  36.6 1.6 %collective-permute-start.6 = (bf16[256,768]{1,0:T(8,128)(2,1)S(1)}, bf16[256,768]{1,0:T(8,128)(2,1)S(1)}, u32[]{:S(2)}, u32[]{:S(2)}) collective-permute-start(bf16[256,768]{1,0:T(8,128)(2,1)S(1)} %bitcast.36), channel_id=1, source_target_pairs={{0,8},{8,0},{16,24},{24,16},{1,9},{9,1},{17,25},{25,17},{2,10},{10... | collective-permute-start | bytes 1179656 | tf_op jit(solution)/shard_map/ppermute | solution.py:166
  39.0 10.1 %shard_map.128 = (bf16[1024,192]{1,0:T(8,128)(2,1)}, bf16[192,1024]{1,0:T(8,128)(2,1)}, bf16[1024,192]{1,0:T(8,128)(2,1)}, bf16[1024,192]{1,0:T(8,128)(2,1)}, bf...) custom-call(s32[3]{0:T(128)} %pad_add_fusion.refs_0_, ...), custom_call_target="tpu_custom_call" | custom-call | flops 3221225472 | bytes 8269836 | tf_op jit(solution)/shard_map/pallas_call | solution.py:483
  49.6 1.2 %collective-permute-start.11 = (bf16[256,768]{1,0:T(8,128)(2,1)}, bf16[256,768]{1,0:T(8,128)(2,1)S(1)}, u32[]{:S(2)}, u32[]{:S(2)}) collective-permute-start(bf16[256,768]{1,0:T(8,128)(2,1)} %get-tuple-element.109), channel_id=1, source_target_pairs={{0,16},{8,24},{16,0},{24,8},{1,17},{9,25},{17,1},{25,9},{2,18},{10... | collective-permute-start | bytes 1179656 | tf_op jit(solution)/shard_map/ppermute | solution.py:166
  50.9 1.8 %collective-permute-start.12 = (bf16[256,768]{1,0:T(8,128)(2,1)}, bf16[256,768]{1,0:T(8,128)(2,1)S(1)}, u32[]{:S(2)}, u32[]{:S(2)}) collective-permute-start(bf16[256,768]{1,0:T(8,128)(2,1)} %get-tuple-element.110), channel_id=1, source_target_pairs={{0,24},{8,16},{16,8},{24,0},{1,25},{9,17},{17,9},{25,1},{2,26},{10... | collective-permute-start | bytes 1179656 | tf_op jit(solution)/shard_map/ppermute | solution.py:166
  52.7 2.9 %collective-permute-done.7.refs_3_ = bf16[256,768]{1,0:T(8,128)(2,1)S(1)} collective-permute-done((bf16[256,768]{1,0:T(8,128)(2,1)S(1)}, bf16[256,768]{1,0:T(8,128)(2,1)S(1)}, u32[]{:S(2)}, u32[]{:S(2)}) %collective-permute-start.7) | collective-permute-done | bytes 393248 | tf_op jit(solution)/shard_map/ppermute | solution.py:166
  59.2 18.4 %shard_map.129 = (bf16[4,4,24,768]{3,2,1,0:T(8,128)(2,1)}, bf16[4,4,24,768]{3,2,1,0:T(8,128)(2,1)}, bf16[256,768]{1,0:T(8,128)(2,1)S(1)}, bf16[256,768]{1,0:T(8,...) custom-call(s32[3]{0:T(128)S(1)} %copy-done.5, ...), custom_call_target="tpu_custom_call" | custom-call | flops 9663676416 | bytes 9842700 | tf_op jit(solution)/shard_map/pallas_call | solution.py:483
  78.4 1.0 collective-permute-start.16
  79.9 1.3 %fusion.1 = (bf16[4,24,768]{2,1,0:T(8,128)(2,1)S(1)}, bf16[4,24,768]{2,1,0:T(8,128)(2,1)S(1)}, f32[4,24,768]{2,1,0:T(8,128)S(1)}, bf16[4,24,768]{2,1,0:T(8,128)(2,1)S(1)}) fusion(bf16[4,4,24,768]{3,2,1,0:T(8,128)(2,1)S(1)} %collective-permute-done.13, bf16[4,4,24,768]{3,2,1,0:T(8,128)(2,1)} %get-tuple-element.112), kind=kLoop, calls=%fused_computation.10 | loop fusion | flops 1105920 | bytes 1916928 | tf_op jit(solution)/shard_map/convert_element_type | solution.py:588
  81.1 1.2 %collective-permute-start.14 = (bf16[4,24,768]{2,1,0:T(8,128)(2,1)S(1)}, bf16[4,24,768]{2,1,0:T(8,128)(2,1)S(1)}, u32[]{:S(2)}, u32[]{:S(2)}) collective-permute-start(bf16[4,24,768]{2,1,0:T(8,128)(2,1)S(1)} %get-tuple-element.148), channel_id=1, source_target_pairs={{0,2},{2,0},{4,6},{6,4},{1,3},{3,1},{5,7},{7,5},{8,10},{10,8},{12,... | collective-permute-start | bytes 442376 | tf_op jit(solution)/shard_map/ppermute | solution.py:166
  82.3 2.6 %collective-permute-start.19 = (bf16[4,24,768]{2,1,0:T(8,128)(2,1)S(1)}, bf16[4,24,768]{2,1,0:T(8,128)(2,1)S(1)}, u32[]{:S(2)}, u32[]{:S(2)}) collective-permute-start(bf16[4,24,768]{2,1,0:T(8,128)(2,1)S(1)} %get-tuple-element.145), channel_id=1, source_target_pairs={{0,4},{2,6},{4,0},{6,2},{1,5},{3,7},{5,1},{7,3},{8,12},{10,14},{12... | collective-permute-start | bytes 442376 | tf_op jit(solution)/shard_map/ppermute | solution.py:166
  85.6 3.8 %collective-permute-done.14 = bf16[4,24,768]{2,1,0:T(8,128)(2,1)S(1)} collective-permute-done((bf16[4,24,768]{2,1,0:T(8,128)(2,1)S(1)}, bf16[4,24,768]{2,1,0:T(8,128)(2,1)S(1)}, u32[]{:S(2)}, u32[]{:S(2)}) %collective-permute-start.14) | collective-permute-done | bytes 147488 | tf_op jit(solution)/shard_map/ppermute | solution.py:166
  89.5 1.0 add_convert_fusion
  91.3 1.0 collective-permute-start.18
  92.4 4.0 %collective-permute-done.19 = bf16[4,24,768]{2,1,0:T(8,128)(2,1)S(1)} collective-permute-done((bf16[4,24,768]{2,1,0:T(8,128)(2,1)S(1)}, bf16[4,24,768]{2,1,0:T(8,128)(2,1)S(1)}, u32[]{:S(2)}, u32[]{:S(2)}) %collective-permute-start.19) | collective-permute-done | bytes 147488 | tf_op jit(solution)/shard_map/ppermute | solution.py:166
  96.5 1.6 %collective-permute-start.23 = (bf16[24,576]{1,0:T(8,128)(2,1)S(1)}, bf16[24,576]{1,0:T(8,128)(2,1)S(1)}, u32[]{:S(2)}, u32[]{:S(2)}) collective-permute-start(bf16[24,576]{1,0:T(8,128)(2,1)S(1)} %get-tuple-element.149), channel_id=1, source_target_pairs={{0,24},{8,16},{16,8},{24,0},{1,25},{9,17},{17,9},{25,1},{2,26},{10... | collective-permute-start | bytes 82952 | tf_op jit(solution)/shard_map/ppermute | solution.py:166
  98.0 1.0 collective-permute-start.22
  99.0 1.0 collective-permute-start.21
  100.0 1.3 %collective-permute-done.17.refs_1_ = bf16[256,768]{1,0:T(8,128)(2,1)S(1)} collective-permute-done((bf16[256,768]{1,0:T(8,128)(2,1)S(1)}, bf16[256,768]{1,0:T(8,128)(2,1)S(1)}, u32[]{:S(2)}, u32[]{:S(2)}) %collective-permute-start.17) | collective-permute-done | bytes 393248 | tf_op jit(solution)/shard_map/ppermute | solution.py:166
  101.4 1.4 %shard_map.130 = bf16[256,768]{1,0:T(8,128)(2,1)} custom-call(f32[1,768]{1,0:T(1,128)S(1)} %copy-done.4, bf16[256,768]{1,0:T(8,128)(2,1)S(1)} %bitcast.33, bf16[256,768]{1,0:T(8,128)(2,1)S(1)} %bitcast.38, bf16[256,768]{1,0:T(8,128)(2,1)S(1)} %get-tuple-element.128.refs_0_, bf16[256,768]{1,0:T(8,128)(2,1)S(1)} %collective-permute-done.17.refs_1_, ...), custom_call_target="tpu_custom_call" | custom-call | flops 786432000 | bytes 2362368 | tf_op jit(solution)/shard_map/pallas_call | solution.py:483
  102.9 1.5 %shard_map.131 = (f32[24,768]{1,0:T(8,128)}, f32[24,768]{1,0:T(8,128)}, f32[24,768]{1,0:T(8,128)}, f32[24,768]{1,0:T(8,128)}, f32[1,24]{1,0:T(1,128)}) custom-call(s32[3]{0:T(128)S(1)} %copy-done.5, f32[1,24]{1,0:T(1,128)S(1)} %dynamic-slice_bitcast_fusion.refs_1_, bf16[24,768]{1,0:T(8,128)(2,1)S(1)} %copy-done.1, bf16[24,768]{1,0:T(8,128)(2,1)S(1)} %copy-done.2, ...), custom_call_target="tpu_custom_call" | custom-call | flops 1000 | bytes 783564 | tf_op jit(solution)/shard_map/pallas_call | solution.py:483
  (67 shorter events, 11.9 us)
Async XLA Ops:
  0.6 17.0 %collective-permute-start.1 = (bf16[256,768]{1,0:T(8,128)(2,1)}, bf16[256,768]{1,0:T(8,128)(2,1)S(1)}, u32[]{:S(2)}, u32[]{:S(2)}) collective-permute-start(bf16[256,768]{1,0:T(8,128)(2,1)} %bitcast.29), channel_id=1, source_target_pairs={{0,16},{8,24},{16,0},{24,8},{1,17},{9,25},{17,1},{25,9},{2,18},{10... | collective-permute-start | bytes 1179656 | tf_op jit(solution)/shard_map/ppermute | solution.py:166
  3.7 14.0 %collective-permute-start = (bf16[256,768]{1,0:T(8,128)(2,1)}, bf16[256,768]{1,0:T(8,128)(2,1)S(1)}, u32[]{:S(2)}, u32[]{:S(2)}) collective-permute-start(bf16[256,768]{1,0:T(8,128)(2,1)} %bitcast.30), channel_id=1, source_target_pairs={{0,8},{8,0},{16,24},{24,16},{1,9},{9,1},{17,25},{25,17},{2,10},{10... | collective-permute-start | bytes 1179656 | tf_op jit(solution)/shard_map/ppermute | solution.py:166
  6.7 27.9 %copy-start.6 = (bf16[256,1,768]{2,0,1:T(8,128)(2,1)S(1)}, bf16[256,1,768]{2,0,1:T(8,128)(2,1)}, u32[]{:S(2)}) copy-start(bf16[256,1,768]{2,0,1:T(8,128)(2,1)} %param.13) | copy-start | bytes 1179652
  17.6 10.9 %copy-start.13 = (bf16[256,768]{1,0:T(8,128)(2,1)}, bf16[256,768]{1,0:T(8,128)(2,1)S(1)}, u32[]{:S(2)}) copy-start(bf16[256,768]{1,0:T(8,128)(2,1)S(1)} %collective-permute-done.1.refs_3_) | copy-start | bytes 1179652
  17.6 10.9 %copy-start.14 = (bf16[256,768]{1,0:T(8,128)(2,1)}, bf16[256,768]{1,0:T(8,128)(2,1)S(1)}, u32[]{:S(2)}) copy-start(bf16[256,768]{1,0:T(8,128)(2,1)S(1)} %collective-permute-done.refs_2_) | copy-start | bytes 1179652
  17.6 10.8 %collective-permute-start.2 = (bf16[256,768]{1,0:T(8,128)(2,1)}, bf16[256,768]{1,0:T(8,128)(2,1)S(1)}, u32[]{:S(2)}, u32[]{:S(2)}) collective-permute-start(bf16[256,768]{1,0:T(8,128)(2,1)} %bitcast.31), channel_id=1, source_target_pairs={{0,24},{8,16},{16,8},{24,0},{1,25},{9,17},{17,9},{25,1},{2,26},{10... | collective-permute-start | bytes 1179656 | tf_op jit(solution)/shard_map/ppermute | solution.py:166
  20.1 13.3 %collective-permute-start.5 = (bf16[4,24,768]{2,1,0:T(8,128)(2,1)S(1)}, bf16[4,24,768]{2,1,0:T(8,128)(2,1)S(1)}, u32[]{:S(2)}, u32[]{:S(2)}) collective-permute-start(bf16[4,24,768]{2,1,0:T(8,128)(2,1)S(1)} %dynamic_update_slice.3), channel_id=1, source_target_pairs={{0,6},{2,4},{4,2},{6,0},{1,7},{3,5},{5,3},{7,1},{8,14},{10,12},{12... | collective-permute-start | bytes 442376 | tf_op jit(solution)/shard_map/ppermute | solution.py:166
  23.7 10.7 %collective-permute-start.4 = (bf16[4,24,768]{2,1,0:T(8,128)(2,1)S(1)}, bf16[4,24,768]{2,1,0:T(8,128)(2,1)S(1)}, u32[]{:S(2)}, u32[]{:S(2)}) collective-permute-start(bf16[4,24,768]{2,1,0:T(8,128)(2,1)S(1)} %dynamic_update_slice.3), channel_id=1, source_target_pairs={{0,4},{2,6},{4,0},{6,2},{1,5},{3,7},{5,1},{7,3},{8,12},{10,14},{12... | collective-permute-start | bytes 442376 | tf_op jit(solution)/shard_map/ppermute | solution.py:166
  23.7 10.7 %collective-permute-start.3 = (bf16[4,24,768]{2,1,0:T(8,128)(2,1)S(1)}, bf16[4,24,768]{2,1,0:T(8,128)(2,1)S(1)}, u32[]{:S(2)}, u32[]{:S(2)}) collective-permute-start(bf16[4,24,768]{2,1,0:T(8,128)(2,1)S(1)} %dynamic_update_slice.3), channel_id=1, source_target_pairs={{0,2},{2,0},{4,6},{6,4},{1,3},{3,1},{5,7},{7,5},{8,10},{10,8},{12,... | collective-permute-start | bytes 442376 | tf_op jit(solution)/shard_map/ppermute | solution.py:166
  34.5 3.7 %collective-permute-start.9 = (bf16[4,4,24,768]{3,2,1,0:T(8,128)(2,1)S(1)}, bf16[4,4,24,768]{3,2,1,0:T(8,128)(2,1)S(1)}, u32[]{:S(2)}, u32[]{:S(2)}) collective-permute-start(bf16[4,4,24,768]{3,2,1,0:T(8,128)(2,1)S(1)} %pad_maximum_fusion.refs_1_), channel_id=1, source_target_pairs={{0,1},{1,0},{2,3},{3,2},{4,5},{5,4},{6,7},{7,6},{8,9},{9,8},{10,11... | collective-permute-start | bytes 1769480 | tf_op jit(solution)/shard_map/ppermute | solution.py:166
  34.6 21.0 %copy-start.5 = (s32[3]{0:T(128)S(1)}, s32[3]{0:T(128)}, u32[]{:S(2)}) copy-start(s32[3]{0:T(128)} %pad_add_fusion.refs_0_) | copy-start | bytes 40
  34.6 16.3 %collective-permute-start.8 = (bf16[256,768]{1,0:T(8,128)(2,1)S(1)}, bf16[256,768]{1,0:T(8,128)(2,1)S(1)}, u32[]{:S(2)}, u32[]{:S(2)}) collective-permute-start(bf16[256,768]{1,0:T(8,128)(2,1)S(1)} %bitcast.34), channel_id=1, source_target_pairs={{0,24},{8,16},{16,8},{24,0},{1,25},{9,17},{17,9},{25,1},{2,26},{10... | collective-permute-start | bytes 1179656 | tf_op jit(solution)/shard_map/ppermute | solution.py:166
  35.8 19.7 %collective-permute-start.7 = (bf16[256,768]{1,0:T(8,128)(2,1)S(1)}, bf16[256,768]{1,0:T(8,128)(2,1)S(1)}, u32[]{:S(2)}, u32[]{:S(2)}) collective-permute-start(bf16[256,768]{1,0:T(8,128)(2,1)S(1)} %bitcast.35), channel_id=1, source_target_pairs={{0,16},{8,24},{16,0},{24,8},{1,17},{9,25},{17,1},{25,9},{2,18},{10... | collective-permute-start | bytes 1179656 | tf_op jit(solution)/shard_map/ppermute | solution.py:166
  36.6 19.0 %collective-permute-start.6 = (bf16[256,768]{1,0:T(8,128)(2,1)S(1)}, bf16[256,768]{1,0:T(8,128)(2,1)S(1)}, u32[]{:S(2)}, u32[]{:S(2)}) collective-permute-start(bf16[256,768]{1,0:T(8,128)(2,1)S(1)} %bitcast.36), channel_id=1, source_target_pairs={{0,8},{8,0},{16,24},{24,16},{1,9},{9,1},{17,25},{25,17},{2,10},{10... | collective-permute-start | bytes 1179656 | tf_op jit(solution)/shard_map/ppermute | solution.py:166
  49.1 28.5 %collective-permute-start.10 = (bf16[256,768]{1,0:T(8,128)(2,1)}, bf16[256,768]{1,0:T(8,128)(2,1)S(1)}, u32[]{:S(2)}, u32[]{:S(2)}) collective-permute-start(bf16[256,768]{1,0:T(8,128)(2,1)} %get-tuple-element.108), channel_id=1, source_target_pairs={{0,8},{8,0},{16,24},{24,16},{1,9},{9,1},{17,25},{25,17},{2,10},{10... | collective-permute-start | bytes 1179656 | tf_op jit(solution)/shard_map/ppermute | solution.py:166
  49.6 28.0 %collective-permute-start.11 = (bf16[256,768]{1,0:T(8,128)(2,1)}, bf16[256,768]{1,0:T(8,128)(2,1)S(1)}, u32[]{:S(2)}, u32[]{:S(2)}) collective-permute-start(bf16[256,768]{1,0:T(8,128)(2,1)} %get-tuple-element.109), channel_id=1, source_target_pairs={{0,16},{8,24},{16,0},{24,8},{1,17},{9,25},{17,1},{25,9},{2,18},{10... | collective-permute-start | bytes 1179656 | tf_op jit(solution)/shard_map/ppermute | solution.py:166
  50.9 26.7 %collective-permute-start.12 = (bf16[256,768]{1,0:T(8,128)(2,1)}, bf16[256,768]{1,0:T(8,128)(2,1)S(1)}, u32[]{:S(2)}, u32[]{:S(2)}) collective-permute-start(bf16[256,768]{1,0:T(8,128)(2,1)} %get-tuple-element.110), channel_id=1, source_target_pairs={{0,24},{8,16},{16,8},{24,0},{1,25},{9,17},{17,9},{25,1},{2,26},{10... | collective-permute-start | bytes 1179656 | tf_op jit(solution)/shard_map/ppermute | solution.py:166
  77.6 11.9 %copy-start = (bf16[256,1,768]{2,0,1:T(8,128)(2,1)S(1)}, bf16[256,1,768]{2,0,1:T(8,128)(2,1)}, u32[]{:S(2)}) copy-start(bf16[256,1,768]{2,0,1:T(8,128)(2,1)} %param.7) | copy-start | bytes 1179652
  77.6 11.9 %copy-start.12 = (bf16[256,768]{1,0:T(8,128)(2,1)S(1)}, bf16[256,768]{1,0:T(8,128)(2,1)}, u32[]{:S(2)}) copy-start(bf16[256,768]{1,0:T(8,128)(2,1)} %get-tuple-element.123) | copy-start | bytes 1179652
  77.6 2.3 %collective-permute-start.13 = (bf16[4,4,24,768]{3,2,1,0:T(8,128)(2,1)}, bf16[4,4,24,768]{3,2,1,0:T(8,128)(2,1)S(1)}, u32[]{:S(2)}, u32[]{:S(2)}) collective-permute-start(bf16[4,4,24,768]{3,2,1,0:T(8,128)(2,1)} %get-tuple-element.113), channel_id=1, source_target_pairs={{0,1},{1,0},{2,3},{3,2},{4,5},{5,4},{6,7},{7,6},{8,9},{9,8},{10,11... | collective-permute-start | bytes 1769480 | tf_op jit(solution)/shard_map/ppermute | solution.py:166
  77.7 7.9 %collective-permute-start.15 = (bf16[128,768]{1,0:T(8,128)(2,1)S(1)}, bf16[128,768]{1,0:T(8,128)(2,1)S(1)}, u32[]{:S(2)}, u32[]{:S(2)}) collective-permute-start(bf16[128,768]{1,0:T(8,128)(2,1)S(1)} %get-tuple-element.114), channel_id=1, source_target_pairs={{0,8},{8,0},{16,24},{24,16},{1,9},{9,1},{17,25},{25,17},{2,10},{10... | collective-permute-start | bytes 589832 | tf_op jit(solution)/shard_map/ppermute | solution.py:166
  78.4 7.2 %collective-permute-start.16 = (bf16[128,768]{1,0:T(8,128)(2,1)S(1)}, bf16[128,768]{1,0:T(8,128)(2,1)S(1)}, u32[]{:S(2)}, u32[]{:S(2)}) collective-permute-start(bf16[128,768]{1,0:T(8,128)(2,1)S(1)} %get-tuple-element.115), channel_id=1, source_target_pairs={{0,16},{8,24},{16,0},{24,8},{1,17},{9,25},{17,1},{25,9},{2,18},{10... | collective-permute-start | bytes 589832 | tf_op jit(solution)/shard_map/ppermute | solution.py:166
  81.1 8.3 %collective-permute-start.14 = (bf16[4,24,768]{2,1,0:T(8,128)(2,1)S(1)}, bf16[4,24,768]{2,1,0:T(8,128)(2,1)S(1)}, u32[]{:S(2)}, u32[]{:S(2)}) collective-permute-start(bf16[4,24,768]{2,1,0:T(8,128)(2,1)S(1)} %get-tuple-element.148), channel_id=1, source_target_pairs={{0,2},{2,0},{4,6},{6,4},{1,3},{3,1},{5,7},{7,5},{8,10},{10,8},{12,... | collective-permute-start | bytes 442376 | tf_op jit(solution)/shard_map/ppermute | solution.py:166
  82.3 14.0 %collective-permute-start.19 = (bf16[4,24,768]{2,1,0:T(8,128)(2,1)S(1)}, bf16[4,24,768]{2,1,0:T(8,128)(2,1)S(1)}, u32[]{:S(2)}, u32[]{:S(2)}) collective-permute-start(bf16[4,24,768]{2,1,0:T(8,128)(2,1)S(1)} %get-tuple-element.145), channel_id=1, source_target_pairs={{0,4},{2,6},{4,0},{6,2},{1,5},{3,7},{5,1},{7,3},{8,12},{10,14},{12... | collective-permute-start | bytes 442376 | tf_op jit(solution)/shard_map/ppermute | solution.py:166
  84.9 11.4 %collective-permute-start.20 = (bf16[4,24,768]{2,1,0:T(8,128)(2,1)S(1)}, bf16[4,24,768]{2,1,0:T(8,128)(2,1)S(1)}, u32[]{:S(2)}, u32[]{:S(2)}) collective-permute-start(bf16[4,24,768]{2,1,0:T(8,128)(2,1)S(1)} %get-tuple-element.146), channel_id=1, source_target_pairs={{0,6},{2,4},{4,2},{6,0},{1,7},{3,5},{5,3},{7,1},{8,14},{10,12},{12... | collective-permute-start | bytes 442376 | tf_op jit(solution)/shard_map/ppermute | solution.py:166
  90.5 11.0 %copy-start.4 = (f32[1,768]{1,0:T(1,128)S(1)}, f32[1,768]{1,0:T(1,128)}, u32[]{:S(2)}) copy-start(f32[1,768]{1,0:T(1,128)} %reshape.51.refs_0_.gain) | copy-start | bytes 9220
  90.6 10.8 %collective-permute-start.17 = (bf16[256,768]{1,0:T(8,128)(2,1)S(1)}, bf16[256,768]{1,0:T(8,128)(2,1)S(1)}, u32[]{:S(2)}, u32[]{:S(2)}) collective-permute-start(bf16[256,768]{1,0:T(8,128)(2,1)S(1)} %get-tuple-element.129), channel_id=1, source_target_pairs={{0,8},{8,0},{16,24},{24,16},{1,9},{9,1},{17,25},{25,17},{2,10},{10... | collective-permute-start | bytes 1179656 | tf_op jit(solution)/shard_map/ppermute | solution.py:166
  91.3 10.1 %collective-permute-start.18 = (bf16[256,768]{1,0:T(8,128)(2,1)S(1)}, bf16[256,768]{1,0:T(8,128)(2,1)S(1)}, u32[]{:S(2)}, u32[]{:S(2)}) collective-permute-start(bf16[256,768]{1,0:T(8,128)(2,1)S(1)} %get-tuple-element.130), channel_id=1, source_target_pairs={{0,16},{8,24},{16,0},{24,8},{1,17},{9,25},{17,1},{25,9},{2,18},{10... | collective-permute-start | bytes 1179656 | tf_op jit(solution)/shard_map/ppermute | solution.py:166
  96.4 6.5 %copy-start.1 = (bf16[24,768]{1,0:T(8,128)(2,1)S(1)}, bf16[24,768]{1,0:T(8,128)(2,1)}, u32[]{:S(2)}) copy-start(bf16[24,768]{1,0:T(8,128)(2,1)} %refs_2_.1) | copy-start | bytes 110596
  96.5 6.4 %collective-permute-start.23 = (bf16[24,576]{1,0:T(8,128)(2,1)S(1)}, bf16[24,576]{1,0:T(8,128)(2,1)S(1)}, u32[]{:S(2)}, u32[]{:S(2)}) collective-permute-start(bf16[24,576]{1,0:T(8,128)(2,1)S(1)} %get-tuple-element.149), channel_id=1, source_target_pairs={{0,24},{8,16},{16,8},{24,0},{1,25},{9,17},{17,9},{25,1},{2,26},{10... | collective-permute-start | bytes 82952 | tf_op jit(solution)/shard_map/ppermute | solution.py:166
  98.0 4.8 %collective-permute-start.22 = (bf16[24,576]{1,0:T(8,128)(2,1)S(1)}, bf16[24,576]{1,0:T(8,128)(2,1)S(1)}, u32[]{:S(2)}, u32[]{:S(2)}) collective-permute-start(bf16[24,576]{1,0:T(8,128)(2,1)S(1)} %get-tuple-element.150), channel_id=1, source_target_pairs={{0,16},{8,24},{16,0},{24,8},{1,17},{9,25},{17,1},{25,9},{2,18},{10... | collective-permute-start | bytes 82952 | tf_op jit(solution)/shard_map/ppermute | solution.py:166
  99.0 3.9 %collective-permute-start.21 = (bf16[24,576]{1,0:T(8,128)(2,1)S(1)}, bf16[24,576]{1,0:T(8,128)(2,1)S(1)}, u32[]{:S(2)}, u32[]{:S(2)}) collective-permute-start(bf16[24,576]{1,0:T(8,128)(2,1)S(1)} %get-tuple-element.151), channel_id=1, source_target_pairs={{0,8},{8,0},{16,24},{24,16},{1,9},{9,1},{17,25},{25,17},{2,10},{10... | collective-permute-start | bytes 82952 | tf_op jit(solution)/shard_map/ppermute | solution.py:166
  (9 other events, 21.9 us)

commit v6 on v3

--- a/solution.py
+++ b/solution.py
@@ -475,7 +475,7 @@
 VMEM, ANY, SMEM = pltpu.VMEM, pl.ANY, pltpu.SMEM
 
 
-def call(kernel, dims, ins, outs, scratch, sems, flops, mib=56):
+def call(kernel, dims, ins, outs, scratch, sems, flops, mib=62):
     args = [a for a, _ in ins]
     shapes = [jax.ShapeDtypeStruct(shape, kind) for shape, kind, _ in outs]
     size = sum(a.size * a.dtype.itemsize for a in args + shapes)

time: 99.4 us -> 99.7 us (level)
    unnamed x40 -> x34, local copies, waits for them, and re-layouts: 2.63 us -> 1.67 us
  transfers between devices with their start and end apart: 24 -> 24, of which waited for: 8 -> 9; matrix products, arithmetic and copies ran while one was open for 6% -> 6% of each run, Pallas kernels for 34% -> 34%
where the time goes in v6:
time: 99.7 us; the launch traced here: 99.2 us
  Pallas kernels  35.2 us (35%)
  starting transfers between devices  30 us (30%)
  waiting for transfers between devices  15.3 us (15%)
  blocking collectives  9.04 us (9%)
  other arithmetic  4.95 us (5%)
  local copies, waits for them, and re-layouts  3.71 us (4%)
    pallas_call x6, Pallas kernels, call(): pl.pallas_call(functools.partial(kernel, dims), out_shape=shapes, in_spec...  35.2 us
    ppermute x24, starting transfers between devices, swap(): return lax.ppermute(value, axis, [(i, i ^ bits) for i in range(size)])  30 us
    ppermute x24, waiting for transfers between devices, swap(): return lax.ppermute(value, axis, [(i, i ^ bits) for i in range(size)])  15.3 us
    all_to_all x1, blocking collectives, head_body(): mine = lax.all_to_all(packed, 'depth', 0, 0, tiled=True)  9.04 us
  transfers between devices with their start and end apart: 24, of which 9 were waited for; matrix products, arithmetic and copies ran while one was open for 6% of the time, Pallas kernels for 34%

profile of v6, /device:TPU:0, one launch (start us, length us, event | category | flops | bytes accessed | tf_op | source)
XLA Modules:
  0.0 99.2 jit_solution(4283098423928258715)
XLA Ops:
  0.6 3.0 %collective-permute-start.1 = (bf16[256,768]{1,0:T(8,128)(2,1)}, bf16[256,768]{1,0:T(8,128)(2,1)S(1)}, u32[]{:S(2)}, u32[]{:S(2)}) collective-permute-start(bf16[256,768]{1,0:T(8,128)(2,1)} %bitcast.29), channel_id=1, source_target_pairs={{0,16},{8,24},{16,0},{24,8},{1,17},{9,25},{17,1},{25,9},{2,18},{10... | collective-permute-start | bytes 1179656 | tf_op jit(solution)/shard_map/ppermute | solution.py:166
  3.7 1.5 %collective-permute-start = (bf16[256,768]{1,0:T(8,128)(2,1)}, bf16[256,768]{1,0:T(8,128)(2,1)S(1)}, u32[]{:S(2)}, u32[]{:S(2)}) collective-permute-start(bf16[256,768]{1,0:T(8,128)(2,1)} %bitcast.30), channel_id=1, source_target_pairs={{0,8},{8,0},{16,24},{24,16},{1,9},{9,1},{17,25},{25,17},{2,10},{10... | collective-permute-start | bytes 1179656 | tf_op jit(solution)/shard_map/ppermute | solution.py:166
  5.2 1.6 %shard_map.126 = (bf16[4,24,576]{2,1,0:T(8,128)(2,1)}, bf16[4,24,192]{2,1,0:T(8,128)(2,1)}) custom-call(bf16[24,768]{1,0:T(8,128)(2,1)} %refs_2_.1, bf16[24,768]{1,0:T(8,128)(2,1)} %refs_3_.1, bf16[24,768]{1,0:T(8,128)(2,1)} %refs_4_.1, bf16[24,768]{1,0:T(8,128)(2,1)} %w_out.1), custom_call_target="tpu_custom_call" | custom-call | flops 1000 | bytes 294912 | tf_op jit(solution)/shard_map/pallas_call | solution.py:482
  6.7 9.0 %all_to_all.5 = bf16[4,24,576]{2,1,0:T(8,128)(2,1)S(1)} all-to-all(bf16[4,24,576]{2,1,0:T(8,128)(2,1)} %get-tuple-element.75), channel_id=1, replica_groups=mesh['depth'=4,'z'=4,'core'=2] {'depth'}, dimensions={0} | all-to-all | bytes 221184 | tf_op jit(solution)/shard_map/all_to_all | solution.py:517
  15.8 0.9 pad_maximum_fusion.1
  16.8 2.5 %collective-permute-start.2 = (bf16[256,768]{1,0:T(8,128)(2,1)}, bf16[256,768]{1,0:T(8,128)(2,1)S(1)}, u32[]{:S(2)}, u32[]{:S(2)}) collective-permute-start(bf16[256,768]{1,0:T(8,128)(2,1)} %bitcast.31), channel_id=1, source_target_pairs={{0,24},{8,16},{16,8},{24,0},{1,25},{9,17},{17,9},{25,1},{2,26},{10... | collective-permute-start | bytes 1179656 | tf_op jit(solution)/shard_map/ppermute | solution.py:166
  19.2 3.6 %collective-permute-start.5 = (bf16[4,24,768]{2,1,0:T(8,128)(2,1)S(1)}, bf16[4,24,768]{2,1,0:T(8,128)(2,1)S(1)}, u32[]{:S(2)}, u32[]{:S(2)}) collective-permute-start(bf16[4,24,768]{2,1,0:T(8,128)(2,1)S(1)} %pad_maximum_fusion.1), channel_id=1, source_target_pairs={{0,6},{2,4},{4,2},{6,0},{1,7},{3,5},{5,3},{7,1},{8,14},{10,12},{12... | collective-permute-start | bytes 442376 | tf_op jit(solution)/shard_map/ppermute | solution.py:166
  24.4 1.3 %reshape.51.refs_0_.gain = f32[1,768]{1,0:T(1,128)} reshape(f32[768]{0:T(1024)} %param.8) | data formatting | bytes 6144 | tf_op jit(solution)/shard_map/reshape | solution.py:503
  26.2 1.4 %collective-permute-done.2.refs_4_ = bf16[256,768]{1,0:T(8,128)(2,1)S(1)} collective-permute-done((bf16[256,768]{1,0:T(8,128)(2,1)}, bf16[256,768]{1,0:T(8,128)(2,1)S(1)}, u32[]{:S(2)}, u32[]{:S(2)}) %collective-permute-start.2) | collective-permute-done | bytes 393248 | tf_op jit(solution)/shard_map/ppermute | solution.py:166
  28.3 4.2 %shard_map.127 = (bf16[1024,768]{1,0:T(8,128)(2,1)}, bf16[768,1024]{1,0:T(8,128)(2,1)}) custom-call(f32[1,768]{1,0:T(1,128)} %reshape.51.refs_0_.gain, bf16[256,768]{1,0:T(8,128)(2,1)} %bitcast.32, bf16[256,768]{1,0:T(8,128)(2,1)} %copy-done.12, bf16[256,768]{1,0:T(8,128)(2,1)} %copy-done.11, bf16[256,768]{1,0:T(8,128)(2,1)} %copy-done.13), custom_call_target="tpu_custom_call" | custom-call | flops 1000 | bytes 4721664 | tf_op jit(solution)/shard_map/pallas_call | solution.py:482
  32.5 1.0 collective-permute-done.4
  33.5 1.0 pad_maximum_fusion.refs_1_
  34.6 1.2 %collective-permute-start.8 = (bf16[256,768]{1,0:T(8,128)(2,1)S(1)}, bf16[256,768]{1,0:T(8,128)(2,1)}, u32[]{:S(2)}, u32[]{:S(2)}) collective-permute-start(bf16[256,768]{1,0:T(8,128)(2,1)S(1)} %bitcast.35), channel_id=1, source_target_pairs={{0,24},{8,16},{16,8},{24,0},{1,25},{9,17},{17,9},{25,1},{2,26},{10... | collective-permute-start | bytes 1179656 | tf_op jit(solution)/shard_map/ppermute | solution.py:166
  36.3 1.9 %collective-permute-start.6 = (bf16[256,768]{1,0:T(8,128)(2,1)S(1)}, bf16[256,768]{1,0:T(8,128)(2,1)}, u32[]{:S(2)}, u32[]{:S(2)}) collective-permute-start(bf16[256,768]{1,0:T(8,128)(2,1)S(1)} %bitcast.37), channel_id=1, source_target_pairs={{0,8},{8,0},{16,24},{24,16},{1,9},{9,1},{17,25},{25,17},{2,10},{10... | collective-permute-start | bytes 1179656 | tf_op jit(solution)/shard_map/ppermute | solution.py:166
  39.0 10.1 %shard_map.128 = (bf16[1024,192]{1,0:T(8,128)(2,1)}, bf16[192,1024]{1,0:T(8,128)(2,1)}, bf16[1024,192]{1,0:T(8,128)(2,1)}, bf16[1024,192]{1,0:T(8,128)(2,1)}, bf...) custom-call(s32[3]{0:T(128)} %pad_add_fusion.refs_0_, ...), custom_call_target="tpu_custom_call" | custom-call | flops 3221225472 | bytes 8269836 | tf_op jit(solution)/shard_map/pallas_call | solution.py:482
  49.3 1.5 %collective-permute-start.11 = (bf16[256,768]{1,0:T(8,128)(2,1)}, bf16[256,768]{1,0:T(8,128)(2,1)S(1)}, u32[]{:S(2)}, u32[]{:S(2)}) collective-permute-start(bf16[256,768]{1,0:T(8,128)(2,1)} %get-tuple-element.109), channel_id=1, source_target_pairs={{0,16},{8,24},{16,0},{24,8},{1,17},{9,25},{17,1},{25,9},{2,18},{10... | collective-permute-start | bytes 1179656 | tf_op jit(solution)/shard_map/ppermute | solution.py:166
  50.9 1.8 %collective-permute-start.12 = (bf16[256,768]{1,0:T(8,128)(2,1)}, bf16[256,768]{1,0:T(8,128)(2,1)S(1)}, u32[]{:S(2)}, u32[]{:S(2)}) collective-permute-start(bf16[256,768]{1,0:T(8,128)(2,1)} %get-tuple-element.110), channel_id=1, source_target_pairs={{0,24},{8,16},{16,8},{24,0},{1,25},{9,17},{17,9},{25,1},{2,26},{10... | collective-permute-start | bytes 1179656 | tf_op jit(solution)/shard_map/ppermute | solution.py:166
  52.6 3.0 %collective-permute-done.7.refs_3_ = bf16[256,768]{1,0:T(8,128)(2,1)} collective-permute-done((bf16[256,768]{1,0:T(8,128)(2,1)S(1)}, bf16[256,768]{1,0:T(8,128)(2,1)}, u32[]{:S(2)}, u32[]{:S(2)}) %collective-permute-start.7) | collective-permute-done | bytes 393248 | tf_op jit(solution)/shard_map/ppermute | solution.py:166
  55.7 16.6 %shard_map.129 = (bf16[4,4,24,768]{3,2,1,0:T(8,128)(2,1)}, bf16[4,4,24,768]{3,2,1,0:T(8,128)(2,1)}, bf16[256,768]{1,0:T(8,128)(2,1)}, bf16[256,768]{1,0:T(8,128)...) custom-call(s32[3]{0:T(128)} %pad_add_fusion.refs_0_, ...), custom_call_target="tpu_custom_call" | custom-call | flops 9663676416 | bytes 9842700 | tf_op jit(solution)/shard_map/pallas_call | solution.py:482
  73.0 1.0 %collective-permute-start.16 = (bf16[128,768]{1,0:T(8,128)(2,1)}, bf16[128,768]{1,0:T(8,128)(2,1)S(1)}, u32[]{:S(2)}, u32[]{:S(2)}) collective-permute-start(bf16[128,768]{1,0:T(8,128)(2,1)} %get-tuple-element.115), channel_id=1, source_target_pairs={{0,16},{8,24},{16,0},{24,8},{1,17},{9,25},{17,1},{25,9},{2,18},{10... | collective-permute-start | bytes 589832 | tf_op jit(solution)/shard_map/ppermute | solution.py:166
  74.6 1.3 %fusion.1 = (bf16[4,24,768]{2,1,0:T(8,128)(2,1)S(1)}, bf16[4,24,768]{2,1,0:T(8,128)(2,1)S(1)}, f32[4,24,768]{2,1,0:T(8,128)S(1)}, bf16[4,24,768]{2,1,0:T(8,128)(2,1)S(1)}) fusion(bf16[4,4,24,768]{3,2,1,0:T(8,128)(2,1)S(1)} %collective-permute-done.13, bf16[4,4,24,768]{3,2,1,0:T(8,128)(2,1)} %get-tuple-element.112), kind=kLoop, calls=%fused_computation.10 | loop fusion | flops 1105920 | bytes 1916928 | tf_op jit(solution)/shard_map/convert_element_type | solution.py:586
  75.9 1.1 %collective-permute-start.14 = (bf16[4,24,768]{2,1,0:T(8,128)(2,1)S(1)}, bf16[4,24,768]{2,1,0:T(8,128)(2,1)S(1)}, u32[]{:S(2)}, u32[]{:S(2)}) collective-permute-start(bf16[4,24,768]{2,1,0:T(8,128)(2,1)S(1)} %get-tuple-element.148), channel_id=1, source_target_pairs={{0,2},{2,0},{4,6},{6,4},{1,3},{3,1},{5,7},{7,5},{8,10},{10,8},{12,... | collective-permute-start | bytes 442376 | tf_op jit(solution)/shard_map/ppermute | solution.py:166
  77.0 2.6 %collective-permute-start.19 = (bf16[4,24,768]{2,1,0:T(8,128)(2,1)S(1)}, bf16[4,24,768]{2,1,0:T(8,128)(2,1)S(1)}, u32[]{:S(2)}, u32[]{:S(2)}) collective-permute-start(bf16[4,24,768]{2,1,0:T(8,128)(2,1)S(1)} %get-tuple-element.145), channel_id=1, source_target_pairs={{0,4},{2,6},{4,0},{6,2},{1,5},{3,7},{5,1},{7,3},{8,12},{10,14},{12... | collective-permute-start | bytes 442376 | tf_op jit(solution)/shard_map/ppermute | solution.py:166
  80.3 3.9 %collective-permute-done.14 = bf16[4,24,768]{2,1,0:T(8,128)(2,1)S(1)} collective-permute-done((bf16[4,24,768]{2,1,0:T(8,128)(2,1)S(1)}, bf16[4,24,768]{2,1,0:T(8,128)(2,1)S(1)}, u32[]{:S(2)}, u32[]{:S(2)}) %collective-permute-start.14) | collective-permute-done | bytes 147488 | tf_op jit(solution)/shard_map/ppermute | solution.py:166
  84.3 1.0 add_convert_fusion
  86.0 1.1 %collective-permute-start.18 = (bf16[256,768]{1,0:T(8,128)(2,1)S(1)}, bf16[256,768]{1,0:T(8,128)(2,1)S(1)}, u32[]{:S(2)}, u32[]{:S(2)}) collective-permute-start(bf16[256,768]{1,0:T(8,128)(2,1)S(1)} %get-tuple-element.130), channel_id=1, source_target_pairs={{0,16},{8,24},{16,0},{24,8},{1,17},{9,25},{17,1},{25,9},{2,18},{10... | collective-permute-start | bytes 1179656 | tf_op jit(solution)/shard_map/ppermute | solution.py:166
  87.1 3.9 %collective-permute-done.19 = bf16[4,24,768]{2,1,0:T(8,128)(2,1)S(1)} collective-permute-done((bf16[4,24,768]{2,1,0:T(8,128)(2,1)S(1)}, bf16[4,24,768]{2,1,0:T(8,128)(2,1)S(1)}, u32[]{:S(2)}, u32[]{:S(2)}) %collective-permute-start.19) | collective-permute-done | bytes 147488 | tf_op jit(solution)/shard_map/ppermute | solution.py:166
  91.1 1.7 %collective-permute-start.23 = (bf16[24,576]{1,0:T(8,128)(2,1)S(1)}, bf16[24,576]{1,0:T(8,128)(2,1)S(1)}, u32[]{:S(2)}, u32[]{:S(2)}) collective-permute-start(bf16[24,576]{1,0:T(8,128)(2,1)S(1)} %get-tuple-element.149), channel_id=1, source_target_pairs={{0,24},{8,16},{16,8},{24,0},{1,25},{9,17},{17,9},{25,1},{2,26},{10... | collective-permute-start | bytes 82952 | tf_op jit(solution)/shard_map/ppermute | solution.py:166
  92.8 0.9 collective-permute-start.22
  94.7 1.5 %collective-permute-done.17.refs_1_ = bf16[256,768]{1,0:T(8,128)(2,1)S(1)} collective-permute-done((bf16[256,768]{1,0:T(8,128)(2,1)S(1)}, bf16[256,768]{1,0:T(8,128)(2,1)S(1)}, u32[]{:S(2)}, u32[]{:S(2)}) %collective-permute-start.17) | collective-permute-done | bytes 393248 | tf_op jit(solution)/shard_map/ppermute | solution.py:166
  96.2 1.4 %shard_map.130 = bf16[256,768]{1,0:T(8,128)(2,1)} custom-call(f32[1,768]{1,0:T(1,128)S(1)} %copy-done.4, bf16[256,768]{1,0:T(8,128)(2,1)S(1)} %bitcast.33, bf16[256,768]{1,0:T(8,128)(2,1)S(1)} %bitcast.38, bf16[256,768]{1,0:T(8,128)(2,1)S(1)} %copy-done.8, bf16[256,768]{1,0:T(8,128)(2,1)S(1)} %collective-permute-done.17.refs_1_, ...), custom_call_target="tpu_custom_call" | custom-call | flops 786432000 | bytes 2362368 | tf_op jit(solution)/shard_map/pallas_call | solution.py:482
  97.7 1.5 %shard_map.131 = (f32[24,768]{1,0:T(8,128)}, f32[24,768]{1,0:T(8,128)}, f32[24,768]{1,0:T(8,128)}, f32[24,768]{1,0:T(8,128)}, f32[1,24]{1,0:T(1,128)}) custom-call(s32[3]{0:T(128)S(1)} %copy-done.5, f32[1,24]{1,0:T(1,128)S(1)} %dynamic-slice_bitcast_fusion.refs_1_, bf16[24,768]{1,0:T(8,128)(2,1)S(1)} %copy-done.1, bf16[24,768]{1,0:T(8,128)(2,1)S(1)} %copy-done.2, ...), custom_call_target="tpu_custom_call" | custom-call | flops 1000 | bytes 783564 | tf_op jit(solution)/shard_map/pallas_call | solution.py:482
  (67 shorter events, 8.5 us)
Async XLA Ops:
  0.6 16.1 %collective-permute-start.1 = (bf16[256,768]{1,0:T(8,128)(2,1)}, bf16[256,768]{1,0:T(8,128)(2,1)S(1)}, u32[]{:S(2)}, u32[]{:S(2)}) collective-permute-start(bf16[256,768]{1,0:T(8,128)(2,1)} %bitcast.29), channel_id=1, source_target_pairs={{0,16},{8,24},{16,0},{24,8},{1,17},{9,25},{17,1},{25,9},{2,18},{10... | collective-permute-start | bytes 1179656 | tf_op jit(solution)/shard_map/ppermute | solution.py:166
  3.7 13.1 %collective-permute-start = (bf16[256,768]{1,0:T(8,128)(2,1)}, bf16[256,768]{1,0:T(8,128)(2,1)S(1)}, u32[]{:S(2)}, u32[]{:S(2)}) collective-permute-start(bf16[256,768]{1,0:T(8,128)(2,1)} %bitcast.30), channel_id=1, source_target_pairs={{0,8},{8,0},{16,24},{24,16},{1,9},{9,1},{17,25},{25,17},{2,10},{10... | collective-permute-start | bytes 1179656 | tf_op jit(solution)/shard_map/ppermute | solution.py:166
  15.8 18.8 %copy-start.6 = (bf16[256,1,768]{2,0,1:T(8,128)(2,1)S(1)}, bf16[256,1,768]{2,0,1:T(8,128)(2,1)}, u32[]{:S(2)}) copy-start(bf16[256,1,768]{2,0,1:T(8,128)(2,1)} %param.13) | copy-start | bytes 1179652
  16.7 10.9 %copy-start.11 = (bf16[256,768]{1,0:T(8,128)(2,1)}, bf16[256,768]{1,0:T(8,128)(2,1)S(1)}, u32[]{:S(2)}) copy-start(bf16[256,768]{1,0:T(8,128)(2,1)S(1)} %collective-permute-done.1.refs_3_) | copy-start | bytes 1179652
  16.7 10.9 %copy-start.12 = (bf16[256,768]{1,0:T(8,128)(2,1)}, bf16[256,768]{1,0:T(8,128)(2,1)S(1)}, u32[]{:S(2)}) copy-start(bf16[256,768]{1,0:T(8,128)(2,1)S(1)} %collective-permute-done.refs_2_) | copy-start | bytes 1179652
  16.8 10.8 %collective-permute-start.2 = (bf16[256,768]{1,0:T(8,128)(2,1)}, bf16[256,768]{1,0:T(8,128)(2,1)S(1)}, u32[]{:S(2)}, u32[]{:S(2)}) collective-permute-start(bf16[256,768]{1,0:T(8,128)(2,1)} %bitcast.31), channel_id=1, source_target_pairs={{0,24},{8,16},{16,8},{24,0},{1,25},{9,17},{17,9},{25,1},{2,26},{10... | collective-permute-start | bytes 1179656 | tf_op jit(solution)/shard_map/ppermute | solution.py:166
  19.2 13.3 %collective-permute-start.5 = (bf16[4,24,768]{2,1,0:T(8,128)(2,1)S(1)}, bf16[4,24,768]{2,1,0:T(8,128)(2,1)S(1)}, u32[]{:S(2)}, u32[]{:S(2)}) collective-permute-start(bf16[4,24,768]{2,1,0:T(8,128)(2,1)S(1)} %pad_maximum_fusion.1), channel_id=1, source_target_pairs={{0,6},{2,4},{4,2},{6,0},{1,7},{3,5},{5,3},{7,1},{8,14},{10,12},{12... | collective-permute-start | bytes 442376 | tf_op jit(solution)/shard_map/ppermute | solution.py:166
  22.8 10.7 %collective-permute-start.4 = (bf16[4,24,768]{2,1,0:T(8,128)(2,1)S(1)}, bf16[4,24,768]{2,1,0:T(8,128)(2,1)S(1)}, u32[]{:S(2)}, u32[]{:S(2)}) collective-permute-start(bf16[4,24,768]{2,1,0:T(8,128)(2,1)S(1)} %pad_maximum_fusion.1), channel_id=1, source_target_pairs={{0,4},{2,6},{4,0},{6,2},{1,5},{3,7},{5,1},{7,3},{8,12},{10,14},{12... | collective-permute-start | bytes 442376 | tf_op jit(solution)/shard_map/ppermute | solution.py:166
  22.8 10.7 %collective-permute-start.3 = (bf16[4,24,768]{2,1,0:T(8,128)(2,1)S(1)}, bf16[4,24,768]{2,1,0:T(8,128)(2,1)}, u32[]{:S(2)}, u32[]{:S(2)}) collective-permute-start(bf16[4,24,768]{2,1,0:T(8,128)(2,1)S(1)} %pad_maximum_fusion.1), channel_id=1, source_target_pairs={{0,2},{2,0},{4,6},{6,4},{1,3},{3,1},{5,7},{7,5},{8,10},{10,8},{12,... | collective-permute-start | bytes 442376 | tf_op jit(solution)/shard_map/ppermute | solution.py:166
  34.5 3.6 %collective-permute-start.9 = (bf16[4,4,24,768]{3,2,1,0:T(8,128)(2,1)S(1)}, bf16[4,4,24,768]{3,2,1,0:T(8,128)(2,1)S(1)}, u32[]{:S(2)}, u32[]{:S(2)}) collective-permute-start(bf16[4,4,24,768]{3,2,1,0:T(8,128)(2,1)S(1)} %pad_maximum_fusion.refs_1_), channel_id=1, source_target_pairs={{0,1},{1,0},{2,3},{3,2},{4,5},{5,4},{6,7},{7,6},{8,9},{9,8},{10,11... | collective-permute-start | bytes 1769480 | tf_op jit(solution)/shard_map/ppermute | solution.py:166
  34.6 16.2 %collective-permute-start.8 = (bf16[256,768]{1,0:T(8,128)(2,1)S(1)}, bf16[256,768]{1,0:T(8,128)(2,1)}, u32[]{:S(2)}, u32[]{:S(2)}) collective-permute-start(bf16[256,768]{1,0:T(8,128)(2,1)S(1)} %bitcast.35), channel_id=1, source_target_pairs={{0,24},{8,16},{16,8},{24,0},{1,25},{9,17},{17,9},{25,1},{2,26},{10... | collective-permute-start | bytes 1179656 | tf_op jit(solution)/shard_map/ppermute | solution.py:166
  35.8 19.9 %collective-permute-start.7 = (bf16[256,768]{1,0:T(8,128)(2,1)S(1)}, bf16[256,768]{1,0:T(8,128)(2,1)}, u32[]{:S(2)}, u32[]{:S(2)}) collective-permute-start(bf16[256,768]{1,0:T(8,128)(2,1)S(1)} %bitcast.36), channel_id=1, source_target_pairs={{0,16},{8,24},{16,0},{24,8},{1,17},{9,25},{17,1},{25,9},{2,18},{10... | collective-permute-start | bytes 1179656 | tf_op jit(solution)/shard_map/ppermute | solution.py:166
  36.3 19.4 %collective-permute-start.6 = (bf16[256,768]{1,0:T(8,128)(2,1)S(1)}, bf16[256,768]{1,0:T(8,128)(2,1)}, u32[]{:S(2)}, u32[]{:S(2)}) collective-permute-start(bf16[256,768]{1,0:T(8,128)(2,1)S(1)} %bitcast.37), channel_id=1, source_target_pairs={{0,8},{8,0},{16,24},{24,16},{1,9},{9,1},{17,25},{25,17},{2,10},{10... | collective-permute-start | bytes 1179656 | tf_op jit(solution)/shard_map/ppermute | solution.py:166
  49.1 23.2 %collective-permute-start.10 = (bf16[256,768]{1,0:T(8,128)(2,1)}, bf16[256,768]{1,0:T(8,128)(2,1)S(1)}, u32[]{:S(2)}, u32[]{:S(2)}) collective-permute-start(bf16[256,768]{1,0:T(8,128)(2,1)} %get-tuple-element.108), channel_id=1, source_target_pairs={{0,8},{8,0},{16,24},{24,16},{1,9},{9,1},{17,25},{25,17},{2,10},{10... | collective-permute-start | bytes 1179656 | tf_op jit(solution)/shard_map/ppermute | solution.py:166
  49.3 22.9 %collective-permute-start.11 = (bf16[256,768]{1,0:T(8,128)(2,1)}, bf16[256,768]{1,0:T(8,128)(2,1)S(1)}, u32[]{:S(2)}, u32[]{:S(2)}) collective-permute-start(bf16[256,768]{1,0:T(8,128)(2,1)} %get-tuple-element.109), channel_id=1, source_target_pairs={{0,16},{8,24},{16,0},{24,8},{1,17},{9,25},{17,1},{25,9},{2,18},{10... | collective-permute-start | bytes 1179656 | tf_op jit(solution)/shard_map/ppermute | solution.py:166
  50.9 21.5 %collective-permute-start.12 = (bf16[256,768]{1,0:T(8,128)(2,1)}, bf16[256,768]{1,0:T(8,128)(2,1)S(1)}, u32[]{:S(2)}, u32[]{:S(2)}) collective-permute-start(bf16[256,768]{1,0:T(8,128)(2,1)} %get-tuple-element.110), channel_id=1, source_target_pairs={{0,24},{8,16},{16,8},{24,0},{1,25},{9,17},{17,9},{25,1},{2,26},{10... | collective-permute-start | bytes 1179656 | tf_op jit(solution)/shard_map/ppermute | solution.py:166
  72.2 12.0 %copy-start = (bf16[256,1,768]{2,0,1:T(8,128)(2,1)S(1)}, bf16[256,1,768]{2,0,1:T(8,128)(2,1)}, u32[]{:S(2)}) copy-start(bf16[256,1,768]{2,0,1:T(8,128)(2,1)} %param.7) | copy-start | bytes 1179652
  72.2 12.0 %copy-start.10 = (bf16[256,768]{1,0:T(8,128)(2,1)S(1)}, bf16[256,768]{1,0:T(8,128)(2,1)}, u32[]{:S(2)}) copy-start(bf16[256,768]{1,0:T(8,128)(2,1)} %get-tuple-element.123) | copy-start | bytes 1179652
  72.4 2.2 %collective-permute-start.13 = (bf16[4,4,24,768]{3,2,1,0:T(8,128)(2,1)}, bf16[4,4,24,768]{3,2,1,0:T(8,128)(2,1)S(1)}, u32[]{:S(2)}, u32[]{:S(2)}) collective-permute-start(bf16[4,4,24,768]{3,2,1,0:T(8,128)(2,1)} %get-tuple-element.113), channel_id=1, source_target_pairs={{0,1},{1,0},{2,3},{3,2},{4,5},{5,4},{6,7},{7,6},{8,9},{9,8},{10,11... | collective-permute-start | bytes 1769480 | tf_op jit(solution)/shard_map/ppermute | solution.py:166
  72.4 8.0 %collective-permute-start.15 = (bf16[128,768]{1,0:T(8,128)(2,1)}, bf16[128,768]{1,0:T(8,128)(2,1)S(1)}, u32[]{:S(2)}, u32[]{:S(2)}) collective-permute-start(bf16[128,768]{1,0:T(8,128)(2,1)} %get-tuple-element.114), channel_id=1, source_target_pairs={{0,8},{8,0},{16,24},{24,16},{1,9},{9,1},{17,25},{25,17},{2,10},{10... | collective-permute-start | bytes 589832 | tf_op jit(solution)/shard_map/ppermute | solution.py:166
  73.0 7.3 %collective-permute-start.16 = (bf16[128,768]{1,0:T(8,128)(2,1)}, bf16[128,768]{1,0:T(8,128)(2,1)S(1)}, u32[]{:S(2)}, u32[]{:S(2)}) collective-permute-start(bf16[128,768]{1,0:T(8,128)(2,1)} %get-tuple-element.115), channel_id=1, source_target_pairs={{0,16},{8,24},{16,0},{24,8},{1,17},{9,25},{17,1},{25,9},{2,18},{10... | collective-permute-start | bytes 589832 | tf_op jit(solution)/shard_map/ppermute | solution.py:166
  75.9 8.4 %collective-permute-start.14 = (bf16[4,24,768]{2,1,0:T(8,128)(2,1)S(1)}, bf16[4,24,768]{2,1,0:T(8,128)(2,1)S(1)}, u32[]{:S(2)}, u32[]{:S(2)}) collective-permute-start(bf16[4,24,768]{2,1,0:T(8,128)(2,1)S(1)} %get-tuple-element.148), channel_id=1, source_target_pairs={{0,2},{2,0},{4,6},{6,4},{1,3},{3,1},{5,7},{7,5},{8,10},{10,8},{12,... | collective-permute-start | bytes 442376 | tf_op jit(solution)/shard_map/ppermute | solution.py:166
  77.0 14.0 %collective-permute-start.19 = (bf16[4,24,768]{2,1,0:T(8,128)(2,1)S(1)}, bf16[4,24,768]{2,1,0:T(8,128)(2,1)S(1)}, u32[]{:S(2)}, u32[]{:S(2)}) collective-permute-start(bf16[4,24,768]{2,1,0:T(8,128)(2,1)S(1)} %get-tuple-element.145), channel_id=1, source_target_pairs={{0,4},{2,6},{4,0},{6,2},{1,5},{3,7},{5,1},{7,3},{8,12},{10,14},{12... | collective-permute-start | bytes 442376 | tf_op jit(solution)/shard_map/ppermute | solution.py:166
  79.6 11.4 %collective-permute-start.20 = (bf16[4,24,768]{2,1,0:T(8,128)(2,1)S(1)}, bf16[4,24,768]{2,1,0:T(8,128)(2,1)S(1)}, u32[]{:S(2)}, u32[]{:S(2)}) collective-permute-start(bf16[4,24,768]{2,1,0:T(8,128)(2,1)S(1)} %get-tuple-element.146), channel_id=1, source_target_pairs={{0,6},{2,4},{4,2},{6,0},{1,7},{3,5},{5,3},{7,1},{8,14},{10,12},{12... | collective-permute-start | bytes 442376 | tf_op jit(solution)/shard_map/ppermute | solution.py:166
  85.3 11.0 %copy-start.4 = (f32[1,768]{1,0:T(1,128)S(1)}, f32[1,768]{1,0:T(1,128)}, u32[]{:S(2)}) copy-start(f32[1,768]{1,0:T(1,128)} %reshape.51.refs_0_.gain) | copy-start | bytes 9220
  85.3 11.0 %copy-start.7 = (bf16[256,1,768]{2,0,1:T(8,128)(2,1)S(1)}, bf16[256,1,768]{2,0,1:T(8,128)(2,1)}, u32[]{:S(2)}) copy-start(bf16[256,1,768]{2,0,1:T(8,128)(2,1)} %param.13) | copy-start | bytes 1179652
  85.3 11.0 %copy-start.8 = (bf16[256,768]{1,0:T(8,128)(2,1)S(1)}, bf16[256,768]{1,0:T(8,128)(2,1)}, u32[]{:S(2)}) copy-start(bf16[256,768]{1,0:T(8,128)(2,1)} %get-tuple-element.128.refs_0_) | copy-start | bytes 1179652
  85.4 10.8 %collective-permute-start.17 = (bf16[256,768]{1,0:T(8,128)(2,1)S(1)}, bf16[256,768]{1,0:T(8,128)(2,1)S(1)}, u32[]{:S(2)}, u32[]{:S(2)}) collective-permute-start(bf16[256,768]{1,0:T(8,128)(2,1)S(1)} %get-tuple-element.129), channel_id=1, source_target_pairs={{0,8},{8,0},{16,24},{24,16},{1,9},{9,1},{17,25},{25,17},{2,10},{10... | collective-permute-start | bytes 1179656 | tf_op jit(solution)/shard_map/ppermute | solution.py:166
  86.0 10.2 %collective-permute-start.18 = (bf16[256,768]{1,0:T(8,128)(2,1)S(1)}, bf16[256,768]{1,0:T(8,128)(2,1)S(1)}, u32[]{:S(2)}, u32[]{:S(2)}) collective-permute-start(bf16[256,768]{1,0:T(8,128)(2,1)S(1)} %get-tuple-element.130), channel_id=1, source_target_pairs={{0,16},{8,24},{16,0},{24,8},{1,17},{9,25},{17,1},{25,9},{2,18},{10... | collective-permute-start | bytes 1179656 | tf_op jit(solution)/shard_map/ppermute | solution.py:166
  91.1 6.5 %collective-permute-start.23 = (bf16[24,576]{1,0:T(8,128)(2,1)S(1)}, bf16[24,576]{1,0:T(8,128)(2,1)S(1)}, u32[]{:S(2)}, u32[]{:S(2)}) collective-permute-start(bf16[24,576]{1,0:T(8,128)(2,1)S(1)} %get-tuple-element.149), channel_id=1, source_target_pairs={{0,24},{8,16},{16,8},{24,0},{1,25},{9,17},{17,9},{25,1},{2,26},{10... | collective-permute-start | bytes 82952 | tf_op jit(solution)/shard_map/ppermute | solution.py:166
  92.8 4.8 %collective-permute-start.22 = (bf16[24,576]{1,0:T(8,128)(2,1)S(1)}, bf16[24,576]{1,0:T(8,128)(2,1)S(1)}, u32[]{:S(2)}, u32[]{:S(2)}) collective-permute-start(bf16[24,576]{1,0:T(8,128)(2,1)S(1)} %get-tuple-element.150), channel_id=1, source_target_pairs={{0,16},{8,24},{16,0},{24,8},{1,17},{9,25},{17,1},{25,9},{2,18},{10... | collective-permute-start | bytes 82952 | tf_op jit(solution)/shard_map/ppermute | solution.py:166
  93.8 3.9 %collective-permute-start.21 = (bf16[24,576]{1,0:T(8,128)(2,1)S(1)}, bf16[24,576]{1,0:T(8,128)(2,1)S(1)}, u32[]{:S(2)}, u32[]{:S(2)}) collective-permute-start(bf16[24,576]{1,0:T(8,128)(2,1)S(1)} %get-tuple-element.151), channel_id=1, source_target_pairs={{0,8},{8,0},{16,24},{24,16},{1,9},{9,1},{17,25},{25,17},{2,10},{10... | collective-permute-start | bytes 82952 | tf_op jit(solution)/shard_map/ppermute | solution.py:166
  (9 other events, 50.4 us)
